TPU v7x, 32 devices: a whole 2x2x4 slice. The times are simulated.
32 devices in a mesh: dp: 8 (over y, x, core), tensor: 4 (over z).
Axes of the slice: x: 2, y: 2, z: 4, core: 2. Of those that a mesh axis runs over, the one named last changes fastest.
Arguments:
- x_in: bfloat16 [8192, 1024], P(('dp', 'tensor')), may hold values from -6 to 6
- cotangent: bfloat16 [8192, 1024], P(('dp', 'tensor')), may hold values from -6 to 6
- segments: int32 [8, 1024], P('dp'), may hold values from 0 to 3, as said below
- norm_one: bfloat16 [1024], P('dp'), may hold values from 0.5 to 1.5
- w_query: bfloat16 [1024, 512], P('dp', 'tensor'), may hold values from -0.1875 to 0.1875
- w_keyval: bfloat16 [1024, 256], P('dp'), may hold values from -0.1875 to 0.1875
- w_attn_out: bfloat16 [512, 1024], P('tensor', 'dp'), may hold values from -1 to 1
- w_zgate: bfloat16 [1024, 1536], P('dp', 'tensor'), may hold values from -0.1875 to 0.1875
- w_xin: bfloat16 [1024, 1536], P('dp', 'tensor'), may hold values from -0.1875 to 0.1875
- w_bcin: bfloat16 [1024, 256], P('dp'), may hold values from -0.1875 to 0.1875
- w_dtin: bfloat16 [1024, 24], P('dp', 'tensor'), may hold values from -0.1875 to 0.1875
- conv_x: float32 [4, 1536], P(None, 'tensor'), may hold values from -0.7 to 0.7
- conv_bc: float32 [4, 256], replicated, may hold values from -0.7 to 0.7
- bias_x: float32 [1536], P('tensor'), may hold values from -0.5 to 0.5
- bias_bc: float32 [256], replicated, may hold values from -0.5 to 0.5
- dt_bias: float32 [24], P('tensor'), may hold values from -6.9 to -2.3
- a_log: float32 [24], P('tensor'), may hold values from 0 to 2.77
- d_skip: float32 [24], P('tensor'), may hold values from 0.5 to 1.5
- ssm_gain: float32 [1536], P('tensor'), may hold values from 0.5 to 1.5
- w_mix_out: bfloat16 [1536, 1024], P('tensor', 'dp'), may hold values from -0.15625 to 0.15625
- norm_two: bfloat16 [1024], P('dp'), may hold values from 0.5 to 1.5
- w_gate: bfloat16 [1024, 2048], P('dp', 'tensor'), may hold values from -0.1875 to 0.1875
- w_up: bfloat16 [1024, 2048], P('dp', 'tensor'), may hold values from -0.1875 to 0.1875
- w_down: bfloat16 [2048, 1024], P('tensor', 'dp'), may hold values from -0.125 to 0.125
Outputs:
- block_out: bfloat16 [8192, 1024], P(('dp', 'tensor'))
- grad_input: float32 [8192, 1024], P(('dp', 'tensor'))
- grad_norm_one: float32 [1024], P('dp')
- grad_w_query: float32 [1024, 512], P('dp', 'tensor')
- grad_w_keyval: float32 [1024, 256], P('dp')
- grad_w_attn_out: float32 [512, 1024], P('tensor', 'dp')
- grad_w_zgate: float32 [1024, 1536], P('dp', 'tensor')
- grad_w_xin: float32 [1024, 1536], P('dp', 'tensor')
- grad_w_bcin: float32 [1024, 256], P('dp')
- grad_w_dtin: float32 [1024, 24], P('dp', 'tensor')
- grad_conv_x: float32 [4, 1536], P(None, 'tensor')
- grad_conv_bc: float32 [4, 256], replicated
- grad_bias_x: float32 [1536], P('tensor')
- grad_bias_bc: float32 [256], replicated
- grad_dt_bias: float32 [24], P('tensor')
- grad_a_log: float32 [24], P('tensor')
- grad_d_skip: float32 [24], P('tensor')
- grad_ssm_gain: float32 [1536], P('tensor')
- grad_w_mix_out: float32 [1536, 1024], P('tensor', 'dp')
- grad_norm_two: float32 [1024], P('dp')
- grad_w_gate: float32 [1024, 2048], P('dp', 'tensor')
- grad_w_up: float32 [1024, 2048], P('dp', 'tensor')
- grad_w_down: float32 [2048, 1024], P('tensor', 'dp')
Inputs may be any that keep to these rules, and one draw needn't show every extreme that they name: `segments`: document numbers never fall along a sequence; every sequence holds exactly 4 documents, one of exactly 800 tokens and three of at least 60 tokens each.
All inputs are finite; a program needn't handle non-finite values.
Results may differ from a plain program's by a relative error of at most 0.024.
Values may be sent and summed in bfloat16 or wider, within the bound.
No kernel may reach another device: no remote copies, remote signals or barrier semaphores. Data moves between devices by JAX's collectives and lax.ppermute only.
A program may use at most 128 MiB of HBM per device.

v0:
```python
import math

import jax
import jax.numpy as jnp
import numpy as np
from jax import lax
from jax.experimental import pallas as pl
from jax.experimental.pallas import tpu as pltpu
from jax.sharding import PartitionSpec as P

QH = 8
KVH = 2
HD = 64
MH = 24
PD = 64
NS = 128
KW = 4
BLOCK = 128
LANES = 128

EPSILON = 1e-05
ROPE_BASE = 100000000000.0
NEG = -1e9
F32 = jnp.float32
BF16 = jnp.bfloat16
MIB = 1024 * 1024


def mm(lhs, rhs):
    return lax.dot_general(lhs, rhs, (((1,), (0,)), ((), ())), preferred_element_type=F32)


def mm_nt(lhs, rhs):
    return lax.dot_general(lhs, rhs, (((1,), (1,)), ((), ())), preferred_element_type=F32)


def mm_tn(lhs, rhs):
    return lax.dot_general(lhs, rhs, (((0,), (0,)), ((), ())), preferred_element_type=F32)


def rms_scale(values):
    return lax.rsqrt(jnp.mean(values * values, axis=-1, keepdims=True) + EPSILON)


def norm_back(grad_normed, normed, scale):
    return scale * (grad_normed - normed * jnp.mean(grad_normed * normed, axis=-1, keepdims=True))


def sigmoid(v):
    return 1.0 / (1.0 + jnp.exp(-v))


def iota(shape, dim):
    return lax.broadcasted_iota(jnp.int32, shape, dim)


def rope_tables(length):
    half = HD // 2
    freqs = np.float32(ROPE_BASE) ** (-(np.arange(half, dtype=np.float32) * np.float32(2.0 / HD)))
    angles = np.arange(length, dtype=np.float32)[:, None] * freqs.astype(np.float32)[None, :]
    cosine, sine = np.cos(angles).astype(np.float32), np.sin(angles).astype(np.float32)
    cos_lanes = np.concatenate([cosine] * 4, axis=1)
    sin_lanes = np.concatenate([-sine, sine, -sine, sine], axis=1)
    return jnp.asarray(cos_lanes), jnp.asarray(sin_lanes)


def swap_halves(values):
    lane = iota(values.shape, 1)
    ahead = pltpu.roll(values, LANES - HD // 2, 1)
    behind = pltpu.roll(values, HD // 2, 1)
    return jnp.where((lane & (HD - 1)) < HD // 2, ahead, behind)


def pair_rows(block):
    low = iota(block.shape, 1) < HD
    zero = jnp.zeros_like(block)
    return jnp.concatenate([jnp.where(low, block, zero), jnp.where(low, zero, block)], axis=0)


def attn_fwd_kernel(q_ref, kv_ref, cos_ref, sin_ref, start_ref, out_ref, lse_ref, lq_ref, lkv_ref):
    length = q_ref.shape[0]
    rows = 256
    cosine, sine = cos_ref[...], sin_ref[...]
    low = iota((length, LANES), 1) < HD
    queries = q_ref[...]
    lq_ref[...] = (queries * cosine + swap_halves(queries) * sine).astype(BF16)
    kv = kv_ref[...]
    kv = jnp.where(low, kv * cosine + swap_halves(kv) * sine, kv)
    lkv_ref[...] = kv.astype(BF16)
    other = pltpu.roll(kv, HD, 1)
    keys = jnp.where(low, kv, other).astype(BF16)
    vals = jnp.where(low, other, kv).astype(BF16)
    half = iota((rows, LANES), 1) < HD
    for step in range(length // rows):
        end = (step + 1) * rows
        span = slice(step * rows, end)
        stacked = pair_rows(lq_ref[span, :].astype(F32)).astype(BF16)
        scores = mm_nt(stacked, keys[:end]) * (1.0 / math.sqrt(HD))
        first = start_ref[span, :][:, :1]
        col = iota((rows, end), 1)
        row = iota((rows, end), 0) + step * rows
        allowed = (col <= row) & (col >= first)
        allowed = jnp.concatenate([allowed.astype(jnp.int32)] * 2, axis=0) > 0
        scores = jnp.where(allowed, scores, NEG)
        top = jnp.max(scores, axis=1, keepdims=True)
        expo = jnp.exp(scores - top)
        total = jnp.sum(expo, axis=1, keepdims=True)
        probs = (expo * (1.0 / total)).astype(BF16)
        result = mm(probs, vals[:end])
        out_ref[span, :] = jnp.where(half, result[:rows], result[rows:]).astype(BF16)
        lse = top + jnp.log(total)
        lse_ref[span, :] = jnp.where(half, lse[:rows], lse[rows:])


def attn_bwd_kernel(
    lq_ref, lkv_ref, lse_ref, out_ref, go_ref, cos_ref, sin_ref, start_ref, gq_ref, gkv_ref, dk_ref, dv_ref
):
    length = lq_ref.shape[0]
    rows = 256
    cosine, sine = cos_ref[...], sin_ref[...]
    low = iota((length, LANES), 1) < HD
    kv = lkv_ref[...].astype(F32)
    other = pltpu.roll(kv, HD, 1)
    keys = jnp.where(low, kv, other).astype(BF16)
    vals = jnp.where(low, other, kv).astype(BF16)
    half = iota((rows, LANES), 1) < HD
    dk_ref[...] = jnp.zeros_like(dk_ref)
    dv_ref[...] = jnp.zeros_like(dv_ref)
    inv = 1.0 / math.sqrt(HD)
    for step in range(length // rows):
        end = (step + 1) * rows
        span = slice(step * rows, end)
        stacked = pair_rows(lq_ref[span, :].astype(F32)).astype(BF16)
        grads = pair_rows(go_ref[span, :].astype(F32))
        outs = out_ref[span, :].astype(F32)
        inner = jnp.sum(grads * jnp.concatenate([outs, outs], axis=0), axis=1, keepdims=True)
        grads = grads.astype(BF16)
        lse = lse_ref[span, :]
        lse = jnp.concatenate([lse[:, :1], lse[:, HD : HD + 1]], axis=0)
        scores = mm_nt(stacked, keys[:end]) * inv
        first = start_ref[span, :][:, :1]
        col = iota((rows, end), 1)
        row = iota((rows, end), 0) + step * rows
        allowed = (col <= row) & (col >= first)
        allowed = jnp.concatenate([allowed.astype(jnp.int32)] * 2, axis=0) > 0
        probs = jnp.exp(jnp.where(allowed, scores, NEG) - lse)
        grad_probs = mm_nt(grads, vals[:end])
        grad_scores = (probs * (grad_probs - inner)).astype(BF16)
        gq = mm(grad_scores, keys[:end]) * inv
        gq = jnp.where(half, gq[:rows], gq[rows:])
        gq_ref[span, :] = (gq * cosine[span] - swap_halves(gq) * sine[span]).astype(BF16)
        dk_ref[:end, :] += mm_tn(grad_scores, stacked)
        dv_ref[:end, :] += mm_tn(probs.astype(BF16), grads)
    dk = dk_ref[...] * inv
    dk = dk + pltpu.roll(dk, HD, 1)
    dk = dk * cosine - swap_halves(dk) * sine
    dv = dv_ref[...]
    dv = dv + pltpu.roll(dv, HD, 1)
    gkv_ref[...] = jnp.where(low, dk, dv).astype(BF16)


def attn_forward(proj, cosine, sine, start_col):
    length = proj.shape[0]
    wide = pl.BlockSpec((length, LANES), lambda i: (0, 0))
    return pl.pallas_call(
        attn_fwd_kernel,
        grid=(1,),
        in_specs=[wide, pl.BlockSpec((length, LANES), lambda i: (0, 1)), wide, wide, wide],
        out_specs=[wide] * 4,
        out_shape=[
            jax.ShapeDtypeStruct((length, LANES), BF16),
            jax.ShapeDtypeStruct((length, LANES), F32),
            jax.ShapeDtypeStruct((length, LANES), BF16),
            jax.ShapeDtypeStruct((length, LANES), BF16),
        ],
        compiler_params=pltpu.CompilerParams(vmem_limit_bytes=32 * MIB),
        cost_estimate=pl.CostEstimate(flops=10**9, bytes_accessed=6 * 10**6, transcendentals=2 * 10**6),
        name="attn_fwd",
    )(proj, proj, cosine, sine, start_col)


def attn_backward(low_q, low_kv, lse, out, grad_out, cosine, sine, start_col):
    length = low_q.shape[0]
    wide = pl.BlockSpec((length, LANES), lambda i: (0, 0))
    return pl.pallas_call(
        attn_bwd_kernel,
        grid=(1,),
        in_specs=[wide] * 8,
        out_specs=[wide] * 2,
        out_shape=[jax.ShapeDtypeStruct((length, LANES), BF16)] * 2,
        scratch_shapes=[pltpu.VMEM((length, LANES), F32)] * 2,
        compiler_params=pltpu.CompilerParams(vmem_limit_bytes=32 * MIB),
        cost_estimate=pl.CostEstimate(flops=3 * 10**9, bytes_accessed=6 * 10**6, transcendentals=2 * 10**6),
        name="attn_bwd",
    )(low_q, low_kv, lse, out, grad_out, cosine, sine, start_col)


def split3(values):
    high = values.astype(BF16).astype(F32)
    rest = values - high
    mid = rest.astype(BF16).astype(F32)
    tail = rest - mid
    return jnp.concatenate([high, mid, tail, jnp.zeros_like(values)], axis=0).astype(BF16)


def spread(rows, width, lanes_each):
    pick = (iota((32, width), 1) // lanes_each) == (iota((32, width), 0) & 7)
    return mm_tn(split3(rows), pick.astype(F32).astype(BF16))


def decay_terms(dt_block, dt_bias, rate, start_row, start_col, base):
    dt_rows = jnp.transpose(dt_block)[:8] + dt_bias
    step = jnp.maximum(dt_rows, 0.0) + jnp.log1p(jnp.exp(-jnp.abs(dt_rows)))
    log_decay = -step * rate
    row = iota((BLOCK, BLOCK), 0) + base
    col = iota((BLOCK, BLOCK), 1) + base
    linked = (col <= row) & (col >= start_col)
    linked_low = jnp.where(linked, 1.0, 0.0).astype(BF16)
    cum = mm_nt(split3(log_decay), linked_low)
    cum = cum[0:8] + cum[8:16] + cum[16:24]
    enter = jnp.exp(jnp.where(start_row < base, cum, NEG))
    last = cum[:, BLOCK - 1 :]
    position = iota((8, BLOCK), 1) + base
    tail = jnp.exp(jnp.where(position >= start_row[:, BLOCK - 1 :], last - cum, NEG))
    return dt_rows, step, log_decay, linked, linked_low, cum, enter, tail


def conv_sum(ext_ref, taps, bias, place):
    total = bias + taps[KW - 1 : KW] * ext_ref[pl.ds(8, BLOCK), :]
    for offset in range(1, KW):
        shifted = ext_ref[pl.ds(8 - offset, BLOCK), :]
        total = total + jnp.where(place >= offset, taps[KW - 1 - offset : KW - offset] * shifted, 0.0)
    return total


def wide_place(start_col, base, width):
    place = iota((BLOCK, BLOCK), 0) + base - start_col
    return jnp.concatenate([place] * (width // LANES), axis=1)


def scan_fwd_kernel(
    cols,
    proj_ref,
    startc_ref,
    startr_ref,
    taps_ref,
    bias_ref,
    dtb_ref,
    rate_ref,
    skip_ref,
    y_ref,
    gated_ref,
    state_out_ref,
    ssq_ref,
    state_ref,
    ext_ref,
):
    zat, xat, dat, width = cols
    channels = xat - zat
    heads = channels // PD
    block = pl.program_id(0)
    base = block * BLOCK

    @pl.when(block == 0)
    def _():
        state_ref[...] = jnp.zeros_like(state_ref)
        ext_ref[0:8, :] = jnp.zeros((8, ext_ref.shape[1]), F32)

    start_col = startc_ref[...]
    start_row = startr_ref[...]
    ext_ref[pl.ds(8, BLOCK), :] = proj_ref[:, xat:dat]
    place = wide_place(start_col, base, dat - xat)
    pre = conv_sum(ext_ref, taps_ref[...], bias_ref[...], place)
    ext_ref[0:8, :] = ext_ref[pl.ds(BLOCK, 8), :]
    conv = (pre * sigmoid(pre)).astype(BF16)
    x_low, b_low, c_low = conv[:, :channels], conv[:, channels : channels + NS], conv[:, channels + NS :]
    x_val = x_low.astype(F32)
    _, step, _, linked, _, cum, enter, tail = decay_terms(
        proj_ref[:, dat:width], dtb_ref[...], rate_ref[...], start_row, start_col, base
    )
    contact = mm_nt(c_low, b_low)
    cum_cols = spread(cum, heads * LANES, LANES)
    enter_x = spread(enter, channels, PD)
    weight_x = spread(tail * step, channels, PD)
    low = iota((BLOCK, LANES), 1) < PD
    zero = jnp.zeros((BLOCK, LANES), F32)
    within = []
    for pair in range(heads // 2):
        mixes = []
        for head in (2 * pair, 2 * pair + 1):
            gap = cum_cols[:, head * LANES : (head + 1) * LANES] - cum[head : head + 1]
            decay = jnp.exp(jnp.where(linked, gap, NEG))
            mixes.append((decay * (contact * step[head : head + 1])).astype(BF16))
        x_pair = x_val[:, pair * LANES : (pair + 1) * LANES]
        both = jnp.concatenate([jnp.where(low, x_pair, zero), jnp.where(low, zero, x_pair)], axis=0).astype(BF16)
        within.append(mm(jnp.concatenate(mixes, axis=1), both))
    state = state_ref[...]
    state_low = state.astype(BF16)
    state_out_ref[0] = state_low
    y = jnp.concatenate(within, axis=1) + enter_x * mm(c_low, state_low) + skip_ref[...] * x_val
    y_ref[...] = y
    state_ref[...] = mm_tn(b_low, (weight_x * x_val).astype(BF16)) + enter_x[BLOCK - 1 :] * state
    z = proj_ref[:, zat:xat]
    gated = y * (z * sigmoid(z))
    gated_ref[...] = gated
    square = gated * gated
    high = square.astype(BF16)
    rest = (square - high.astype(F32)).astype(BF16)
    ones = jnp.ones((16, channels), BF16)
    ssq_ref[...] = (mm_nt(ones, high) + mm_nt(ones, rest))[:8]


def scan_bwd_kernel(
    cols,
    proj_ref,
    prev_ref,
    startc_ref,
    startr_ref,
    taps_ref,
    bias_ref,
    dtb_ref,
    rate_ref,
    skip_ref,
    y_ref,
    state_in_ref,
    grad_ref,
    stats_ref,
    gain_ref,
    out_ref,
    conv_acc_ref,
    head_acc_ref,
    skip_acc_ref,
    dstate_ref,
    ext_ref,
    dext_ref,
    pext_ref,
):
    zat, xat, dat, width = cols
    channels = xat - zat
    heads = channels // PD
    turn = pl.program_id(0)
    block = pl.num_programs(0) - 1 - turn
    base = block * BLOCK

    @pl.when(turn == 0)
    def _():
        dstate_ref[...] = jnp.zeros_like(dstate_ref)
        conv_acc_ref[...] = jnp.zeros_like(conv_acc_ref)
        head_acc_ref[...] = jnp.zeros_like(head_acc_ref)
        skip_acc_ref[...] = jnp.zeros_like(skip_acc_ref)
        dext_ref[pl.ds(BLOCK, 8), :] = jnp.zeros((8, dext_ref.shape[1]), F32)
        pext_ref[pl.ds(BLOCK, 8), :] = jnp.zeros((8, LANES), jnp.int32)

    start_col = startc_ref[...]
    start_row = startr_ref[...]
    taps = taps_ref[...]
    ext_ref[0:8, :] = prev_ref[:, xat:dat]
    ext_ref[pl.ds(8, BLOCK), :] = proj_ref[:, xat:dat]
    place = wide_place(start_col, base, dat - xat)
    pre = conv_sum(ext_ref, taps, bias_ref[...], place)
    pre_sig = sigmoid(pre)
    conv = (pre * pre_sig).astype(BF16)
    x_low, b_low, c_low = conv[:, :channels], conv[:, channels : channels + NS], conv[:, channels + NS :]
    x_val = x_low.astype(F32)
    rate = rate_ref[...]
    dt_rows, step, log_decay, linked, linked_low, cum, enter, tail = decay_terms(
        proj_ref[:, dat:width], dtb_ref[...], rate, start_row, start_col, base
    )
    contact = mm_nt(c_low, b_low)
    cum_cols = spread(cum, heads * LANES, LANES)
    enter_x = spread(enter, channels, PD)
    weight = tail * step
    weight_x = spread(weight, channels, PD)

    z = proj_ref[:, zat:xat]
    z_sig = sigmoid(z)
    z_silu = z * z_sig
    y_val = y_ref[...]
    stats = spread(stats_ref[...], 2 * channels, channels)
    scale_x, inner_x = stats[:, :channels], stats[:, channels:]
    grad = scale_x * (grad_ref[...] * gain_ref[...] - y_val * z_silu * scale_x * inner_x)
    dy = grad * z_silu
    out_ref[:, :channels] = (grad * y_val * (z_sig * (1.0 + z * (1.0 - z_sig)))).astype(BF16)

    low = iota((BLOCK, LANES), 1) < PD
    strict = linked & (iota((BLOCK, BLOCK), 0) > iota((BLOCK, BLOCK), 1))
    zero = jnp.zeros((BLOCK, LANES), F32)
    dcontact = zero
    dx_parts, w_parts, step_rows = [], [], []
    for pair in range(heads // 2):
        lanes = slice(pair * LANES, (pair + 1) * LANES)
        dy_pair = dy[:, lanes]
        dy_both = jnp.concatenate([jnp.where(low, dy_pair, zero), jnp.where(low, zero, dy_pair)], axis=0).astype(BF16)
        outer = mm_nt(dy_both, x_low[:, lanes])
        mixes = []
        for slot in range(2):
            head = 2 * pair + slot
            gap = cum_cols[:, head * LANES : (head + 1) * LANES] - cum[head : head + 1]
            decay = jnp.exp(jnp.where(linked, gap, NEG))
            step_row = step[head : head + 1]
            share = outer[slot * BLOCK : (slot + 1) * BLOCK] * decay
            dcontact = dcontact + share * step_row
            flow = share * contact
            step_rows.append(jnp.sum(flow, axis=0, keepdims=True))
            w_parts.append(jnp.where(strict, flow * step_row, 0.0).astype(BF16))
            mixes.append((decay * (contact * step_row)).astype(BF16))
        dx_parts.append(mm_tn(jnp.concatenate(mixes, axis=0), dy_both))
    pad = [jnp.zeros((8 - heads, BLOCK), F32)] if heads < 8 else []
    dstep = jnp.concatenate(step_rows + pad, axis=0)
    pick_rows = (iota((16, heads * BLOCK), 1) // BLOCK) == iota((16, heads * BLOCK), 0)
    pick_rows = jnp.where(pick_rows, 1.0, 0.0).astype(BF16)
    dcum = mm_nt(pick_rows, jnp.concatenate(w_parts, axis=1))[:8]
    dcum = dcum - mm(pick_rows, jnp.concatenate(w_parts, axis=0))[:8]

    state_low = state_in_ref[0]
    dstate = dstate_ref[...]
    dstate_low = dstate.astype(BF16)
    pick_x = (iota((16, channels), 1) // PD) == iota((16, channels), 0)
    pick_f = jnp.where(pick_x, 1.0, 0.0)
    pick_x = pick_f.astype(BF16)
    from_state = enter_x * mm(c_low, state_low)
    dcum = dcum + mm_nt(pick_x, (dy * from_state).astype(BF16))[:8]
    dye = (enter_x * dy).astype(BF16)
    through = mm(b_low, dstate_low)
    dweight = mm_nt(pick_x, (x_val * through).astype(BF16))[:8]
    wx = (weight_x * x_val).astype(BF16)
    kept_x = enter_x[BLOCK - 1 :]
    dkept = jnp.sum(dstate * state_low.astype(F32), axis=0, keepdims=True) * kept_x
    dkept = jnp.sum(pick_f[:8] * dkept, axis=1, keepdims=True)
    moved = dweight * weight
    lane = iota((8, BLOCK), 1)
    dlast = jnp.sum(moved, axis=1, keepdims=True) + dkept
    dcum = dcum - moved + jnp.where(lane == BLOCK - 1, dlast, 0.0)
    dstep = dstep + dweight * tail
    dc = mm_nt(dye, state_low)
    db = mm_nt(wx, dstate_low)
    dstate_ref[...] = mm_tn(c_low, dye) + kept_x * dstate
    dcontact_low = dcontact.astype(BF16)
    dc = dc + mm(dcontact_low, b_low)
    db = db + mm_tn(dcontact_low, c_low)
    dx = jnp.concatenate(dx_parts, axis=1) + weight_x * through + skip_ref[...] * dy

    dlog = mm(split3(dcum), linked_low)
    dlog = dlog[0:8] + dlog[8:16] + dlog[16:24]
    dstep = dstep - dlog * rate
    ddt = dstep * sigmoid(dt_rows)
    head_acc_ref[0:8, :] += ddt
    head_acc_ref[8:16, :] += dlog * log_decay
    skip_acc_ref[0:1, :] += jnp.sum(dy * x_val, axis=0, keepdims=True)
    ddt_cols = jnp.transpose(jnp.concatenate([ddt, jnp.zeros((BLOCK - 8, BLOCK), F32)], axis=0))
    out_ref[:, dat - zat : width - zat] = ddt_cols.astype(BF16)

    dpre = jnp.concatenate([dx, db, dc], axis=1) * (pre_sig * (1.0 + pre * (1.0 - pre_sig)))
    conv_acc_ref[KW : KW + 1, :] += jnp.sum(dpre, axis=0, keepdims=True)
    dext_ref[0:BLOCK, :] = dpre
    pext_ref[0:BLOCK, :] = iota((BLOCK, BLOCK), 0) + base - start_col
    draw = taps[KW - 1 : KW] * dpre
    conv_acc_ref[KW - 1 : KW, :] += jnp.sum(dpre * ext_ref[pl.ds(8, BLOCK), :], axis=0, keepdims=True)
    for offset in range(1, KW):
        tap = KW - 1 - offset
        kept = jnp.where(place >= offset, dpre * ext_ref[pl.ds(8 - offset, BLOCK), :], 0.0)
        conv_acc_ref[tap : tap + 1, :] += jnp.sum(kept, axis=0, keepdims=True)
        later = pext_ref[pl.ds(offset, BLOCK), :]
        later = jnp.concatenate([later] * ((dat - xat) // LANES), axis=1)
        draw = draw + jnp.where(later >= offset, taps[tap : tap + 1] * dext_ref[pl.ds(offset, BLOCK), :], 0.0)
    dext_ref[pl.ds(BLOCK, 8), :] = dext_ref[0:8, :]
    pext_ref[pl.ds(BLOCK, 8), :] = pext_ref[0:8, :]
    out_ref[:, xat - zat : dat - zat] = draw.astype(BF16)


def scan_specs(cols, turn):
    zat, xat, dat, width = cols
    channels = xat - zat
    conv_width = dat - xat
    fixed = lambda shape: pl.BlockSpec(shape, lambda c: (0,) * len(shape))
    params = [
        fixed((8, conv_width)),
        fixed((1, conv_width)),
        fixed((8, LANES)),
        fixed((8, LANES)),
        fixed((1, channels)),
    ]
    starts = [
        pl.BlockSpec((BLOCK, LANES), lambda c: (turn(c), 0)),
        pl.BlockSpec((8, BLOCK), lambda c: (0, turn(c))),
    ]
    return starts, params


def scan_forward(cols, proj, start_col, start_row, params):
    zat, xat, dat, width = cols
    channels = xat - zat
    length = proj.shape[0]
    blocks = length // BLOCK
    starts, param_specs = scan_specs(cols, lambda c: c)
    body = lambda *refs: scan_fwd_kernel(cols, *refs)
    return pl.pallas_call(
        body,
        grid=(blocks,),
        in_specs=[pl.BlockSpec((BLOCK, width), lambda c: (c, 0))] + starts + param_specs,
        out_specs=[
            pl.BlockSpec((BLOCK, channels), lambda c: (c, 0)),
            pl.BlockSpec((BLOCK, channels), lambda c: (c, 0)),
            pl.BlockSpec((1, NS, channels), lambda c: (c, 0, 0)),
            pl.BlockSpec((8, BLOCK), lambda c: (0, c)),
        ],
        out_shape=[
            jax.ShapeDtypeStruct((length, channels), F32),
            jax.ShapeDtypeStruct((length, channels), F32),
            jax.ShapeDtypeStruct((blocks, NS, channels), BF16),
            jax.ShapeDtypeStruct((8, length), F32),
        ],
        scratch_shapes=[
            pltpu.VMEM((NS, channels), F32),
            pltpu.VMEM((BLOCK + 8, dat - xat), F32),
        ],
        compiler_params=pltpu.CompilerParams(vmem_limit_bytes=24 * MIB),
        cost_estimate=pl.CostEstimate(flops=2 * 10**9, bytes_accessed=10**7, transcendentals=2 * 10**6),
        name="scan_fwd",
    )(proj, start_col, start_row, *params)


def scan_backward(cols, proj, start_col, start_row, params, y, states, grad, stats, gain):
    zat, xat, dat, width = cols
    channels = xat - zat
    length = proj.shape[0]
    blocks = length // BLOCK
    turn = lambda c: blocks - 1 - c
    starts, param_specs = scan_specs(cols, turn)
    body = lambda *refs: scan_bwd_kernel(cols, *refs)
    tall = BLOCK // 8
    return pl.pallas_call(
        body,
        grid=(blocks,),
        in_specs=[
            pl.BlockSpec((BLOCK, width), lambda c: (turn(c), 0)),
            pl.BlockSpec((8, width), lambda c: (jnp.maximum(turn(c) * tall - 1, 0), 0)),
        ]
        + starts
        + param_specs
        + [
            pl.BlockSpec((BLOCK, channels), lambda c: (turn(c), 0)),
            pl.BlockSpec((1, NS, channels), lambda c: (turn(c), 0, 0)),
            pl.BlockSpec((BLOCK, channels), lambda c: (turn(c), 0)),
            pl.BlockSpec((8, BLOCK), lambda c: (0, turn(c))),
            pl.BlockSpec((1, channels), lambda c: (0, 0)),
        ],
        out_specs=[
            pl.BlockSpec((BLOCK, width - zat), lambda c: (turn(c), 0)),
            pl.BlockSpec((8, dat - xat), lambda c: (0, 0)),
            pl.BlockSpec((16, LANES), lambda c: (0, 0)),
            pl.BlockSpec((8, channels), lambda c: (0, 0)),
        ],
        out_shape=[
            jax.ShapeDtypeStruct((length, width - zat), BF16),
            jax.ShapeDtypeStruct((8, dat - xat), F32),
            jax.ShapeDtypeStruct((16, LANES), F32),
            jax.ShapeDtypeStruct((8, channels), F32),
        ],
        scratch_shapes=[
            pltpu.VMEM((NS, channels), F32),
            pltpu.VMEM((BLOCK + 8, dat - xat), F32),
            pltpu.VMEM((BLOCK + 8, dat - xat), F32),
            pltpu.VMEM((BLOCK + 8, LANES), jnp.int32),
        ],
        compiler_params=pltpu.CompilerParams(vmem_limit_bytes=24 * MIB),
        cost_estimate=pl.CostEstimate(flops=6 * 10**9, bytes_accessed=2 * 10**7, transcendentals=3 * 10**6),
        name="scan_bwd",
    )(proj, proj, start_col, start_row, *params, y, states, grad, stats, gain)


def turned(ref, own):
    eye = jnp.where(iota((own, own), 0) == iota((own, own), 1), 1.0, 0.0).astype(BF16)
    return mm_nt(eye, ref[...]).astype(BF16)


def pack_mixer_kernel(cols, place_ref, q_ref, kv_ref, z_ref, x_ref, bc_ref, dt_ref, one_ref, two_ref, att_ref, mix_ref, out_ref):
    zat, xat, dat, width = cols
    own, qwidth = q_ref.shape
    channels = xat - zat
    out_ref[:, :qwidth] = q_ref[...]
    kv = kv_ref[...].astype(F32)
    keys, vals = kv[:, :LANES], kv[:, LANES:]
    first = place_ref[0] == 0
    keys = jnp.where(first, keys, pltpu.roll(keys, HD, 1))
    vals = jnp.where(first, pltpu.roll(vals, HD, 1), vals)
    out_ref[:, qwidth:zat] = jnp.where(iota((own, LANES), 1) < HD, keys, vals).astype(BF16)
    out_ref[:, zat:xat] = z_ref[...]
    out_ref[:, xat : xat + channels] = x_ref[...]
    out_ref[:, xat + channels : dat] = bc_ref[...]
    row, lane = iota((16, LANES), 0), iota((16, LANES), 1)
    pick = jnp.where((lane == row + HD) & (row < 2), 1.0, 0.0).astype(BF16)
    gains = iota((16, own), 0)
    gains = jnp.where(gains == 0, one_ref[...].astype(F32), jnp.where(gains == 1, two_ref[...].astype(F32), 0.0))
    out_ref[:, dat:width] = mm_tn(gains.astype(BF16), pick).astype(BF16)
    out_ref[:, dat : dat + dt_ref.shape[1]] = dt_ref[...]
    out_ref[:, width : width + qwidth] = turned(att_ref, own)
    out_ref[:, width + qwidth :] = turned(mix_ref, own)


def pack_mixer(cols, kv_head, *shards):
    own, qwidth = shards[0].shape
    zat, xat, dat, width = cols
    body = lambda *refs: pack_mixer_kernel(cols, *refs)
    whole = lambda shape: pl.BlockSpec(shape, lambda i: (0, 0))
    shape = (own, width + qwidth + xat - zat)
    return pl.pallas_call(
        body,
        grid=(1,),
        in_specs=[pl.BlockSpec(memory_space=pltpu.SMEM)] + [whole(shard.shape) for shard in shards],
        out_specs=whole(shape),
        out_shape=jax.ShapeDtypeStruct(shape, BF16),
        compiler_params=pltpu.CompilerParams(vmem_limit_bytes=60 * MIB),
        cost_estimate=pl.CostEstimate(flops=10**7, bytes_accessed=10**6, transcendentals=0),
        name="pack_mixer",
    )(kv_head, *shards)


def pack_ffn_kernel(gate_ref, up_ref, down_ref, out_ref):
    own, hidden = gate_ref.shape
    out_ref[:, :hidden] = gate_ref[...]
    out_ref[:, hidden : 2 * hidden] = up_ref[...]
    out_ref[:, 2 * hidden :] = turned(down_ref, own)


def pack_ffn(gate, up, down):
    own, hidden = gate.shape
    whole = lambda shape: pl.BlockSpec(shape, lambda i: (0, 0))
    shape = (own, 3 * hidden)
    return pl.pallas_call(
        pack_ffn_kernel,
        grid=(1,),
        in_specs=[whole(gate.shape), whole(up.shape), whole(down.shape)],
        out_specs=whole(shape),
        out_shape=jax.ShapeDtypeStruct(shape, BF16),
        compiler_params=pltpu.CompilerParams(vmem_limit_bytes=60 * MIB),
        cost_estimate=pl.CostEstimate(flops=10**7, bytes_accessed=10**6, transcendentals=0),
        name="pack_ffn",
    )(gate, up, down)


def piece_at(rank_ref, refs, shift):
    if shift == 0:
        return refs[0][...]
    below, above = refs[2 * shift - 1][...], refs[2 * shift][...]
    return jnp.where(rank_ref[0] >= shift, below, above)


def norm_kernel(parts, rank_ref, *refs):
    gain_ref, out_ref = refs[2 * parts - 1], refs[2 * parts]
    rows = refs[0].shape[0]
    gain = gain_ref[...]
    for shift in range(parts):
        values = piece_at(rank_ref, refs, shift).astype(F32)
        spot = lax.rem(rank_ref[0] + (parts - shift), parts) * rows
        out_ref[pl.ds(pl.multiple_of(spot, rows), rows), :] = (values * rms_scale(values) * gain).astype(BF16)


def norm_rows(rank, parts, pieces, gain):
    rows, model = pieces[0].shape
    body = lambda *refs: norm_kernel(parts, *refs)
    whole = lambda shape: pl.BlockSpec(shape, lambda i: (0, 0))
    return pl.pallas_call(
        body,
        grid=(1,),
        in_specs=[pl.BlockSpec(memory_space=pltpu.SMEM)]
        + [whole((rows, model))] * len(pieces)
        + [whole((1, model))],
        out_specs=whole((parts * rows, model)),
        out_shape=jax.ShapeDtypeStruct((parts * rows, model), BF16),
        compiler_params=pltpu.CompilerParams(vmem_limit_bytes=24 * MIB),
        cost_estimate=pl.CostEstimate(flops=10**7, bytes_accessed=5 * 10**6, transcendentals=0),
        name="norm_rows",
    )(rank, *pieces, gain)


def branch_back_kernel(parts, rank_ref, *refs):
    count = 2 * parts - 1
    out_w_ref, am_ref, gain_ref, gatt_ref, gmix_ref, gow_ref, inner_ref, ggain_ref, sum_ref = refs[count:]
    rows = refs[0].shape[0]
    qwidth = gatt_ref.shape[1]
    sum_ref[...] = jnp.zeros_like(sum_ref)
    total = jnp.zeros((1, gmix_ref.shape[1]), F32)
    ones = jnp.ones((16, gmix_ref.shape[1]), BF16)
    for shift in range(parts):
        grads = piece_at(rank_ref, refs, shift)
        spot = pl.multiple_of(lax.rem(rank_ref[0] + (parts - shift), parts) * rows, rows)
        here = pl.ds(spot, rows)
        both = am_ref[here, :]
        grad_am = mm(grads, out_w_ref[...])
        gatt_ref[here, :] = grad_am[:, :qwidth].astype(BF16)
        grad_mixed = grad_am[:, qwidth:]
        gmix_ref[here, :] = grad_mixed
        product = grad_mixed * both[:, qwidth:].astype(F32)
        total = total + jnp.sum(product, axis=0, keepdims=True)
        high = product.astype(BF16)
        rest = (product - high.astype(F32)).astype(BF16)
        inner_ref[:, here] = (mm_nt(ones, high) + mm_nt(ones, rest))[:8]
        sum_ref[...] += mm_tn(grads, both)
    gow_ref[...] = sum_ref[...].astype(BF16)
    ggain_ref[...] = jnp.broadcast_to(total / gain_ref[...], ggain_ref.shape)


def branch_back(rank, parts, pieces, out_w, att_mixed, gain):
    rows, model = pieces[0].shape
    length, width = att_mixed.shape
    channels = gain.shape[1]
    body = lambda *refs: branch_back_kernel(parts, *refs)
    whole = lambda shape: pl.BlockSpec(shape, lambda i: (0, 0))
    shapes = [
        ((length, width - channels), BF16),
        ((length, channels), F32),
        ((model, width), BF16),
        ((8, length), F32),
        ((8, channels), F32),
    ]
    return pl.pallas_call(
        body,
        grid=(1,),
        in_specs=[pl.BlockSpec(memory_space=pltpu.SMEM)]
        + [whole((rows, model))] * len(pieces)
        + [whole((model, width)), whole((length, width)), whole((1, channels))],
        out_specs=[whole(shape) for shape, _ in shapes],
        out_shape=[jax.ShapeDtypeStruct(shape, dtype) for shape, dtype in shapes],
        scratch_shapes=[pltpu.VMEM((model, width), F32)],
        compiler_params=pltpu.CompilerParams(vmem_limit_bytes=32 * MIB),
        cost_estimate=pl.CostEstimate(flops=2 * 10**9, bytes_accessed=10**7, transcendentals=0),
        name="branch_back",
    )(rank, *pieces, out_w, att_mixed, gain)


def wgrad_kernel(step, own, core_ref, rows_ref, gq_ref, gkv_ref, grest_ref, gow_ref, theirs_ref, ours_ref):
    turn = pl.program_id(0)
    first = core_ref[0] == 0
    sources = []
    for ref in (gq_ref, gkv_ref, grest_ref, gow_ref):
        sources += [(ref, lane) for lane in range(0, ref.shape[1], LANES)]
    for index in range(len(sources) // step):

        @pl.when(turn == index)
        def _(index=index):
            lanes = sources[index * step : (index + 1) * step]
            at = 0
            while at < step:
                ref, lane = lanes[at]
                count = 1
                while at + count < step and lanes[at + count][0] is ref:
                    count += 1
                span = slice(lane, lane + count * LANES)
                to = slice(at * LANES, (at + count) * LANES)
                value = ref[:, span].astype(F32) if ref is gow_ref else mm_tn(rows_ref[...], ref[:, span])
                for chip in range(value.shape[0] // (2 * own)):
                    even = value[2 * chip * own : (2 * chip + 1) * own]
                    odd = value[(2 * chip + 1) * own : (2 * chip + 2) * own]
                    rows = slice(chip * own, (chip + 1) * own)
                    ours_ref[rows, to] = jnp.where(first, even, odd).astype(BF16)
                    theirs_ref[rows, to] = jnp.where(first, odd, even).astype(BF16)
                at += count


def mixer_wgrad(core, own, rows_one, grad_q, grad_kv, grad_rest, grad_out_w):
    length, model = rows_one.shape
    width = grad_q.shape[1] + grad_kv.shape[1] + grad_rest.shape[1] + grad_out_w.shape[1]
    step = 3
    whole = lambda shape: pl.BlockSpec(shape, lambda i: (0, 0))
    args = (rows_one, grad_q, grad_kv, grad_rest, grad_out_w)
    return pl.pallas_call(
        lambda *refs: wgrad_kernel(step, own, *refs),
        grid=(width // (step * LANES),),
        in_specs=[pl.BlockSpec(memory_space=pltpu.SMEM)] + [whole(arg.shape) for arg in args],
        out_specs=[pl.BlockSpec((model // 2, step * LANES), lambda i: (0, i))] * 2,
        out_shape=[jax.ShapeDtypeStruct((model // 2, width), BF16)] * 2,
        compiler_params=pltpu.CompilerParams(vmem_limit_bytes=32 * MIB),
        cost_estimate=pl.CostEstimate(flops=3 * 10**9, bytes_accessed=10**7, transcendentals=0),
        name="mixer_wgrad",
    )(core, *args)


EXTRA = 16


def back_proj_kernel(zat, rank_ref, gq_ref, gkv_ref, grest_ref, w_ref, rows_ref, gain_ref, two_ref, conv_ref, *refs):
    turn = pl.program_id(0)
    outs, share_ref = refs[:-1], refs[-1]
    qwidth = gq_ref.shape[1]
    rows = gq_ref.shape[0]
    term = mm_nt(gq_ref[...], w_ref[:, :qwidth]) + mm_nt(gkv_ref[...], w_ref[:, qwidth:zat])
    term = term + mm_nt(grest_ref[...], w_ref[:, zat:])
    share = jnp.sum(term * rows_ref[...].astype(F32), axis=0, keepdims=True) / gain_ref[...]

    @pl.when(turn == 0)
    def _():
        share_ref[...] = jnp.zeros_like(share_ref)
        share_ref[1:2, :] = two_ref[0:1, :]
        share_ref[8:16, 0 : 2 * NS] = conv_ref[:, conv_ref.shape[1] - 2 * NS :]

    share_ref[0:1, :] += share
    for index in range(len(outs)):

        @pl.when(turn == index)
        def _(index=index):
            outs[index][0:rows, :] = term.astype(outs[index].dtype)

    @pl.when(turn == pl.num_programs(0) - 1)
    def _():
        for out in outs:
            out[rows : rows + EXTRA, :] = share_ref[...].astype(out.dtype)


def back_proj(rank, parts, zat, width, grad_q, grad_kv, grad_rest, mixer_w, rows_one, gain, gain_two, conv_acc):
    length, model = rows_one.shape
    rows = length // parts
    at = lambda s, rank_ref: (lax.rem(rank_ref[0] + s, parts), 0)
    fixed = lambda s, rank_ref: (0, 0)
    spec = pltpu.PrefetchScalarGridSpec(
        num_scalar_prefetch=1,
        grid=(parts,),
        in_specs=[
            pl.BlockSpec((rows, grad_q.shape[1]), at),
            pl.BlockSpec((rows, grad_kv.shape[1]), at),
            pl.BlockSpec((rows, grad_rest.shape[1]), at),
            pl.BlockSpec((model, width), fixed),
            pl.BlockSpec((rows, model), at),
            pl.BlockSpec((1, model), fixed),
            pl.BlockSpec(gain_two.shape, fixed),
            pl.BlockSpec(conv_acc.shape, fixed),
        ],
        out_specs=[pl.BlockSpec((rows + EXTRA, model), fixed)] * parts,
        scratch_shapes=[pltpu.VMEM((EXTRA, model), F32)],
    )
    return pl.pallas_call(
        lambda *refs: back_proj_kernel(zat, *refs),
        grid_spec=spec,
        out_shape=[jax.ShapeDtypeStruct((rows + EXTRA, model), F32)]
        + [jax.ShapeDtypeStruct((rows + EXTRA, model), BF16)] * (parts - 1),
        compiler_params=pltpu.CompilerParams(vmem_limit_bytes=32 * MIB),
        cost_estimate=pl.CostEstimate(flops=3 * 10**9, bytes_accessed=10**7, transcendentals=0),
        name="back_proj",
    )(rank, grad_q, grad_kv, grad_rest, mixer_w, rows_one, gain, gain_two, conv_acc)


def ffn_kernel(middle_ref, cot_ref, gain_ref, w_ref, out_ref, gmid_ref, glow_ref, ggain_ref, gw_ref, low_ref, sum_ref, gsum_ref):
    step = pl.program_id(0)
    hidden = w_ref.shape[1] // 3

    @pl.when(step == 0)
    def _():
        middle = middle_ref[...]
        low_ref[...] = (middle * rms_scale(middle) * gain_ref[...]).astype(BF16)
        sum_ref[...] = jnp.zeros_like(sum_ref)
        gsum_ref[...] = jnp.zeros_like(gsum_ref)

    low = low_ref[...]
    cot = cot_ref[...]
    gate_pre = mm(low, w_ref[:, :hidden])
    up_pre = mm(low, w_ref[:, hidden : 2 * hidden])
    sig = sigmoid(gate_pre)
    silu_gate = gate_pre * sig
    act = (silu_gate * up_pre).astype(BF16)
    sum_ref[...] += mm_nt(act, w_ref[:, 2 * hidden :])
    gw_ref[:, 2 * hidden :] = mm_tn(cot, act).astype(BF16)
    grad_hidden = mm(cot, w_ref[:, 2 * hidden :])
    grad_gate = (grad_hidden * up_pre * sig * (1.0 + gate_pre * (1.0 - sig))).astype(BF16)
    grad_up = (grad_hidden * silu_gate).astype(BF16)
    gw_ref[:, :hidden] = mm_tn(low, grad_gate).astype(BF16)
    gw_ref[:, hidden : 2 * hidden] = mm_tn(low, grad_up).astype(BF16)
    gsum_ref[...] += mm_nt(grad_gate, w_ref[:, :hidden]) + mm_nt(grad_up, w_ref[:, hidden : 2 * hidden])

    @pl.when(step == pl.num_programs(0) - 1)
    def _():
        middle = middle_ref[...]
        out_ref[...] = (middle + sum_ref[...]).astype(BF16)
        scale = rms_scale(middle)
        normed = middle * scale
        grad_two = gsum_ref[...]
        ggain_ref[...] = jnp.broadcast_to(jnp.sum(grad_two * normed, axis=0, keepdims=True), ggain_ref.shape)
        grad_middle = cot_ref[...].astype(F32) + norm_back(grad_two * gain_ref[...], normed, scale)
        gmid_ref[...] = grad_middle
        glow_ref[...] = grad_middle.astype(BF16)


def ffn_both(middle, cotangent, gain, ffn_w, parts):
    rows, model = middle.shape
    piece = ffn_w.shape[1] // parts
    rowspec = pl.BlockSpec((rows, model), lambda s: (0, 0))
    wspec = pl.BlockSpec((model, piece), lambda s: (0, s))
    return pl.pallas_call(
        ffn_kernel,
        grid=(parts,),
        in_specs=[rowspec, rowspec, pl.BlockSpec((1, model), lambda s: (0, 0)), wspec],
        out_specs=[rowspec, rowspec, rowspec, pl.BlockSpec((8, model), lambda s: (0, 0)), wspec],
        out_shape=[
            jax.ShapeDtypeStruct((rows, model), BF16),
            jax.ShapeDtypeStruct((rows, model), F32),
            jax.ShapeDtypeStruct((rows, model), BF16),
            jax.ShapeDtypeStruct((8, model), F32),
            jax.ShapeDtypeStruct(ffn_w.shape, BF16),
        ],
        scratch_shapes=[
            pltpu.VMEM((rows, model), BF16),
            pltpu.VMEM((rows, model), F32),
            pltpu.VMEM((rows, model), F32),
        ],
        compiler_params=pltpu.CompilerParams(vmem_limit_bytes=60 * MIB),
        cost_estimate=pl.CostEstimate(flops=10**10, bytes_accessed=3 * 10**7, transcendentals=10**6),
        name="ffn_both",
    )(middle, cotangent, gain, ffn_w)


def lane_rows(values, rows):
    padded = jnp.pad(values, (0, rows - values.shape[0]))
    return jnp.broadcast_to(padded[:, None], (rows, LANES))


def shifted(values, axis, size, shift):
    return lax.ppermute(values, axis, [(i, (i + shift) % size) for i in range(size)])


def sent(values, pairs):
    return lax.ppermute(values, "tensor", pairs)


def after(values, *earlier):
    return lax.optimization_barrier((values, earlier))[0]


def first_phase(values, parts):
    up = [(i, i + 1) for i in range(parts - 1)]
    return sent(values, up), sent(values, [(j, i) for i, j in up])


def second_phase(values, firsts, parts):
    first_up, first_down = firsts
    if parts == 4:
        below = [first_up, sent(first_up, [(1, 2), (2, 3)]), sent(first_up, [(1, 3)])]
        above = [first_down, sent(first_down, [(2, 1), (1, 0)]), sent(first_down, [(2, 0)])]
    else:
        up = lambda shift: [(i, i + shift) for i in range(parts - shift)]
        below = [first_up] + [sent(values, up(shift)) for shift in range(2, parts)]
        above = [first_down] + [sent(values, [(j, i) for i, j in up(shift)]) for shift in range(2, parts)]
    pieces = [values]
    for shift in range(1, parts):
        pieces += [below[shift - 1], above[parts - shift - 1]]
    return pieces


def sum_first(terms, parts):
    if parts != 4:
        return [shifted(terms[shift].astype(BF16), "tensor", parts, shift) for shift in range(1, parts)]
    low = lambda value: value.astype(BF16)
    up = [sent(low(terms[2]), [(0, 1), (1, 2)]), sent(low(terms[3]), [(0, 2)])]
    return up + [sent(low(terms[2]), [(3, 2), (2, 1)]), sent(low(terms[1]), [(3, 1)])]


def sum_second(terms, firsts, parts):
    if parts != 4:
        return firsts
    firsts = [first.astype(F32) for first in firsts]
    up = terms[1].astype(F32) + firsts[0] + firsts[1]
    down = terms[3].astype(F32) + firsts[2] + firsts[3]
    return [
        sent(up.astype(BF16), [(0, 1), (1, 2), (2, 3)]),
        sent(down.astype(BF16), [(3, 2), (2, 1), (1, 0)]),
    ]


def sum_last(terms, seconds):
    total = terms[0].astype(F32)
    for second in seconds:
        total = total + second.astype(F32)
    return total


def chip_total(theirs, ours, earlier):
    size = lax.axis_size("dp")
    theirs = after(lax.ppermute(theirs, "dp", [(i, i ^ 1) for i in range(size)]), earlier)
    return (ours.astype(F32) + theirs.astype(F32)).astype(BF16)


def sum_over_chips(values):
    size = lax.axis_size("dp")
    groups = [list(range(core, size, 2)) for core in range(2)]
    return lax.psum_scatter(values, "dp", scatter_dimension=0, axis_index_groups=groups, tiled=True)


def rows_of(values, rank, shift, parts):
    rows = values.shape[0] // parts
    return lax.dynamic_slice(values, (lax.rem(rank + shift, parts) * rows, 0), (rows, values.shape[1]))


def group_total(values, parts):
    total = values.astype(F32)
    for shift in range(1, parts):
        total = total + shifted(values, "tensor", parts, shift).astype(F32)
    return total


def butterfly(values, axis, size):
    if size & (size - 1):
        return lax.psum(values, axis)
    step = 1
    while step < size:
        values = values + lax.ppermute(values, axis, [(i, i ^ step) for i in range(size)])
        step *= 2
    return values


def local(
    x_in,
    cotangent,
    segments,
    norm_one,
    w_query,
    w_keyval,
    w_attn_out,
    w_zgate,
    w_xin,
    w_bcin,
    w_dtin,
    conv_x,
    conv_bc,
    bias_x,
    bias_bc,
    dt_bias,
    a_log,
    d_skip,
    ssm_gain,
    w_mix_out,
    norm_two,
    w_gate,
    w_up,
    w_down,
):
    parts = lax.axis_size("tensor")
    rank = lax.axis_index("tensor")
    own = w_query.shape[0]
    length = segments.shape[1]
    qwidth = w_query.shape[1]
    channels = w_zgate.shape[1]
    heads = w_dtin.shape[1]
    hidden_own = w_gate.shape[1]
    width_ssm = MH * PD
    kv_head = (rank * (qwidth // HD)) // (QH // KVH)
    zat = 2 * qwidth
    xat = zat + channels
    bat = xat + channels
    dat = bat + 2 * NS
    width = dat + LANES
    cols = (zat, xat, dat, width)

    mixer_own = pack_mixer(
        cols,
        kv_head.astype(jnp.int32)[None],
        w_query,
        w_keyval,
        w_zgate,
        w_xin,
        w_bcin,
        w_dtin,
        norm_one[None, :],
        norm_two[None, :],
        w_attn_out,
        w_mix_out,
    )
    mixer_w = lax.all_gather(mixer_own, "dp", axis=0, tiled=True)
    proj_w = mixer_w[:, :width]
    out_w = mixer_w[:, width:]
    gain_one = mixer_w[:, dat + HD].astype(F32)[None, :]
    gain_two = mixer_w[:, dat + HD + 1].astype(F32)[None, :]
    ffn_own = pack_ffn(w_gate, w_up, w_down)
    ffn_first, x_first = lax.optimization_barrier((first_phase(ffn_own, parts), first_phase(x_in, parts)))
    ffn_pieces = second_phase(ffn_own, ffn_first, parts)
    x_pieces = second_phase(x_in, x_first, parts)
    ffn_own = jnp.concatenate(
        ffn_pieces[:1]
        + [jnp.where(rank >= k, ffn_pieces[2 * k - 1], ffn_pieces[2 * k]) for k in range(1, parts)],
        axis=1,
    )
    ffn_w = lax.all_gather(ffn_own, "dp", axis=0, tiled=True)

    seg = segments[0]
    start = jnp.sum((seg[None, :] < seg[:, None]).astype(jnp.int32), axis=1)
    start_col = jnp.broadcast_to(start[:, None], (length, LANES))
    start_row = jnp.broadcast_to(start[None, :], (8, length))
    cosine, sine = rope_tables(length)
    taps = jnp.pad(jnp.concatenate([conv_x, conv_bc], axis=1), ((0, 8 - KW), (0, 0)))
    bias = jnp.concatenate([bias_x, bias_bc])[None, :]
    params = (taps, bias, lane_rows(dt_bias, 8), lane_rows(jnp.exp(a_log), 8), jnp.repeat(d_skip, PD)[None, :])

    residual = x_in.astype(F32)
    scale_one = rms_scale(residual)
    normed_one = residual * scale_one
    rank_arg = rank.astype(jnp.int32)[None]
    rows_one = norm_rows(rank_arg, parts, x_pieces, gain_one)
    proj = mm(rows_one, proj_w)
    y, gated, states, squares = scan_forward(cols, proj, start_col, start_row, params)
    attended, lse, low_q, low_kv = attn_forward(proj, cosine, sine, start_col)
    scale_ssm = lax.rsqrt(group_total(squares[:1], parts) / width_ssm + EPSILON)
    mixed = (gated * scale_ssm[0][:, None] * ssm_gain[None, :]).astype(BF16)
    att_mixed = jnp.concatenate([attended, mixed], axis=1)
    terms = [mm_nt(rows_of(att_mixed, rank, shift, parts), out_w) for shift in range(parts)]
    middle = residual + sum_last(terms, sum_second(terms, sum_first(terms, parts), parts))
    block_out, grad_middle, grad_low, grad_gain_two, grad_ffn_w = ffn_both(middle, cotangent, gain_two, ffn_w, parts)

    branch_pieces = second_phase(grad_low, first_phase(grad_low, parts), parts)
    grad_ffn_own = lax.psum_scatter(grad_ffn_w, "dp", scatter_dimension=0, tiled=True)
    piece = grad_ffn_own.shape[1] // parts
    ffn_terms = [grad_ffn_own[:, k * piece : (k + 1) * piece] for k in range(parts)]
    ffn_terms = ffn_terms[:1] + ffn_terms[:0:-1]

    grad_att, grad_mixed, grad_out_w, inner, grad_gain_ssm = branch_back(
        rank_arg, parts, branch_pieces, out_w, att_mixed, ssm_gain[None, :]
    )
    inner = group_total(inner[:1], parts) / width_ssm
    stats = jnp.concatenate([scale_ssm, inner, jnp.zeros((6, length), F32)], axis=0)
    grad_q, grad_kv = attn_backward(low_q, low_kv, lse, attended, grad_att, cosine, sine, start_col)
    grad_rest, conv_acc, head_acc, skip_acc = scan_backward(
        cols, proj, start_col, start_row, params, y, states, grad_mixed, stats, ssm_gain[None, :]
    )
    core = lax.rem(lax.axis_index("dp"), 2).astype(jnp.int32)[None]
    theirs, ours = mixer_wgrad(core, own, rows_one, grad_q, grad_kv, grad_rest, grad_out_w)
    terms = back_proj(
        rank_arg, parts, zat, width, grad_q, grad_kv, after(grad_rest, theirs), mixer_w, rows_one, gain_one, grad_gain_two, conv_acc
    )
    chip_share = chip_total(theirs, ours, terms)
    firsts = after(sum_first(terms, parts), chip_share, grad_ffn_own)
    seconds = sum_second(terms, firsts, parts)
    seconds, ffn_firsts = lax.optimization_barrier((seconds, sum_first(ffn_terms, parts)))
    grad_ffn = sum_last(ffn_terms, sum_second(ffn_terms, ffn_firsts, parts))
    summed = sum_last(terms, seconds)
    grad_one, shared_small = summed[:-EXTRA], summed[-EXTRA:]
    grad_input = grad_middle + norm_back(grad_one * gain_one, normed_one, scale_one)
    grad_w = after(sum_over_chips(chip_share), seconds).astype(F32)

    model = x_in.shape[1]
    wide = lambda rows: jnp.pad(rows, ((0, 0), (0, model - rows.shape[1])))
    head_sums = jnp.sum(head_acc, axis=1)[None, :]
    small = jnp.concatenate(
        [
            shared_small,
            wide(conv_acc),
            wide(grad_gain_ssm[:1]),
            wide(skip_acc[:1]),
            wide(head_sums),
            jnp.zeros((5, model), F32),
        ],
        axis=0,
    )
    small = butterfly(small, "dp", lax.axis_size("dp"))
    at = EXTRA
    grad_conv_x = small[at : at + KW, :channels]
    grad_bias_x = small[at + KW, :channels]
    grad_ssm_gain = small[at + 8, :channels]
    grad_d_skip = jnp.sum(small[at + 9, :channels].reshape(heads, PD), axis=1)
    grad_dt_bias = small[at + 10, :heads]
    grad_a_log = small[at + 10, 8 : 8 + heads]
    grad_conv_bc = small[8 : 8 + KW, : 2 * NS]
    grad_bias_bc = small[8 + KW, : 2 * NS]
    place = lax.axis_index("dp") * own
    norm_grads = lax.dynamic_slice(small, (0, place), (2, own))
    grad_norm_one, grad_norm_two = norm_grads[0], norm_grads[1]

    grad_keyval = jnp.zeros((own, 2 * KVH * HD), F32)
    grad_keyval = lax.dynamic_update_slice(grad_keyval, grad_w[:, qwidth : qwidth + HD], (0, kv_head * HD))
    grad_keyval = lax.dynamic_update_slice(
        grad_keyval, grad_w[:, qwidth + HD : zat], (0, (KVH + kv_head) * HD)
    )
    shared = jnp.concatenate([grad_keyval, grad_w[:, bat:dat]], axis=1)
    shared = group_total(shared.astype(BF16), parts)

    return (
        block_out,
        grad_input,
        grad_norm_one,
        grad_w[:, :qwidth],
        shared[:, : 2 * KVH * HD],
        grad_w[:, width : width + qwidth].T,
        grad_w[:, zat:xat],
        grad_w[:, xat:bat],
        shared[:, 2 * KVH * HD :],
        grad_w[:, dat : dat + heads],
        grad_conv_x,
        grad_conv_bc,
        grad_bias_x,
        grad_bias_bc,
        grad_dt_bias,
        grad_a_log,
        grad_d_skip,
        grad_ssm_gain,
        grad_w[:, width + qwidth :].T,
        grad_norm_two,
        grad_ffn[:, :hidden_own],
        grad_ffn[:, hidden_own : 2 * hidden_own],
        grad_ffn[:, 2 * hidden_own :].T,
    )


def solution(mesh):
    return jax.shard_map(
        local,
        mesh=mesh,
        in_specs=(
            P(("dp", "tensor"), None),
            P(("dp", "tensor"), None),
            P("dp", None),
            P("dp"),
            P("dp", "tensor"),
            P("dp", None),
            P("tensor", "dp"),
            P("dp", "tensor"),
            P("dp", "tensor"),
            P("dp", None),
            P("dp", "tensor"),
            P(None, "tensor"),
            P(),
            P("tensor"),
            P(),
            P("tensor"),
            P("tensor"),
            P("tensor"),
            P("tensor"),
            P("tensor", "dp"),
            P("dp"),
            P("dp", "tensor"),
            P("dp", "tensor"),
            P("tensor", "dp"),
        ),
        out_specs=(
            P(("dp", "tensor"), None),
            P(("dp", "tensor"), None),
            P("dp"),
            P("dp", "tensor"),
            P("dp", None),
            P("tensor", "dp"),
            P("dp", "tensor"),
            P("dp", "tensor"),
            P("dp", None),
            P("dp", "tensor"),
            P(None, "tensor"),
            P(),
            P("tensor"),
            P(),
            P("tensor"),
            P("tensor"),
            P("tensor"),
            P("tensor"),
            P("tensor", "dp"),
            P("dp"),
            P("dp", "tensor"),
            P("dp", "tensor"),
            P("tensor", "dp"),
        ),
        check_vma=False,
    )
```

profile of v0, /device:TPU:0, one launch (start us, length us, event | category | flops | bytes accessed | tf_op | source)
XLA Modules:
  0.0 406.1 jit_solution(16612194599915522737)
XLA Ops:
  7.2 1.4 copy.59.refs_6_
  8.7 2.2 pack_mixer.1
  10.9 5.0 %collective-permute-start.2 = (bf16[256,1024]{1,0:T(8,128)(2,1)}, bf16[256,1024]{1,0:T(8,128)(2,1)S(1)}, u32[]{:S(2)}, u32[]{:S(2)}) collective-permute-start(bf16[256,1024]{1,0:T(8,128)(2,1)} %refs_1_.3), channel_id=1, source_target_pairs={{0,1},{1,2},{2,3},{4,5},{5,6},{6,7},{8,9},{9,10},{10,11},{12,13},{... | collective-permute-start | bytes 1572872 | tf_op jit(solution)/shard_map/ppermute | solution.py:920
  17.2 2.0 pack_ffn.1
  19.2 4.7 %collective-permute-start = (bf16[128,1536]{1,0:T(8,128)(2,1)}, bf16[128,1536]{1,0:T(8,128)(2,1)S(1)}, u32[]{:S(2)}, u32[]{:S(2)}) collective-permute-start(bf16[128,1536]{1,0:T(8,128)(2,1)} %pack_ffn.1), channel_id=1, source_target_pairs={{0,1},{1,2},{2,3},{4,5},{5,6},{6,7},{8,9},{9,10},{10,11},{12,13},{... | collective-permute-start | bytes 1179656 | tf_op jit(solution)/shard_map/ppermute | solution.py:920
  25.2 10.6 %collective-permute-done = bf16[128,1536]{1,0:T(8,128)(2,1)S(1)} collective-permute-done((bf16[128,1536]{1,0:T(8,128)(2,1)}, bf16[128,1536]{1,0:T(8,128)(2,1)S(1)}, u32[]{:S(2)}, u32[]{:S(2)}) %collective-permute-start) | collective-permute-done | bytes 393248 | tf_op jit(solution)/shard_map/ppermute | solution.py:920
  35.8 4.0 collective-permute-done.1
  43.9 20.9 %collective-permute-done.17 = bf16[128,1536]{1,0:T(8,128)(2,1)S(1)} collective-permute-done((bf16[128,1536]{1,0:T(8,128)(2,1)S(1)}, bf16[128,1536]{1,0:T(8,128)(2,1)S(1)}, u32[]{:S(2)}, u32[]{:S(2)}) %collective-permute-start.17) | collective-permute-done | bytes 393248 | tf_op jit(solution)/shard_map/ppermute | solution.py:920
  69.8 1.5 collective-permute-start.7
  72.1 2.1 convert_reduce_fusion.1
  74.2 9.9 %collective-permute-done.4.refs_3_ = bf16[256,1024]{1,0:T(8,128)(2,1)S(1)} collective-permute-done((bf16[256,1024]{1,0:T(8,128)(2,1)S(1)}, bf16[256,1024]{1,0:T(8,128)(2,1)S(1)}, u32[]{:S(2)}, u32[]{:S(2)}) %collective-permute-start.4) | collective-permute-done | bytes 524320 | tf_op jit(solution)/shard_map/ppermute | solution.py:920
  85.7 6.1 %collective-permute-done.6.refs_5_ = bf16[256,1024]{1,0:T(8,128)(2,1)S(1)} collective-permute-done((bf16[256,1024]{1,0:T(8,128)(2,1)S(1)}, bf16[256,1024]{1,0:T(8,128)(2,1)S(1)}, u32[]{:S(2)}, u32[]{:S(2)}) %collective-permute-start.6) | collective-permute-done | bytes 524320 | tf_op jit(solution)/shard_map/ppermute | solution.py:920
  96.8 2.1 norm_rows.1.refs_1_.refs_5_
  99.2 3.4 fusion.q_ref.kv_ref.refs_0_.refs_1_
  103.0 8.2 %scan_fwd.1 = (f32[1024,384]{1,0:T(8,128)S(1)}, f32[1024,384]{1,0:T(8,128)S(1)}, bf16[8,128,384]{2,1,0:T(8,128)(2,1)S(1)}, f32[8,1024]{1,0:T(8,128)S(1)}) custom-call(f32[1024,1408]{1,0:T(8,128)S(1)} %fusion.q_ref.kv_ref.refs_0_.refs_1_, s32[1024,128]{1,0:T(8,128)S(1)} %broadcast_in_dim.70.start_ref.refs_1_.refs_2_, ...), custom_call_target="tpu_custom_call" | custom-call | flops 2000000000 | bytes 10000000 | tf_op jit(solution)/shard_map/scan_fwd/pallas_call | solution.py:497
  113.3 4.1 %collective-permute-start.10 = (f32[1,1024]{1,0:T(1,128)S(1)}, f32[1,1024]{1,0:T(1,128)S(1)}, u32[]{:S(2)}, u32[]{:S(2)}) collective-permute-start(f32[1,1024]{1,0:T(1,128)S(1)} %slice.117), channel_id=1, source_target_pairs={{0,3},{1,0},{2,1},{3,2},{4,7},{5,4},{6,5},{7,6},{8,11},{9,8},{10,9... | collective-permute-start | bytes 12296 | tf_op jit(solution)/shard_map/ppermute | solution.py:916
  118.2 4.4 %attn_fwd.1 = (bf16[1024,128]{1,0:T(8,128)(2,1)S(1)}, f32[1024,128]{1,0:T(8,128)S(1)}, bf16[1024,128]{1,0:T(8,128)(2,1)S(1)}, bf16[1024,128]{1,0:T(8,128)(2,1)S(1)}) custom-call(f32[1024,1408]{1,0:T(8,128)S(1)} %fusion.q_ref.kv_ref.refs_0_.refs_1_, f32[1024,1408]{1,0:T(8,128)S(1)} %fusion.q_ref.kv_ref.refs_0_.refs_1_, f32[1024,128]{1,0:T(8,128)S(1)} %copy-done.8, ...), custom_call_target="tpu_custom_call" | custom-call | flops 1000000000 | bytes 6000000 | tf_op jit(solution)/shard_map/attn_fwd/pallas_call | solution.py:165
  124.5 6.2 %collective-permute-start.11 = (bf16[256,1024]{1,0:T(8,128)(2,1)}, bf16[256,1024]{1,0:T(8,128)(2,1)}, u32[]{:S(2)}, u32[]{:S(2)}) collective-permute-start(bf16[256,1024]{1,0:T(8,128)(2,1)} %convolution_convert_fusion), channel_id=1, source_target_pairs={{0,1},{1,2},{4,5},{5,6},{8,9},{9,10},{12,13},{13,14},{16,17},{17,1... | collective-permute-start | bytes 1572872 | tf_op jit(solution)/shard_map/ppermute | solution.py:920
  130.7 1.6 fusion.36
  132.3 2.1 collective-permute-start.12
  135.2 7.3 %collective-permute-done.11 = bf16[256,1024]{1,0:T(8,128)(2,1)} collective-permute-done((bf16[256,1024]{1,0:T(8,128)(2,1)}, bf16[256,1024]{1,0:T(8,128)(2,1)}, u32[]{:S(2)}, u32[]{:S(2)}) %collective-permute-start.11) | collective-permute-done | bytes 524320 | tf_op jit(solution)/shard_map/ppermute | solution.py:920
  142.5 5.6 %collective-permute-done.12 = bf16[256,1024]{1,0:T(8,128)(2,1)} collective-permute-done((bf16[256,1024]{1,0:T(8,128)(2,1)}, bf16[256,1024]{1,0:T(8,128)(2,1)}, u32[]{:S(2)}, u32[]{:S(2)}) %collective-permute-start.12) | collective-permute-done | bytes 524320 | tf_op jit(solution)/shard_map/ppermute | solution.py:920
  148.2 2.9 add_convert_fusion.4
  151.7 2.1 collective-permute-start.13
  156.2 1.8 fusion.10
  158.0 2.0 collective-permute-done.13
  160.0 13.1 %collective-permute-done.16 = bf16[256,1024]{1,0:T(8,128)(2,1)} collective-permute-done((bf16[256,1024]{1,0:T(8,128)(2,1)}, bf16[256,1024]{1,0:T(8,128)(2,1)}, u32[]{:S(2)}, u32[]{:S(2)}) %collective-permute-start.16) | collective-permute-done | bytes 524320 | tf_op jit(solution)/shard_map/ppermute | solution.py:920
  173.1 2.5 fusion.8
  175.6 17.5 %ffn_both.1 = (bf16[256,1024]{1,0:T(8,128)(2,1)}, f32[256,1024]{1,0:T(8,128)}, bf16[256,1024]{1,0:T(8,128)(2,1)}, f32[8,1024]{1,0:T(8,128)}, bf16[1024,6144]{1,0:T(8,128)(2,1)}) custom-call(f32[256,1024]{1,0:T(8,128)} %get-tuple-element.202.middle_ref, bf16[256,1024]{1,0:T(8,128)(2,1)} %cot_ref.1, f32[1,1024]{1,0:T(1,128)} %bitcast.32, ...), custom_call_target="tpu_custom_call" | custom-call | flops 10000000000 | bytes 30000000 | tf_op jit(solution)/shard_map/ffn_both/pallas_call | solution.py:887
  194.5 5.4 %collective-permute-start.21 = (bf16[256,1024]{1,0:T(8,128)(2,1)}, bf16[256,1024]{1,0:T(8,128)(2,1)}, u32[]{:S(2)}, u32[]{:S(2)}) collective-permute-start(bf16[256,1024]{1,0:T(8,128)(2,1)} %get-tuple-element.82.refs_1_), channel_id=1, source_target_pairs={{0,1},{1,2},{2,3},{4,5},{5,6},{6,7},{8,9},{9,10},{10,11},{12,13},{... | collective-permute-start | bytes 1572872 | tf_op jit(solution)/shard_map/ppermute | solution.py:920
  199.9 12.5 %collective-permute-done.22.refs_7_ = bf16[256,1024]{1,0:T(8,128)(2,1)} collective-permute-done((bf16[256,1024]{1,0:T(8,128)(2,1)}, bf16[256,1024]{1,0:T(8,128)(2,1)}, u32[]{:S(2)}, u32[]{:S(2)}) %collective-permute-start.22) | collective-permute-done | bytes 524320 | tf_op jit(solution)/shard_map/ppermute | solution.py:920
  213.6 1.5 collective-permute-start.24
  216.4 1.7 collective-permute-start.26
  218.2 1.4 slice.155.refs_8_
  219.7 4.9 %collective-permute-done.23.refs_3_ = bf16[256,1024]{1,0:T(8,128)(2,1)} collective-permute-done((bf16[256,1024]{1,0:T(8,128)(2,1)}, bf16[256,1024]{1,0:T(8,128)(2,1)}, u32[]{:S(2)}, u32[]{:S(2)}) %collective-permute-start.23) | collective-permute-done | bytes 524320 | tf_op jit(solution)/shard_map/ppermute | solution.py:920
  224.6 6.1 %collective-permute-done.25.refs_5_ = bf16[256,1024]{1,0:T(8,128)(2,1)} collective-permute-done((bf16[256,1024]{1,0:T(8,128)(2,1)}, bf16[256,1024]{1,0:T(8,128)(2,1)}, u32[]{:S(2)}, u32[]{:S(2)}) %collective-permute-start.25) | collective-permute-done | bytes 524320 | tf_op jit(solution)/shard_map/ppermute | solution.py:920
  230.8 5.5 %branch_back.1 = (bf16[1024,128]{1,0:T(8,128)(2,1)S(1)}, f32[1024,384]{1,0:T(8,128)S(1)}, bf16[1024,512]{1,0:T(8,128)(2,1)S(1)}, f32[8,1024]{1,0:T(8,128)S(1)}, f32[8,384]{1,0:T(8,128)S(1)}) custom-call(s32[1]{0:T(128)} %bitcast.refs_0_, bf16[256,1024]{1,0:T(8,128)(2,1)S(1)} %copy-done.24, bf16[256,1024]{1,0:T(8,128)(2,1)} %collective-permute-done.21.refs_2_, ...), custom_call_target="tpu_custom_call" | custom-call | flops 2000000000 | bytes 10000000 | tf_op jit(solution)/shard_map/branch_back/pallas_call | solution.py:717
  236.3 2.5 collective-permute-start.27
  238.8 3.7 collective-permute-start.28
  242.5 6.6 %attn_bwd.1 = (bf16[1024,128]{1,0:T(8,128)(2,1)S(1)}, bf16[1024,128]{1,0:T(8,128)(2,1)S(1)}) custom-call(bf16[1024,128]{1,0:T(8,128)(2,1)S(1)} %copy-done.26, bf16[1024,128]{1,0:T(8,128)(2,1)S(1)} %copy-done.28, f32[1024,128]{1,0:T(8,128)S(1)} %copy-done.23, bf16[1024,128]{1,0:T(8,128)(2,1)S(1)} %get-tuple-element.72.out_ref, ...), custom_call_target="tpu_custom_call" | custom-call | flops 3000000000 | bytes 6000000 | tf_op jit(solution)/shard_map/attn_bwd/pallas_call | solution.py:185
  249.3 18.7 %scan_bwd.1 = (bf16[1024,1152]{1,0:T(8,128)(2,1)S(1)}, f32[8,640]{1,0:T(8,128)S(1)}, f32[16,128]{1,0:T(8,128)S(1)}, f32[8,384]{1,0:T(8,128)S(1)}) custom-call(f32[1024,1408]{1,0:T(8,128)S(1)} %bitcast.27, f32[1024,1408]{1,0:T(8,128)S(1)} %bitcast.27, s32[1024,128]{1,0:T(8,128)S(1)} %broadcast_in_dim.70.start_ref.refs_1_.refs_2_, ...), custom_call_target="tpu_custom_call" | custom-call | flops 6000000000 | bytes 20000000 | tf_op jit(solution)/shard_map/scan_bwd/pallas_call | solution.py:532
  268.1 6.1 %mixer_wgrad.1 = (bf16[512,1920]{1,0:T(8,128)(2,1)S(1)}, bf16[512,1920]{1,0:T(8,128)(2,1)S(1)}) custom-call(s32[1]{0:T(128)} %bitcast.6.refs_0_, bf16[1024,1024]{1,0:T(8,128)(2,1)S(1)} %norm_rows.1.refs_1_.refs_5_, bf16[1024,128]{1,0:T(8,128)(2,1)S(1)} %get-tuple-element.84.refs_2_.refs_1_, bf16[1024,128]{1,0:T(8,128)(2,1)S(1)} %get-tuple-element.85.refs_3_.refs_2_, ...), custom_call_target="tpu_custom_call" | custom-call | flops 3000000000 | bytes 10000000 | tf_op jit(solution)/shard_map/mixer_wgrad/pallas_call | solution.py:767
  274.2 5.1 %back_proj.1 = (f32[272,1024]{1,0:T(8,128)S(1)}, bf16[272,1024]{1,0:T(8,128)(2,1)S(1)}, bf16[272,1024]{1,0:T(8,128)(2,1)S(1)}, bf16[272,1024]{1,0:T(8,128)(2,1)S(1)}) custom-call(s32[1]{0:T(128)} %bitcast.refs_0_, bf16[1024,128]{1,0:T(8,128)(2,1)S(1)} %get-tuple-element.84.refs_2_.refs_1_, bf16[1024,128]{1,0:T(8,128)(2,1)S(1)} %get-tuple-element.85.refs_3_.refs_2_, ...), custom_call_target="tpu_custom_call" | custom-call | flops 3000000000 | bytes 10000000 | tf_op jit(solution)/shard_map/back_proj/pallas_call | solution.py:831
  281.9 1.8 add_convert_fusion
  284.7 3.9 collective-permute-start.30
  290.7 1.5 collective-permute-start.33
  292.2 9.4 %collective-permute-done.30 = bf16[272,1024]{1,0:T(8,128)(2,1)S(1)} collective-permute-done((bf16[272,1024]{1,0:T(8,128)(2,1)S(1)}, bf16[272,1024]{1,0:T(8,128)(2,1)S(1)}, u32[]{:S(2)}, u32[]{:S(2)}) %collective-permute-start.30) | collective-permute-done | bytes 557088 | tf_op jit(solution)/shard_map/ppermute | solution.py:920
  301.6 11.5 %collective-permute-done.31 = bf16[272,1024]{1,0:T(8,128)(2,1)S(1)} collective-permute-done((bf16[272,1024]{1,0:T(8,128)(2,1)S(1)}, bf16[272,1024]{1,0:T(8,128)(2,1)S(1)}, u32[]{:S(2)}, u32[]{:S(2)}) %collective-permute-start.31) | collective-permute-done | bytes 557088 | tf_op jit(solution)/shard_map/ppermute | solution.py:920
  314.7 2.5 add_convert_fusion.1
  317.2 1.4 collective-permute-start.36
  319.7 7.6 %collective-permute-start.37 = (bf16[128,1536]{1,0:T(8,128)(2,1)}, bf16[128,1536]{1,0:T(8,128)(2,1)}, u32[]{:S(2)}, u32[]{:S(2)}) collective-permute-start(bf16[128,1536]{1,0:T(8,128)(2,1)} %get-tuple-element.195), channel_id=1, source_target_pairs={{0,1},{1,2},{4,5},{5,6},{8,9},{9,10},{12,13},{13,14},{16,17},{17,1... | collective-permute-start | bytes 1179656 | tf_op jit(solution)/shard_map/ppermute | solution.py:920
  328.4 3.3 collective-permute-start.35
  332.4 5.3 %collective-permute-start.38 = (bf16[128,1536]{1,0:T(8,128)(2,1)}, bf16[128,1536]{1,0:T(8,128)(2,1)}, u32[]{:S(2)}, u32[]{:S(2)}) collective-permute-start(bf16[128,1536]{1,0:T(8,128)(2,1)} %get-tuple-element.194), channel_id=1, source_target_pairs={{0,2},{4,6},{8,10},{12,14},{16,18},{20,22},{24,26},{28,30}} | collective-permute-start | bytes 1179656 | tf_op jit(solution)/shard_map/ppermute | solution.py:920
  337.8 1.4 collective-permute-start.40
  339.9 14.3 %collective-permute-done.38 = bf16[128,1536]{1,0:T(8,128)(2,1)} collective-permute-done((bf16[128,1536]{1,0:T(8,128)(2,1)}, bf16[128,1536]{1,0:T(8,128)(2,1)}, u32[]{:S(2)}, u32[]{:S(2)}) %collective-permute-start.38) | collective-permute-done | bytes 393248 | tf_op jit(solution)/shard_map/ppermute | solution.py:920
  357.9 3.9 collective-permute-start.45
  361.8 3.2 collective-permute-start.46
  368.5 2.5 add_convert_fusion.6
  371.0 2.2 collective-permute-start.47
  374.7 1.5 copy.61
  380.8 1.8 collective-permute-start.42
  383.7 3.1 collective-permute-done.42
  386.8 1.8 collective-permute-start.43
  389.3 2.7 collective-permute-done.43
  (283 shorter events, 65.4 us)
Async XLA Ops:
  7.2 64.9 %all-gather.3.cloned.1.call-start = ((), (), s32[]{:S(2)}) async-start(), calls=%async_computation.2 | async-start | bytes 4423680 | tf_op jit(solution)/shard_map/all_gather | solution.py:1065
  10.9 164.7 %all-gather.5.cloned.1.call-start = ((), (), s32[]{:S(2)}) async-start(), calls=%async_computation.3 | async-start | bytes 14155776 | tf_op jit(solution)/shard_map/all_gather | solution.py:1079
  10.9 28.9 %collective-permute-start.2 = (bf16[256,1024]{1,0:T(8,128)(2,1)}, bf16[256,1024]{1,0:T(8,128)(2,1)S(1)}, u32[]{:S(2)}, u32[]{:S(2)}) collective-permute-start(bf16[256,1024]{1,0:T(8,128)(2,1)} %refs_1_.3), channel_id=1, source_target_pairs={{0,1},{1,2},{2,3},{4,5},{5,6},{6,7},{8,9},{9,10},{10,11},{12,13},{... | collective-permute-start | bytes 1572872 | tf_op jit(solution)/shard_map/ppermute | solution.py:920
  15.9 24.0 %collective-permute-start.3 = (bf16[256,1024]{1,0:T(8,128)(2,1)}, bf16[256,1024]{1,0:T(8,128)(2,1)S(1)}, u32[]{:S(2)}, u32[]{:S(2)}) collective-permute-start(bf16[256,1024]{1,0:T(8,128)(2,1)} %refs_1_.3), channel_id=1, source_target_pairs={{1,0},{2,1},{3,2},{5,4},{6,5},{7,6},{9,8},{10,9},{11,10},{13,12},{... | collective-permute-start | bytes 1572872 | tf_op jit(solution)/shard_map/ppermute | solution.py:920
  19.1 45.8 %copy-start.40 = (bf16[128,1536]{1,0:T(8,128)(2,1)S(1)}, bf16[128,1536]{1,0:T(8,128)(2,1)}, u32[]{:S(2)}) copy-start(bf16[128,1536]{1,0:T(8,128)(2,1)} %pack_ffn.1) | copy-start | bytes 1179652
  19.2 16.6 %collective-permute-start = (bf16[128,1536]{1,0:T(8,128)(2,1)}, bf16[128,1536]{1,0:T(8,128)(2,1)S(1)}, u32[]{:S(2)}, u32[]{:S(2)}) collective-permute-start(bf16[128,1536]{1,0:T(8,128)(2,1)} %pack_ffn.1), channel_id=1, source_target_pairs={{0,1},{1,2},{2,3},{4,5},{5,6},{6,7},{8,9},{9,10},{10,11},{12,13},{... | collective-permute-start | bytes 1179656 | tf_op jit(solution)/shard_map/ppermute | solution.py:920
  23.9 16.0 %collective-permute-start.1 = (bf16[128,1536]{1,0:T(8,128)(2,1)}, bf16[128,1536]{1,0:T(8,128)(2,1)S(1)}, u32[]{:S(2)}, u32[]{:S(2)}) collective-permute-start(bf16[128,1536]{1,0:T(8,128)(2,1)} %pack_ffn.1), channel_id=1, source_target_pairs={{1,0},{2,1},{3,2},{5,4},{6,5},{7,6},{9,8},{10,9},{11,10},{13,12},{... | collective-permute-start | bytes 1179656 | tf_op jit(solution)/shard_map/ppermute | solution.py:920
  39.8 28.6 %copy-start.12 = (bf16[256,1024]{1,0:T(8,128)(2,1)}, bf16[256,1024]{1,0:T(8,128)(2,1)S(1)}, u32[]{:S(2)}) copy-start(bf16[256,1024]{1,0:T(8,128)(2,1)S(1)} %collective-permute-done.3.refs_7_) | copy-start | bytes 1572868
  39.8 4.0 collective-permute-start.20
  40.5 24.3 %collective-permute-start.18 = (bf16[128,1536]{1,0:T(8,128)(2,1)S(1)}, bf16[128,1536]{1,0:T(8,128)(2,1)S(1)}, u32[]{:S(2)}, u32[]{:S(2)}) collective-permute-start(bf16[128,1536]{1,0:T(8,128)(2,1)S(1)} %collective-permute-done), channel_id=1, source_target_pairs={{1,2},{2,3},{5,6},{6,7},{9,10},{10,11},{13,14},{14,15},{17,18},{18... | collective-permute-start | bytes 1179656 | tf_op jit(solution)/shard_map/ppermute | solution.py:920
  41.2 23.7 %collective-permute-start.19 = (bf16[128,1536]{1,0:T(8,128)(2,1)S(1)}, bf16[128,1536]{1,0:T(8,128)(2,1)S(1)}, u32[]{:S(2)}, u32[]{:S(2)}) collective-permute-start(bf16[128,1536]{1,0:T(8,128)(2,1)S(1)} %collective-permute-done.1), channel_id=1, source_target_pairs={{2,1},{1,0},{6,5},{5,4},{10,9},{9,8},{14,13},{13,12},{18,17},{17,1... | collective-permute-start | bytes 1179656 | tf_op jit(solution)/shard_map/ppermute | solution.py:920
  42.5 22.3 %collective-permute-start.17 = (bf16[128,1536]{1,0:T(8,128)(2,1)S(1)}, bf16[128,1536]{1,0:T(8,128)(2,1)S(1)}, u32[]{:S(2)}, u32[]{:S(2)}) collective-permute-start(bf16[128,1536]{1,0:T(8,128)(2,1)S(1)} %collective-permute-done.1), channel_id=1, source_target_pairs={{2,0},{6,4},{10,8},{14,12},{18,16},{22,20},{26,24},{30,28}} | collective-permute-start | bytes 1179656 | tf_op jit(solution)/shard_map/ppermute | solution.py:920
  65.1 27.6 %copy-start.3 = (bf16[256,1024]{1,0:T(8,128)(2,1)S(1)}, bf16[256,1024]{1,0:T(8,128)(2,1)}, u32[]{:S(2)}) copy-start(bf16[256,1024]{1,0:T(8,128)(2,1)} %refs_1_.3) | copy-start | bytes 1572868
  66.4 248.3 %reduce-scatter.3.cloned.1.call-start = ((), (), s32[]{:S(2)}) async-start(), calls=%async_computation.4 | async-start | bytes 14155776 | tf_op jit(solution)/shard_map/reduce_scatter | solution.py:1106
  66.4 17.7 %collective-permute-start.4 = (bf16[256,1024]{1,0:T(8,128)(2,1)S(1)}, bf16[256,1024]{1,0:T(8,128)(2,1)S(1)}, u32[]{:S(2)}, u32[]{:S(2)}) collective-permute-start(bf16[256,1024]{1,0:T(8,128)(2,1)S(1)} %collective-permute-done.3.refs_7_), channel_id=1, source_target_pairs={{2,0},{6,4},{10,8},{14,12},{18,16},{22,20},{26,24},{30,28}} | collective-permute-start | bytes 1572872 | tf_op jit(solution)/shard_map/ppermute | solution.py:920
  67.7 17.2 %collective-permute-start.5 = (bf16[256,1024]{1,0:T(8,128)(2,1)S(1)}, bf16[256,1024]{1,0:T(8,128)(2,1)S(1)}, u32[]{:S(2)}, u32[]{:S(2)}) collective-permute-start(bf16[256,1024]{1,0:T(8,128)(2,1)S(1)} %collective-permute-done.2.refs_2_), channel_id=1, source_target_pairs={{1,2},{2,3},{5,6},{6,7},{9,10},{10,11},{13,14},{14,15},{17,18},{18... | collective-permute-start | bytes 1572872 | tf_op jit(solution)/shard_map/ppermute | solution.py:920
  68.5 23.4 %collective-permute-start.6 = (bf16[256,1024]{1,0:T(8,128)(2,1)S(1)}, bf16[256,1024]{1,0:T(8,128)(2,1)S(1)}, u32[]{:S(2)}, u32[]{:S(2)}) collective-permute-start(bf16[256,1024]{1,0:T(8,128)(2,1)S(1)} %collective-permute-done.3.refs_7_), channel_id=1, source_target_pairs={{2,1},{1,0},{6,5},{5,4},{10,9},{9,8},{14,13},{13,12},{18,17},{17,1... | collective-permute-start | bytes 1572872 | tf_op jit(solution)/shard_map/ppermute | solution.py:920
  69.8 22.9 %collective-permute-start.7 = (bf16[256,1024]{1,0:T(8,128)(2,1)S(1)}, bf16[256,1024]{1,0:T(8,128)(2,1)}, u32[]{:S(2)}, u32[]{:S(2)}) collective-permute-start(bf16[256,1024]{1,0:T(8,128)(2,1)S(1)} %collective-permute-done.2.refs_2_), channel_id=1, source_target_pairs={{1,3},{5,7},{9,11},{13,15},{17,19},{21,23},{25,27},{29,31}} | collective-permute-start | bytes 1572872 | tf_op jit(solution)/shard_map/ppermute | solution.py:920
  113.3 9.3 %collective-permute-start.10 = (f32[1,1024]{1,0:T(1,128)S(1)}, f32[1,1024]{1,0:T(1,128)S(1)}, u32[]{:S(2)}, u32[]{:S(2)}) collective-permute-start(f32[1,1024]{1,0:T(1,128)S(1)} %slice.117), channel_id=1, source_target_pairs={{0,3},{1,0},{2,1},{3,2},{4,7},{5,4},{6,5},{7,6},{8,11},{9,8},{10,9... | collective-permute-start | bytes 12296 | tf_op jit(solution)/shard_map/ppermute | solution.py:916
  117.4 5.6 %collective-permute-start.8 = (f32[1,1024]{1,0:T(1,128)S(1)}, f32[1,1024]{1,0:T(1,128)S(1)}, u32[]{:S(2)}, u32[]{:S(2)}) collective-permute-start(f32[1,1024]{1,0:T(1,128)S(1)} %slice.117), channel_id=1, source_target_pairs={{0,1},{1,2},{2,3},{3,0},{4,5},{5,6},{6,7},{7,4},{8,9},{9,10},{10,1... | collective-permute-start | bytes 12296 | tf_op jit(solution)/shard_map/ppermute | solution.py:916
  117.6 5.4 %collective-permute-start.9 = (f32[1,1024]{1,0:T(1,128)S(1)}, f32[1,1024]{1,0:T(1,128)S(1)}, u32[]{:S(2)}, u32[]{:S(2)}) collective-permute-start(f32[1,1024]{1,0:T(1,128)S(1)} %slice.117), channel_id=1, source_target_pairs={{0,2},{1,3},{2,0},{3,1},{4,6},{5,7},{6,4},{7,5},{8,10},{9,11},{10,... | collective-permute-start | bytes 12296 | tf_op jit(solution)/shard_map/ppermute | solution.py:916
  124.5 18.0 %collective-permute-start.11 = (bf16[256,1024]{1,0:T(8,128)(2,1)}, bf16[256,1024]{1,0:T(8,128)(2,1)}, u32[]{:S(2)}, u32[]{:S(2)}) collective-permute-start(bf16[256,1024]{1,0:T(8,128)(2,1)} %convolution_convert_fusion), channel_id=1, source_target_pairs={{0,1},{1,2},{4,5},{5,6},{8,9},{9,10},{12,13},{13,14},{16,17},{17,1... | collective-permute-start | bytes 1572872 | tf_op jit(solution)/shard_map/ppermute | solution.py:920
  132.3 15.9 %collective-permute-start.12 = (bf16[256,1024]{1,0:T(8,128)(2,1)}, bf16[256,1024]{1,0:T(8,128)(2,1)}, u32[]{:S(2)}, u32[]{:S(2)}) collective-permute-start(bf16[256,1024]{1,0:T(8,128)(2,1)} %get-tuple-element.213), channel_id=1, source_target_pairs={{0,2},{4,6},{8,10},{12,14},{16,18},{20,22},{24,26},{28,30}} | collective-permute-start | bytes 1572872 | tf_op jit(solution)/shard_map/ppermute | solution.py:920
  134.4 19.5 %copy-start.36 = (f32[256,1024]{1,0:T(8,128)S(1)}, f32[256,1024]{1,0:T(8,128)}, u32[]{:S(2)}) copy-start(f32[256,1024]{1,0:T(8,128)} %get-tuple-element.214) | copy-start | bytes 3145732
  134.4 19.4 %collective-permute-start.14 = (bf16[256,1024]{1,0:T(8,128)(2,1)}, bf16[256,1024]{1,0:T(8,128)(2,1)S(1)}, u32[]{:S(2)}, u32[]{:S(2)}) collective-permute-start(bf16[256,1024]{1,0:T(8,128)(2,1)} %convolution_convert_fusion), channel_id=1, source_target_pairs={{3,2},{2,1},{7,6},{6,5},{11,10},{10,9},{15,14},{14,13},{19,18},{18... | collective-permute-start | bytes 1572872 | tf_op jit(solution)/shard_map/ppermute | solution.py:920
  151.0 2.8 collective-permute-start.15
  151.7 8.3 %collective-permute-start.13 = (bf16[256,1024]{1,0:T(8,128)(2,1)}, bf16[256,1024]{1,0:T(8,128)(2,1)}, u32[]{:S(2)}, u32[]{:S(2)}) collective-permute-start(bf16[256,1024]{1,0:T(8,128)(2,1)} %get-tuple-element.196), channel_id=1, source_target_pairs={{0,1},{1,2},{2,3},{4,5},{5,6},{6,7},{8,9},{9,10},{10,11},{12,13},{... | collective-permute-start | bytes 1572872 | tf_op jit(solution)/shard_map/ppermute | solution.py:920
  154.9 18.2 %collective-permute-start.16 = (bf16[256,1024]{1,0:T(8,128)(2,1)}, bf16[256,1024]{1,0:T(8,128)(2,1)}, u32[]{:S(2)}, u32[]{:S(2)}) collective-permute-start(bf16[256,1024]{1,0:T(8,128)(2,1)} %add_convert_fusion.3), channel_id=1, source_target_pairs={{3,2},{2,1},{1,0},{7,6},{6,5},{5,4},{11,10},{10,9},{9,8},{15,14},{... | collective-permute-start | bytes 1572872 | tf_op jit(solution)/shard_map/ppermute | solution.py:920
  193.1 161.8 %reduce-scatter.5.cloned.1.call-start = ((), (), s32[]{:S(2)}) async-start(), calls=%async_computation.5 | async-start | bytes 2457600 | tf_op jit(solution)/shard_map/reduce_scatter | solution.py:983
  193.2 19.1 %collective-permute-start.22 = (bf16[256,1024]{1,0:T(8,128)(2,1)}, bf16[256,1024]{1,0:T(8,128)(2,1)}, u32[]{:S(2)}, u32[]{:S(2)}) collective-permute-start(bf16[256,1024]{1,0:T(8,128)(2,1)} %get-tuple-element.82.refs_1_), channel_id=1, source_target_pairs={{1,0},{2,1},{3,2},{5,4},{6,5},{7,6},{9,8},{10,9},{11,10},{13,12},{... | collective-permute-start | bytes 1572872 | tf_op jit(solution)/shard_map/ppermute | solution.py:920
  194.5 19.1 %collective-permute-start.21 = (bf16[256,1024]{1,0:T(8,128)(2,1)}, bf16[256,1024]{1,0:T(8,128)(2,1)}, u32[]{:S(2)}, u32[]{:S(2)}) collective-permute-start(bf16[256,1024]{1,0:T(8,128)(2,1)} %get-tuple-element.82.refs_1_), channel_id=1, source_target_pairs={{0,1},{1,2},{2,3},{4,5},{5,6},{6,7},{8,9},{9,10},{10,11},{12,13},{... | collective-permute-start | bytes 1572872 | tf_op jit(solution)/shard_map/ppermute | solution.py:920
  212.3 12.3 %collective-permute-start.23 = (bf16[256,1024]{1,0:T(8,128)(2,1)}, bf16[256,1024]{1,0:T(8,128)(2,1)}, u32[]{:S(2)}, u32[]{:S(2)}) collective-permute-start(bf16[256,1024]{1,0:T(8,128)(2,1)} %collective-permute-done.22.refs_7_), channel_id=1, source_target_pairs={{2,0},{6,4},{10,8},{14,12},{18,16},{22,20},{26,24},{30,28}} | collective-permute-start | bytes 1572872 | tf_op jit(solution)/shard_map/ppermute | solution.py:920
  213.6 11.0 %collective-permute-start.24 = (bf16[256,1024]{1,0:T(8,128)(2,1)}, bf16[256,1024]{1,0:T(8,128)(2,1)}, u32[]{:S(2)}, u32[]{:S(2)}) collective-permute-start(bf16[256,1024]{1,0:T(8,128)(2,1)} %collective-permute-done.21.refs_2_), channel_id=1, source_target_pairs={{1,2},{2,3},{5,6},{6,7},{9,10},{10,11},{13,14},{14,15},{17,18},{18... | collective-permute-start | bytes 1572872 | tf_op jit(solution)/shard_map/ppermute | solution.py:920
  215.1 15.6 %collective-permute-start.25 = (bf16[256,1024]{1,0:T(8,128)(2,1)}, bf16[256,1024]{1,0:T(8,128)(2,1)}, u32[]{:S(2)}, u32[]{:S(2)}) collective-permute-start(bf16[256,1024]{1,0:T(8,128)(2,1)} %collective-permute-done.22.refs_7_), channel_id=1, source_target_pairs={{2,1},{1,0},{6,5},{5,4},{10,9},{9,8},{14,13},{13,12},{18,17},{17,1... | collective-permute-start | bytes 1572872 | tf_op jit(solution)/shard_map/ppermute | solution.py:920
  216.4 14.3 %collective-permute-start.26 = (bf16[256,1024]{1,0:T(8,128)(2,1)}, bf16[256,1024]{1,0:T(8,128)(2,1)}, u32[]{:S(2)}, u32[]{:S(2)}) collective-permute-start(bf16[256,1024]{1,0:T(8,128)(2,1)} %collective-permute-done.21.refs_2_), channel_id=1, source_target_pairs={{1,3},{5,7},{9,11},{13,15},{17,19},{21,23},{25,27},{29,31}} | collective-permute-start | bytes 1572872 | tf_op jit(solution)/shard_map/ppermute | solution.py:920
  219.7 22.8 %copy-start.9 = (f32[1024,128]{1,0:T(8,128)S(1)}, f32[1024,128]{1,0:T(8,128)}, u32[]{:S(2)}) copy-start(f32[1024,128]{1,0:T(8,128)} %constant.68.clone.cos_ref) | copy-start | bytes 1572868
  219.7 22.8 %copy-start.11 = (f32[1024,128]{1,0:T(8,128)S(1)}, f32[1024,128]{1,0:T(8,128)}, u32[]{:S(2)}) copy-start(f32[1024,128]{1,0:T(8,128)} %constant.69.clone.sin_ref) | copy-start | bytes 1572868
  219.7 22.8 %copy-start.23 = (f32[1024,128]{1,0:T(8,128)S(1)}, f32[1024,128]{1,0:T(8,128)}, u32[]{:S(2)}) copy-start(f32[1024,128]{1,0:T(8,128)} %copy-done.22) | copy-start | bytes 1572868
  219.7 22.8 %copy-start.26 = (bf16[1024,128]{1,0:T(8,128)(2,1)S(1)}, bf16[1024,128]{1,0:T(8,128)(2,1)}, u32[]{:S(2)}) copy-start(bf16[1024,128]{1,0:T(8,128)(2,1)} %copy-done.25) | copy-start | bytes 786436
  219.7 22.8 %copy-start.28 = (bf16[1024,128]{1,0:T(8,128)(2,1)S(1)}, bf16[1024,128]{1,0:T(8,128)(2,1)}, u32[]{:S(2)}) copy-start(bf16[1024,128]{1,0:T(8,128)(2,1)} %copy-done.27) | copy-start | bytes 786436
  230.8 18.5 %slice-start = ((s8[5767168]{0:T(1024)(128)(4,1)}), s8[1572864]{0:T(1024)(128)(4,1)S(1)}, s32[]{:S(2)}) async-start(s8[5767168]{0:T(1024)(128)(4,1)} %bitcast.26), calls=%async_computation.6 | async-start | bytes 3145728
  236.3 12.9 %collective-permute-start.27 = (f32[1,1024]{1,0:T(1,128)S(1)}, f32[1,1024]{1,0:T(1,128)S(1)}, u32[]{:S(2)}, u32[]{:S(2)}) collective-permute-start(f32[1,1024]{1,0:T(1,128)S(1)} %slice.120), channel_id=1, source_target_pairs={{0,1},{1,2},{2,3},{3,0},{4,5},{5,6},{6,7},{7,4},{8,9},{9,10},{10,1... | collective-permute-start | bytes 12296 | tf_op jit(solution)/shard_map/ppermute | solution.py:916
  238.8 10.4 %collective-permute-start.28 = (f32[1,1024]{1,0:T(1,128)S(1)}, f32[1,1024]{1,0:T(1,128)S(1)}, u32[]{:S(2)}, u32[]{:S(2)}) collective-permute-start(f32[1,1024]{1,0:T(1,128)S(1)} %slice.120), channel_id=1, source_target_pairs={{0,2},{1,3},{2,0},{3,1},{4,6},{5,7},{6,4},{7,5},{8,10},{9,11},{10,... | collective-permute-start | bytes 12296 | tf_op jit(solution)/shard_map/ppermute | solution.py:916
  242.5 6.7 %collective-permute-start.29 = (f32[1,1024]{1,0:T(1,128)S(1)}, f32[1,1024]{1,0:T(1,128)S(1)}, u32[]{:S(2)}, u32[]{:S(2)}) collective-permute-start(f32[1,1024]{1,0:T(1,128)S(1)} %slice.120), channel_id=1, source_target_pairs={{0,3},{1,0},{2,1},{3,2},{4,7},{5,4},{6,5},{7,6},{8,11},{9,8},{10,9... | collective-permute-start | bytes 12296 | tf_op jit(solution)/shard_map/ppermute | solution.py:916
  274.1 7.8 %collective-permute-start.34 = (bf16[512,1920]{1,0:T(8,128)(2,1)S(1)}, bf16[512,1920]{1,0:T(8,128)(2,1)S(1)}, u32[]{:S(2)}, u32[]{:S(2)}) collective-permute-start(bf16[512,1920]{1,0:T(8,128)(2,1)S(1)} %get-tuple-element.92), channel_id=1, source_target_pairs={{0,4},{4,0},{8,12},{12,8},{16,20},{20,16},{24,28},{28,24},{1,5},{5... | collective-permute-start | bytes 5898248 | tf_op jit(solution)/shard_map/ppermute | solution.py:976
  284.7 16.8 %collective-permute-start.30 = (bf16[272,1024]{1,0:T(8,128)(2,1)S(1)}, bf16[272,1024]{1,0:T(8,128)(2,1)S(1)}, u32[]{:S(2)}, u32[]{:S(2)}) collective-permute-start(bf16[272,1024]{1,0:T(8,128)(2,1)S(1)} %copy-done.21), channel_id=1, source_target_pairs={{0,1},{1,2},{4,5},{5,6},{8,9},{9,10},{12,13},{13,14},{16,17},{17,1... | collective-permute-start | bytes 1671176 | tf_op jit(solution)/shard_map/ppermute | solution.py:920
  288.7 24.4 %collective-permute-start.31 = (bf16[272,1024]{1,0:T(8,128)(2,1)S(1)}, bf16[272,1024]{1,0:T(8,128)(2,1)S(1)}, u32[]{:S(2)}, u32[]{:S(2)}) collective-permute-start(bf16[272,1024]{1,0:T(8,128)(2,1)S(1)} %copy-done.7), channel_id=1, source_target_pairs={{0,2},{4,6},{8,10},{12,14},{16,18},{20,22},{24,26},{28,30}} | collective-permute-start | bytes 1671176 | tf_op jit(solution)/shard_map/ppermute | solution.py:920
  290.0 23.1 %collective-permute-start.32 = (bf16[272,1024]{1,0:T(8,128)(2,1)S(1)}, bf16[272,1024]{1,0:T(8,128)(2,1)S(1)}, u32[]{:S(2)}, u32[]{:S(2)}) collective-permute-start(bf16[272,1024]{1,0:T(8,128)(2,1)S(1)} %copy-done.21), channel_id=1, source_target_pairs={{3,2},{2,1},{7,6},{6,5},{11,10},{10,9},{15,14},{14,13},{19,18},{18... | collective-permute-start | bytes 1671176 | tf_op jit(solution)/shard_map/ppermute | solution.py:920
  290.7 24.0 %collective-permute-start.33 = (bf16[272,1024]{1,0:T(8,128)(2,1)S(1)}, bf16[272,1024]{1,0:T(8,128)(2,1)}, u32[]{:S(2)}, u32[]{:S(2)}) collective-permute-start(bf16[272,1024]{1,0:T(8,128)(2,1)S(1)} %get-tuple-element.97), channel_id=1, source_target_pairs={{3,1},{7,5},{11,9},{15,13},{19,17},{23,21},{27,25},{31,29}} | collective-permute-start | bytes 1671176 | tf_op jit(solution)/shard_map/ppermute | solution.py:920
  317.2 37.0 %collective-permute-start.36 = (bf16[272,1024]{1,0:T(8,128)(2,1)}, bf16[272,1024]{1,0:T(8,128)(2,1)S(1)}, u32[]{:S(2)}, u32[]{:S(2)}) collective-permute-start(bf16[272,1024]{1,0:T(8,128)(2,1)} %add_convert_fusion.1), channel_id=1, source_target_pairs={{3,2},{2,1},{1,0},{7,6},{6,5},{5,4},{11,10},{10,9},{9,8},{15,14},{... | collective-permute-start | bytes 1671176 | tf_op jit(solution)/shard_map/ppermute | solution.py:920
  319.7 18.1 %collective-permute-start.37 = (bf16[128,1536]{1,0:T(8,128)(2,1)}, bf16[128,1536]{1,0:T(8,128)(2,1)}, u32[]{:S(2)}, u32[]{:S(2)}) collective-permute-start(bf16[128,1536]{1,0:T(8,128)(2,1)} %get-tuple-element.195), channel_id=1, source_target_pairs={{0,1},{1,2},{4,5},{5,6},{8,9},{9,10},{12,13},{13,14},{16,17},{17,1... | collective-permute-start | bytes 1179656 | tf_op jit(solution)/shard_map/ppermute | solution.py:920
  328.4 39.7 %copy-start.5 = (f32[272,1024]{1,0:T(8,128)S(1)}, f32[272,1024]{1,0:T(8,128)}, u32[]{:S(2)}) copy-start(f32[272,1024]{1,0:T(8,128)} %copy-done.4) | copy-start | bytes 3342340
  328.4 25.8 %collective-permute-start.35 = (bf16[272,1024]{1,0:T(8,128)(2,1)}, bf16[272,1024]{1,0:T(8,128)(2,1)S(1)}, u32[]{:S(2)}, u32[]{:S(2)}) collective-permute-start(bf16[272,1024]{1,0:T(8,128)(2,1)} %add_convert_fusion.2), channel_id=1, source_target_pairs={{0,1},{1,2},{2,3},{4,5},{5,6},{6,7},{8,9},{9,10},{10,11},{12,13},{... | collective-permute-start | bytes 1671176 | tf_op jit(solution)/shard_map/ppermute | solution.py:920
  331.7 22.5 %collective-permute-start.39 = (bf16[128,1536]{1,0:T(8,128)(2,1)}, bf16[128,1536]{1,0:T(8,128)(2,1)S(1)}, u32[]{:S(2)}, u32[]{:S(2)}) collective-permute-start(bf16[128,1536]{1,0:T(8,128)(2,1)} %get-tuple-element.195), channel_id=1, source_target_pairs={{3,2},{2,1},{7,6},{6,5},{11,10},{10,9},{15,14},{14,13},{19,18},{18... | collective-permute-start | bytes 1179656 | tf_op jit(solution)/shard_map/ppermute | solution.py:920
  332.4 21.8 %collective-permute-start.38 = (bf16[128,1536]{1,0:T(8,128)(2,1)}, bf16[128,1536]{1,0:T(8,128)(2,1)}, u32[]{:S(2)}, u32[]{:S(2)}) collective-permute-start(bf16[128,1536]{1,0:T(8,128)(2,1)} %get-tuple-element.194), channel_id=1, source_target_pairs={{0,2},{4,6},{8,10},{12,14},{16,18},{20,22},{24,26},{28,30}} | collective-permute-start | bytes 1179656 | tf_op jit(solution)/shard_map/ppermute | solution.py:920
  337.8 16.4 %collective-permute-start.40 = (bf16[128,1536]{1,0:T(8,128)(2,1)}, bf16[128,1536]{1,0:T(8,128)(2,1)}, u32[]{:S(2)}, u32[]{:S(2)}) collective-permute-start(bf16[128,1536]{1,0:T(8,128)(2,1)} %get-tuple-element.193), channel_id=1, source_target_pairs={{3,1},{7,5},{11,9},{15,13},{19,17},{23,21},{27,25},{31,29}} | collective-permute-start | bytes 1179656 | tf_op jit(solution)/shard_map/ppermute | solution.py:920
  357.9 22.8 %collective-permute-start.44 = (bf16[128,512]{1,0:T(8,128)(2,1)}, bf16[128,512]{1,0:T(8,128)(2,1)}, u32[]{:S(2)}, u32[]{:S(2)}) collective-permute-start(bf16[128,512]{1,0:T(8,128)(2,1)} %pad_maximum_fusion.2), channel_id=1, source_target_pairs={{0,1},{1,2},{2,3},{3,0},{4,5},{5,6},{6,7},{7,4},{8,9},{9,10},{10,1... | collective-permute-start | bytes 393224 | tf_op jit(solution)/shard_map/ppermute | solution.py:916
  357.9 24.6 %collective-permute-start.45 = (bf16[128,512]{1,0:T(8,128)(2,1)}, bf16[128,512]{1,0:T(8,128)(2,1)}, u32[]{:S(2)}, u32[]{:S(2)}) collective-permute-start(bf16[128,512]{1,0:T(8,128)(2,1)} %pad_maximum_fusion.2), channel_id=1, source_target_pairs={{0,2},{1,3},{2,0},{3,1},{4,6},{5,7},{6,4},{7,5},{8,10},{9,11},{10,... | collective-permute-start | bytes 393224 | tf_op jit(solution)/shard_map/ppermute | solution.py:916
  361.8 20.7 %collective-permute-start.46 = (bf16[128,512]{1,0:T(8,128)(2,1)}, bf16[128,512]{1,0:T(8,128)(2,1)}, u32[]{:S(2)}, u32[]{:S(2)}) collective-permute-start(bf16[128,512]{1,0:T(8,128)(2,1)} %pad_maximum_fusion.2), channel_id=1, source_target_pairs={{0,3},{1,0},{2,1},{3,2},{4,7},{5,4},{6,5},{7,6},{8,11},{9,8},{10,9... | collective-permute-start | bytes 393224 | tf_op jit(solution)/shard_map/ppermute | solution.py:916
  371.0 25.2 %collective-permute-start.47 = (bf16[128,1536]{1,0:T(8,128)(2,1)}, bf16[128,1536]{1,0:T(8,128)(2,1)}, u32[]{:S(2)}, u32[]{:S(2)}) collective-permute-start(bf16[128,1536]{1,0:T(8,128)(2,1)} %get-tuple-element.191), channel_id=1, source_target_pairs={{0,1},{1,2},{2,3},{4,5},{5,6},{6,7},{8,9},{9,10},{10,11},{12,13},{... | collective-permute-start | bytes 1179656 | tf_op jit(solution)/shard_map/ppermute | solution.py:920
  376.3 3.2 collective-permute-start.41
  379.4 16.7 %collective-permute-start.48 = (bf16[128,1536]{1,0:T(8,128)(2,1)}, bf16[128,1536]{1,0:T(8,128)(2,1)S(1)}, u32[]{:S(2)}, u32[]{:S(2)}) collective-permute-start(bf16[128,1536]{1,0:T(8,128)(2,1)} %get-tuple-element.192), channel_id=1, source_target_pairs={{3,2},{2,1},{1,0},{7,6},{6,5},{5,4},{11,10},{10,9},{9,8},{15,14},{... | collective-permute-start | bytes 1179656 | tf_op jit(solution)/shard_map/ppermute | solution.py:920
  380.8 6.0 %collective-permute-start.42 = (f32[32,1024]{1,0:T(8,128)S(1)}, f32[32,1024]{1,0:T(8,128)S(1)}, u32[]{:S(2)}, u32[]{:S(2)}) collective-permute-start(f32[32,1024]{1,0:T(8,128)S(1)} %add.200), channel_id=1, source_target_pairs={{0,8},{4,12},{8,0},{12,4},{16,24},{20,28},{24,16},{28,20},{1,9},{5... | collective-permute-start | bytes 393224 | tf_op jit(solution)/shard_map/ppermute | solution.py:1003
  386.8 5.2 %collective-permute-start.43 = (f32[32,1024]{1,0:T(8,128)S(1)}, f32[32,1024]{1,0:T(8,128)S(1)}, u32[]{:S(2)}, u32[]{:S(2)}) collective-permute-start(f32[32,1024]{1,0:T(8,128)S(1)} %add.201), channel_id=1, source_target_pairs={{0,16},{4,20},{8,24},{12,28},{16,0},{20,4},{24,8},{28,12},{1,17},{... | collective-permute-start | bytes 393224 | tf_op jit(solution)/shard_map/ppermute | solution.py:1003
  (57 other events, 295.3 us)
Sparse Core Ops, SparseCore 0:
  11.0 38.3 all-gather.2
  66.5 70.3 all-gather.4
  193.3 92.1 reduce-scatter.2
  288.4 34.1 reduce-scatter.4
where the time goes:
time: 413 us; the launch traced here: 406 us
  waiting for transfers between devices  145 us (35%)
  starting transfers between devices  99.2 us (24%)
  Pallas kernels  78.3 us (19%)
  local copies, waits for them, and re-layouts  33.7 us (8%)
  other arithmetic  24 us (6%)
  between operations  15.5 us (4%)
  matrix products  11 us (3%)
    ppermute x36, waiting for transfers between devices, sent(): return lax.ppermute(values, 'tensor', pairs)  138 us
    ppermute x36, starting transfers between devices, sent(): return lax.ppermute(values, 'tensor', pairs)  77.1 us
    unnamed x141, local copies, waits for them, and re-layouts  20.5 us
    pallas_call x1, Pallas kernels, scan_backward(): pl.pallas_call(body, grid=(blocks,), in_specs=[pl.BlockSpec((BLOCK, width...  18.7 us
    ppermute x9, starting transfers between devices, shifted(): lax.ppermute(values, axis, [(i, (i + shift) % size) for i in range(size)])  18.2 us
    pallas_call x1, Pallas kernels, ffn_both(): pl.pallas_call(ffn_kernel, grid=(parts,), in_specs=[rowspec, rowspec, pl....  17.5 us
  transfers between devices with their start and end apart: 53, of which 18 were waited for; matrix products, arithmetic and copies ran while one was open for 11% of the time, Pallas kernels for 14%

commit v1 on v0

--- a/solution.py
+++ b/solution.py
@@ -668,7 +668,7 @@
         + [whole((1, model))],
         out_specs=whole((parts * rows, model)),
         out_shape=jax.ShapeDtypeStruct((parts * rows, model), BF16),
-        compiler_params=pltpu.CompilerParams(vmem_limit_bytes=24 * MIB),
+        compiler_params=pltpu.CompilerParams(vmem_limit_bytes=60 * MIB),
         cost_estimate=pl.CostEstimate(flops=10**7, bytes_accessed=5 * 10**6, transcendentals=0),
         name="norm_rows",
     )(rank, *pieces, gain)
@@ -776,14 +776,10 @@
     )(core, *args)
 
 
-EXTRA = 16
-
-
-def back_proj_kernel(zat, rank_ref, gq_ref, gkv_ref, grest_ref, w_ref, rows_ref, gain_ref, two_ref, conv_ref, *refs):
+def back_proj_kernel(zat, rank_ref, gq_ref, gkv_ref, grest_ref, w_ref, rows_ref, gain_ref, two_ref, *refs):
     turn = pl.program_id(0)
     outs, share_ref = refs[:-1], refs[-1]
     qwidth = gq_ref.shape[1]
-    rows = gq_ref.shape[0]
     term = mm_nt(gq_ref[...], w_ref[:, :qwidth]) + mm_nt(gkv_ref[...], w_ref[:, qwidth:zat])
     term = term + mm_nt(grest_ref[...], w_ref[:, zat:])
     share = jnp.sum(term * rows_ref[...].astype(F32), axis=0, keepdims=True) / gain_ref[...]
@@ -792,22 +788,16 @@
     def _():
         share_ref[...] = jnp.zeros_like(share_ref)
         share_ref[1:2, :] = two_ref[0:1, :]
-        share_ref[8:16, 0 : 2 * NS] = conv_ref[:, conv_ref.shape[1] - 2 * NS :]
 
     share_ref[0:1, :] += share
     for index in range(len(outs)):
 
         @pl.when(turn == index)
         def _(index=index):
-            outs[index][0:rows, :] = term.astype(outs[index].dtype)
-
-    @pl.when(turn == pl.num_programs(0) - 1)
-    def _():
-        for out in outs:
-            out[rows : rows + EXTRA, :] = share_ref[...].astype(out.dtype)
-
-
-def back_proj(rank, parts, zat, width, grad_q, grad_kv, grad_rest, mixer_w, rows_one, gain, gain_two, conv_acc):
+            outs[index][...] = term.astype(outs[index].dtype)
+
+
+def back_proj(rank, parts, zat, width, grad_q, grad_kv, grad_rest, mixer_w, rows_one, gain, gain_two):
     length, model = rows_one.shape
     rows = length // parts
     at = lambda s, rank_ref: (lax.rem(rank_ref[0] + s, parts), 0)
@@ -823,20 +813,19 @@
             pl.BlockSpec((rows, model), at),
             pl.BlockSpec((1, model), fixed),
             pl.BlockSpec(gain_two.shape, fixed),
-            pl.BlockSpec(conv_acc.shape, fixed),
         ],
-        out_specs=[pl.BlockSpec((rows + EXTRA, model), fixed)] * parts,
-        scratch_shapes=[pltpu.VMEM((EXTRA, model), F32)],
+        out_specs=[pl.BlockSpec((rows, model), fixed)] * parts + [pl.BlockSpec((8, model), fixed)],
     )
     return pl.pallas_call(
         lambda *refs: back_proj_kernel(zat, *refs),
         grid_spec=spec,
-        out_shape=[jax.ShapeDtypeStruct((rows + EXTRA, model), F32)]
-        + [jax.ShapeDtypeStruct((rows + EXTRA, model), BF16)] * (parts - 1),
+        out_shape=[jax.ShapeDtypeStruct((rows, model), F32)]
+        + [jax.ShapeDtypeStruct((rows, model), BF16)] * (parts - 1)
+        + [jax.ShapeDtypeStruct((8, model), F32)],
         compiler_params=pltpu.CompilerParams(vmem_limit_bytes=32 * MIB),
         cost_estimate=pl.CostEstimate(flops=3 * 10**9, bytes_accessed=10**7, transcendentals=0),
         name="back_proj",
-    )(rank, grad_q, grad_kv, grad_rest, mixer_w, rows_one, gain, gain_two, conv_acc)
+    )(rank, grad_q, grad_kv, grad_rest, mixer_w, rows_one, gain, gain_two)
 
 
 def ffn_kernel(middle_ref, cot_ref, gain_ref, w_ref, out_ref, gmid_ref, glow_ref, ggain_ref, gw_ref, low_ref, sum_ref, gsum_ref):
@@ -944,20 +933,23 @@
     return pieces
 
 
-def sum_first(terms, parts):
+def sum_first(terms, rank, parts):
     if parts != 4:
         return [shifted(terms[shift].astype(BF16), "tensor", parts, shift) for shift in range(1, parts)]
-    low = lambda value: value.astype(BF16)
-    up = [sent(low(terms[2]), [(0, 1), (1, 2)]), sent(low(terms[3]), [(0, 2)])]
-    return up + [sent(low(terms[2]), [(3, 2), (2, 1)]), sent(low(terms[1]), [(3, 1)])]
-
-
-def sum_second(terms, firsts, parts):
+    far = jnp.where(rank == 0, terms[3], terms[1])
+    return [
+        sent(terms[2].astype(BF16), [(0, 1), (3, 2)]),
+        sent(terms[2].astype(BF16), [(1, 2), (2, 1)]),
+        sent(far.astype(BF16), [(0, 2), (3, 1)]),
+    ]
+
+
+def sum_second(terms, firsts, rank, parts):
     if parts != 4:
         return firsts
-    firsts = [first.astype(F32) for first in firsts]
-    up = terms[1].astype(F32) + firsts[0] + firsts[1]
-    down = terms[3].astype(F32) + firsts[2] + firsts[3]
+    near, cross = firsts[0].astype(F32), firsts[1].astype(F32) + firsts[2].astype(F32)
+    up = terms[1].astype(F32) + jnp.where(rank == 1, near, cross)
+    down = terms[3].astype(F32) + jnp.where(rank == 1, cross, near)
     return [
         sent(up.astype(BF16), [(0, 1), (1, 2), (2, 3)]),
         sent(down.astype(BF16), [(3, 2), (2, 1), (1, 0)]),
@@ -995,10 +987,7 @@
     return total
 
 
-def butterfly(values, axis, size):
-    if size & (size - 1):
-        return lax.psum(values, axis)
-    step = 1
+def butterfly(values, axis, size, step):
     while step < size:
         values = values + lax.ppermute(values, axis, [(i, i ^ step) for i in range(size)])
         step *= 2
@@ -1069,14 +1058,8 @@
     gain_two = mixer_w[:, dat + HD + 1].astype(F32)[None, :]
     ffn_own = pack_ffn(w_gate, w_up, w_down)
     ffn_first, x_first = lax.optimization_barrier((first_phase(ffn_own, parts), first_phase(x_in, parts)))
-    ffn_pieces = second_phase(ffn_own, ffn_first, parts)
     x_pieces = second_phase(x_in, x_first, parts)
-    ffn_own = jnp.concatenate(
-        ffn_pieces[:1]
-        + [jnp.where(rank >= k, ffn_pieces[2 * k - 1], ffn_pieces[2 * k]) for k in range(1, parts)],
-        axis=1,
-    )
-    ffn_w = lax.all_gather(ffn_own, "dp", axis=0, tiled=True)
+    ffn_pieces = second_phase(ffn_own, after(ffn_first, x_pieces), parts)
 
     seg = segments[0]
     start = jnp.sum((seg[None, :] < seg[:, None]).astype(jnp.int32), axis=1)
@@ -1094,12 +1077,19 @@
     rows_one = norm_rows(rank_arg, parts, x_pieces, gain_one)
     proj = mm(rows_one, proj_w)
     y, gated, states, squares = scan_forward(cols, proj, start_col, start_row, params)
+    ffn_pieces = after(ffn_pieces, squares)
+    ffn_own = jnp.concatenate(
+        ffn_pieces[:1]
+        + [jnp.where(rank >= k, ffn_pieces[2 * k - 1], ffn_pieces[2 * k]) for k in range(1, parts)],
+        axis=1,
+    )
+    ffn_w = lax.all_gather(ffn_own, "dp", axis=0, tiled=True)
     attended, lse, low_q, low_kv = attn_forward(proj, cosine, sine, start_col)
     scale_ssm = lax.rsqrt(group_total(squares[:1], parts) / width_ssm + EPSILON)
     mixed = (gated * scale_ssm[0][:, None] * ssm_gain[None, :]).astype(BF16)
     att_mixed = jnp.concatenate([attended, mixed], axis=1)
     terms = [mm_nt(rows_of(att_mixed, rank, shift, parts), out_w) for shift in range(parts)]
-    middle = residual + sum_last(terms, sum_second(terms, sum_first(terms, parts), parts))
+    middle = residual + sum_last(terms, sum_second(terms, sum_first(terms, rank, parts), rank, parts))
     block_out, grad_middle, grad_low, grad_gain_two, grad_ffn_w = ffn_both(middle, cotangent, gain_two, ffn_w, parts)
 
     branch_pieces = second_phase(grad_low, first_phase(grad_low, parts), parts)
@@ -1119,54 +1109,66 @@
     )
     core = lax.rem(lax.axis_index("dp"), 2).astype(jnp.int32)[None]
     theirs, ours = mixer_wgrad(core, own, rows_one, grad_q, grad_kv, grad_rest, grad_out_w)
-    terms = back_proj(
-        rank_arg, parts, zat, width, grad_q, grad_kv, after(grad_rest, theirs), mixer_w, rows_one, gain_one, grad_gain_two, conv_acc
+    *terms, norm_shares = back_proj(
+        rank_arg, parts, zat, width, grad_q, grad_kv, after(grad_rest, theirs), mixer_w, rows_one, gain_one, grad_gain_two
     )
-    chip_share = chip_total(theirs, ours, terms)
-    firsts = after(sum_first(terms, parts), chip_share, grad_ffn_own)
-    seconds = sum_second(terms, firsts, parts)
-    seconds, ffn_firsts = lax.optimization_barrier((seconds, sum_first(ffn_terms, parts)))
-    grad_ffn = sum_last(ffn_terms, sum_second(ffn_terms, ffn_firsts, parts))
-    summed = sum_last(terms, seconds)
-    grad_one, shared_small = summed[:-EXTRA], summed[-EXTRA:]
-    grad_input = grad_middle + norm_back(grad_one * gain_one, normed_one, scale_one)
-    grad_w = after(sum_over_chips(chip_share), seconds).astype(F32)
 
     model = x_in.shape[1]
     wide = lambda rows: jnp.pad(rows, ((0, 0), (0, model - rows.shape[1])))
     head_sums = jnp.sum(head_acc, axis=1)[None, :]
     small = jnp.concatenate(
         [
-            shared_small,
             wide(conv_acc),
+            norm_shares[:2],
             wide(grad_gain_ssm[:1]),
             wide(skip_acc[:1]),
             wide(head_sums),
-            jnp.zeros((5, model), F32),
+            jnp.zeros((3, model), F32),
         ],
         axis=0,
     )
-    small = butterfly(small, "dp", lax.axis_size("dp"))
-    at = EXTRA
-    grad_conv_x = small[at : at + KW, :channels]
-    grad_bias_x = small[at + KW, :channels]
-    grad_ssm_gain = small[at + 8, :channels]
-    grad_d_skip = jnp.sum(small[at + 9, :channels].reshape(heads, PD), axis=1)
-    grad_dt_bias = small[at + 10, :heads]
-    grad_a_log = small[at + 10, 8 : 8 + heads]
-    grad_conv_bc = small[8 : 8 + KW, : 2 * NS]
-    grad_bias_bc = small[8 + KW, : 2 * NS]
+    size = lax.axis_size("dp")
+    small = small + lax.ppermute(small, "dp", [(i, i ^ 1) for i in range(size)])
+
+    chip_share = chip_total(theirs, ours, small)
+    small = butterfly(after(small, chip_share), "dp", size, 2)
+    firsts = after(sum_first(terms, rank, parts), small, grad_ffn_own)
+    seconds = sum_second(terms, firsts, rank, parts)
+    grad_w = sum_over_chips(chip_share)
+    seconds, ffn_firsts, grad_w = lax.optimization_barrier((seconds, sum_first(ffn_terms, rank, parts), grad_w))
+    ffn_seconds = sum_second(ffn_terms, ffn_firsts, rank, parts)
+    grad_one = sum_last(terms, seconds)
+    grad_input = grad_middle + norm_back(grad_one * gain_one, normed_one, scale_one)
+
+    grad_conv_x = small[:KW, :channels]
+    grad_bias_x = small[KW, :channels]
+    grad_ssm_gain = small[10, :channels]
+    grad_d_skip = jnp.sum(small[11, :channels].reshape(heads, PD), axis=1)
+    grad_dt_bias = small[12, :heads]
+    grad_a_log = small[12, 8 : 8 + heads]
+
     place = lax.axis_index("dp") * own
-    norm_grads = lax.dynamic_slice(small, (0, place), (2, own))
-    grad_norm_one, grad_norm_two = norm_grads[0], norm_grads[1]
-
-    grad_keyval = jnp.zeros((own, 2 * KVH * HD), F32)
-    grad_keyval = lax.dynamic_update_slice(grad_keyval, grad_w[:, qwidth : qwidth + HD], (0, kv_head * HD))
-    grad_keyval = lax.dynamic_update_slice(
-        grad_keyval, grad_w[:, qwidth + HD : zat], (0, (KVH + kv_head) * HD)
+    norm_parts = lax.dynamic_slice(small, (8, place), (2, own))
+    conv_parts = small[: KW + 1, channels : channels + 2 * NS]
+    small_rows = jnp.concatenate(
+        [
+            jnp.pad(norm_parts, ((0, 0), (0, LANES - own))),
+            conv_parts[:, :NS],
+            conv_parts[:, NS:],
+            jnp.zeros((own - 2 * KW - 4, LANES), F32),
+        ],
+        axis=0,
     )
-    shared = jnp.concatenate([grad_keyval, grad_w[:, bat:dat]], axis=1)
-    shared = group_total(shared.astype(BF16), parts)
+    keyval = jnp.zeros((own, 2 * KVH * HD), BF16)
+    keyval = lax.dynamic_update_slice(keyval, grad_w[:, qwidth : qwidth + HD], (0, kv_head * HD))
+    keyval = lax.dynamic_update_slice(keyval, grad_w[:, qwidth + HD : zat], (0, (KVH + kv_head) * HD))
+    shared = group_total(jnp.concatenate([keyval, grad_w[:, bat:dat], small_rows.astype(BF16)], axis=1), parts)
+    grad_ffn = sum_last(ffn_terms, ffn_seconds)
+    grad_w = grad_w.astype(F32)
+    small_rows = shared[:, 2 * KVH * HD + 2 * NS :]
+    grad_norm_one, grad_norm_two = small_rows[0, :own], small_rows[1, :own]
+    conv_parts = jnp.concatenate([small_rows[2 : KW + 3], small_rows[KW + 3 : 2 * KW + 4]], axis=1)
+    grad_conv_bc, grad_bias_bc = conv_parts[:KW], conv_parts[KW]
 
     return (
         block_out,
@@ -1177,7 +1179,7 @@
         grad_w[:, width : width + qwidth].T,
         grad_w[:, zat:xat],
         grad_w[:, xat:bat],
-        shared[:, 2 * KVH * HD :],
+        shared[:, 2 * KVH * HD : 2 * KVH * HD + 2 * NS],
         grad_w[:, dat : dat + heads],
         grad_conv_x,
         grad_conv_bc,

time: 413 us -> 399 us (0.966)
  waiting for transfers between devices: 145 us -> 129 us
  local copies, waits for them, and re-layouts: 33.7 us -> 22.4 us
  other arithmetic: 24 us -> 33.5 us
    ppermute x36 -> x33, waiting for transfers between devices: 138 us -> 116 us  [sent(): return lax.ppermute(values, 'tensor', pairs)]
    unnamed x141 -> x115, local copies, waits for them, and re-layouts: 20.5 us -> 10.3 us
    all_gather x1, waiting for transfers between devices: 0.01 us -> 6.38 us  [local(): ffn_w = lax.all_gather(ffn_own, 'dp', axis=0, tiled=True)]
    ppermute x36 -> x33, starting transfers between devices: 77.1 us -> 76.6 us  [sent(): return lax.ppermute(values, 'tensor', pairs)]
  transfers between devices with their start and end apart: 53 -> 50, of which waited for: 18 -> 18; matrix products, arithmetic and copies ran while one was open for 11% -> 13% of each run, Pallas kernels for 14% -> 16%
where the time goes in v1:
time: 399 us; the launch traced here: 392 us
  waiting for transfers between devices  129 us (32%)
  starting transfers between devices  100 us (25%)
  Pallas kernels  81.4 us (20%)
  other arithmetic  33.5 us (8%)
  local copies, waits for them, and re-layouts  22.4 us (6%)
  between operations  15.4 us (4%)
  matrix products  10.1 us (3%)
    ppermute x33, waiting for transfers between devices, sent(): return lax.ppermute(values, 'tensor', pairs)  116 us
    ppermute x33, starting transfers between devices, sent(): return lax.ppermute(values, 'tensor', pairs)  76.6 us
    ppermute x9, starting transfers between devices, shifted(): lax.ppermute(values, axis, [(i, (i + shift) % size) for i in range(size)])  20.7 us
    pallas_call x1, Pallas kernels, scan_backward(): pl.pallas_call(body, grid=(blocks,), in_specs=[pl.BlockSpec((BLOCK, width...  18.8 us
    pallas_call x1, Pallas kernels, ffn_both(): pl.pallas_call(ffn_kernel, grid=(parts,), in_specs=[rowspec, rowspec, pl....  17.5 us
    unnamed x115, local copies, waits for them, and re-layouts  10.3 us
    pallas_call x1, Pallas kernels, scan_forward(): pl.pallas_call(body, grid=(blocks,), in_specs=[pl.BlockSpec((BLOCK, width...  8.2 us
  transfers between devices with their start and end apart: 50, of which 18 were waited for; matrix products, arithmetic and copies ran while one was open for 13% of the time, Pallas kernels for 16%

profile of v1, /device:TPU:0, one launch (start us, length us, event | category | flops | bytes accessed | tf_op | source)
XLA Modules:
  0.0 391.9 jit_solution(13824271660653534722)
XLA Ops:
  8.7 2.2 pack_mixer.1
  11.0 5.0 %collective-permute-start.2 = (bf16[256,1024]{1,0:T(8,128)(2,1)}, bf16[256,1024]{1,0:T(8,128)(2,1)S(1)}, u32[]{:S(2)}, u32[]{:S(2)}) collective-permute-start(bf16[256,1024]{1,0:T(8,128)(2,1)} %refs_1_.3), channel_id=1, source_target_pairs={{0,1},{1,2},{2,3},{4,5},{5,6},{6,7},{8,9},{9,10},{10,11},{12,13},{... | collective-permute-start | bytes 1572872 | tf_op jit(solution)/shard_map/ppermute | solution.py:909
  17.3 2.0 pack_ffn.1
  19.3 4.6 %collective-permute-start = (bf16[128,1536]{1,0:T(8,128)(2,1)}, bf16[128,1536]{1,0:T(8,128)(2,1)S(1)}, u32[]{:S(2)}, u32[]{:S(2)}) collective-permute-start(bf16[128,1536]{1,0:T(8,128)(2,1)} %pack_ffn.1), channel_id=1, source_target_pairs={{0,1},{1,2},{2,3},{4,5},{5,6},{6,7},{8,9},{9,10},{10,11},{12,13},{... | collective-permute-start | bytes 1179656 | tf_op jit(solution)/shard_map/ppermute | solution.py:909
  25.1 10.7 %collective-permute-done = bf16[128,1536]{1,0:T(8,128)(2,1)S(1)} collective-permute-done((bf16[128,1536]{1,0:T(8,128)(2,1)}, bf16[128,1536]{1,0:T(8,128)(2,1)S(1)}, u32[]{:S(2)}, u32[]{:S(2)}) %collective-permute-start) | collective-permute-done | bytes 393248 | tf_op jit(solution)/shard_map/ppermute | solution.py:909
  35.9 4.0 %collective-permute-done.1 = bf16[128,1536]{1,0:T(8,128)(2,1)S(1)} collective-permute-done((bf16[128,1536]{1,0:T(8,128)(2,1)}, bf16[128,1536]{1,0:T(8,128)(2,1)S(1)}, u32[]{:S(2)}, u32[]{:S(2)}) %collective-permute-start.1) | collective-permute-done | bytes 393248 | tf_op jit(solution)/shard_map/ppermute | solution.py:909
  44.8 12.8 %collective-permute-done.4.refs_3_ = bf16[256,1024]{1,0:T(8,128)(2,1)S(1)} collective-permute-done((bf16[256,1024]{1,0:T(8,128)(2,1)S(1)}, bf16[256,1024]{1,0:T(8,128)(2,1)S(1)}, u32[]{:S(2)}, u32[]{:S(2)}) %collective-permute-start.4) | collective-permute-done | bytes 524320 | tf_op jit(solution)/shard_map/ppermute | solution.py:909
  57.6 8.9 %collective-permute-done.6.refs_5_ = bf16[256,1024]{1,0:T(8,128)(2,1)S(1)} collective-permute-done((bf16[256,1024]{1,0:T(8,128)(2,1)S(1)}, bf16[256,1024]{1,0:T(8,128)(2,1)S(1)}, u32[]{:S(2)}, u32[]{:S(2)}) %collective-permute-start.6) | collective-permute-done | bytes 524320 | tf_op jit(solution)/shard_map/ppermute | solution.py:909
  69.2 1.4 collective-permute-start.17
  72.0 2.0 convert_reduce_fusion.1
  74.1 4.4 %norm_rows.1.refs_1_.refs_5_ = bf16[1024,1024]{1,0:T(8,128)(2,1)} custom-call(s32[1]{0:T(128)} %bitcast.refs_0_, bf16[256,1024]{1,0:T(8,128)(2,1)} %refs_1_.3, bf16[256,1024]{1,0:T(8,128)(2,1)} %copy-done.31, bf16[256,1024]{1,0:T(8,128)(2,1)} %copy-done.33, bf16[256,1024]{1,0:T(8,128)(2,1)} %copy-done.34, bf16[256,1024]{1,0:T(8,128)(2,1)} %copy-done.35, ...), custom_call_target="tpu_custom_call" | custom-call | flops 10000000 | bytes 5000000 | tf_op jit(solution)/shard_map/norm_rows/pallas_call | solution.py:663
  78.5 5.0 %fusion.q_ref.kv_ref.refs_0_.refs_1_ = f32[1024,1408]{1,0:T(8,128)S(1)} fusion(bf16[1024,1024]{1,0:T(8,128)(2,1)} %norm_rows.1.refs_1_.refs_5_, bf16[1024,1920]{1,0:T(8,128)(2,1)S(1)} %copy-done.2), kind=kOutput, calls=%fused_computation.2 | convolution fusion | flops 2952790016 | bytes 10747904 | tf_op jit(solution)/shard_map/dot_general | solution.py:30
  83.8 8.2 %scan_fwd.1 = (f32[1024,384]{1,0:T(8,128)S(1)}, f32[1024,384]{1,0:T(8,128)S(1)}, bf16[8,128,384]{2,1,0:T(8,128)(2,1)S(1)}, f32[8,1024]{1,0:T(8,128)S(1)}) custom-call(f32[1024,1408]{1,0:T(8,128)S(1)} %fusion.q_ref.kv_ref.refs_0_.refs_1_, s32[1024,128]{1,0:T(8,128)S(1)} %broadcast_in_dim.73.start_ref.refs_1_.refs_2_, ...), custom_call_target="tpu_custom_call" | custom-call | flops 2000000000 | bytes 10000000 | tf_op jit(solution)/shard_map/scan_fwd/pallas_call | solution.py:497
  92.1 1.6 broadcast_select_fusion.4
  96.3 4.0 %collective-permute-start.10 = (f32[1,1024]{1,0:T(1,128)S(1)}, f32[1,1024]{1,0:T(1,128)S(1)}, u32[]{:S(2)}, u32[]{:S(2)}) collective-permute-start(f32[1,1024]{1,0:T(1,128)S(1)} %slice.135), channel_id=1, source_target_pairs={{0,3},{1,0},{2,1},{3,2},{4,7},{5,4},{6,5},{7,6},{8,11},{9,8},{10,9... | collective-permute-start | bytes 12296 | tf_op jit(solution)/shard_map/ppermute | solution.py:905
  100.4 2.7 collective-permute-start.8
  103.1 1.4 collective-permute-start.9
  104.6 2.8 copy-done.1
  107.4 4.4 %attn_fwd.1 = (bf16[1024,128]{1,0:T(8,128)(2,1)S(1)}, f32[1024,128]{1,0:T(8,128)S(1)}, bf16[1024,128]{1,0:T(8,128)(2,1)S(1)}, bf16[1024,128]{1,0:T(8,128)(2,1)S(1)}) custom-call(f32[1024,1408]{1,0:T(8,128)S(1)} %copy-done.1, f32[1024,1408]{1,0:T(8,128)S(1)} %copy-done.1, f32[1024,128]{1,0:T(8,128)S(1)} %copy-done.7, f32[1024,128]{1,0:T(8,128)S(1)} %copy-done.8, ...), custom_call_target="tpu_custom_call" | custom-call | flops 1000000000 | bytes 6000000 | tf_op jit(solution)/shard_map/attn_fwd/pallas_call | solution.py:165
  112.7 1.6 select_convert_fusion
  114.4 3.2 collective-permute-start.13
  120.2 1.5 collective-permute-start.12
  121.7 8.6 %collective-permute-done.13 = bf16[256,1024]{1,0:T(8,128)(2,1)S(1)} collective-permute-done((bf16[256,1024]{1,0:T(8,128)(2,1)}, bf16[256,1024]{1,0:T(8,128)(2,1)S(1)}, u32[]{:S(2)}, u32[]{:S(2)}) %collective-permute-start.13) | collective-permute-done | bytes 524320 | tf_op jit(solution)/shard_map/ppermute | solution.py:909
  130.3 9.1 %collective-permute-done.11 = bf16[256,1024]{1,0:T(8,128)(2,1)S(1)} collective-permute-done((bf16[256,1024]{1,0:T(8,128)(2,1)}, bf16[256,1024]{1,0:T(8,128)(2,1)S(1)}, u32[]{:S(2)}, u32[]{:S(2)}) %collective-permute-start.11) | collective-permute-done | bytes 524320 | tf_op jit(solution)/shard_map/ppermute | solution.py:909
  140.2 3.3 fusion.9
  143.5 5.3 %collective-permute-start.14 = (bf16[256,1024]{1,0:T(8,128)(2,1)}, bf16[256,1024]{1,0:T(8,128)(2,1)}, u32[]{:S(2)}, u32[]{:S(2)}) collective-permute-start(bf16[256,1024]{1,0:T(8,128)(2,1)} %get-tuple-element.217), channel_id=1, source_target_pairs={{0,1},{1,2},{2,3},{4,5},{5,6},{6,7},{8,9},{9,10},{10,11},{12,13},{... | collective-permute-start | bytes 1572872 | tf_op jit(solution)/shard_map/ppermute | solution.py:909
  150.1 1.7 fusion.22
  151.8 7.0 %collective-permute-done.14 = bf16[256,1024]{1,0:T(8,128)(2,1)} collective-permute-done((bf16[256,1024]{1,0:T(8,128)(2,1)}, bf16[256,1024]{1,0:T(8,128)(2,1)}, u32[]{:S(2)}, u32[]{:S(2)}) %collective-permute-start.14) | collective-permute-done | bytes 524320 | tf_op jit(solution)/shard_map/ppermute | solution.py:909
  158.8 4.9 %collective-permute-done.15 = bf16[256,1024]{1,0:T(8,128)(2,1)} collective-permute-done((bf16[256,1024]{1,0:T(8,128)(2,1)}, bf16[256,1024]{1,0:T(8,128)(2,1)}, u32[]{:S(2)}, u32[]{:S(2)}) %collective-permute-start.15) | collective-permute-done | bytes 524320 | tf_op jit(solution)/shard_map/ppermute | solution.py:909
  163.7 2.5 fusion.16
  166.2 6.4 %all-gather.5.cloned.1.call-done.w_ref = bf16[1024,6144]{1,0:T(8,128)(2,1)} async-done(((bf16[128,6144]{1,0:T(8,128)(2,1)}), bf16[1024,6144]{1,0:T(8,128)(2,1)}) %all-gather.5.cloned.1.call-update) | async-done | bytes 12582928 | tf_op jit(solution)/shard_map/all_gather | solution.py:1086
  172.6 17.5 %ffn_both.1 = (bf16[256,1024]{1,0:T(8,128)(2,1)}, f32[256,1024]{1,0:T(8,128)}, bf16[256,1024]{1,0:T(8,128)(2,1)}, f32[8,1024]{1,0:T(8,128)}, bf16[1024,6144]{1,0:T(8,128)(2,1)}) custom-call(f32[256,1024]{1,0:T(8,128)} %get-tuple-element.223.middle_ref, bf16[256,1024]{1,0:T(8,128)(2,1)} %cot_ref.1, f32[1,1024]{1,0:T(1,128)} %bitcast.32, ...), custom_call_target="tpu_custom_call" | custom-call | flops 10000000000 | bytes 30000000 | tf_op jit(solution)/shard_map/ffn_both/pallas_call | solution.py:876
  192.4 5.4 %collective-permute-start.20 = (bf16[256,1024]{1,0:T(8,128)(2,1)S(1)}, bf16[256,1024]{1,0:T(8,128)(2,1)}, u32[]{:S(2)}, u32[]{:S(2)}) collective-permute-start(bf16[256,1024]{1,0:T(8,128)(2,1)S(1)} %copy-done.12), channel_id=1, source_target_pairs={{0,1},{1,2},{2,3},{4,5},{5,6},{6,7},{8,9},{9,10},{10,11},{12,13},{... | collective-permute-start | bytes 1572872 | tf_op jit(solution)/shard_map/ppermute | solution.py:909
  197.7 9.4 %collective-permute-done.21.refs_7_ = bf16[256,1024]{1,0:T(8,128)(2,1)} collective-permute-done((bf16[256,1024]{1,0:T(8,128)(2,1)S(1)}, bf16[256,1024]{1,0:T(8,128)(2,1)}, u32[]{:S(2)}, u32[]{:S(2)}) %collective-permute-start.21) | collective-permute-done | bytes 524320 | tf_op jit(solution)/shard_map/ppermute | solution.py:909
  208.4 1.5 collective-permute-start.23
  211.2 1.7 collective-permute-start.25
  215.5 9.6 %collective-permute-done.22.refs_3_ = bf16[256,1024]{1,0:T(8,128)(2,1)} collective-permute-done((bf16[256,1024]{1,0:T(8,128)(2,1)}, bf16[256,1024]{1,0:T(8,128)(2,1)}, u32[]{:S(2)}, u32[]{:S(2)}) %collective-permute-start.22) | collective-permute-done | bytes 524320 | tf_op jit(solution)/shard_map/ppermute | solution.py:909
  225.1 9.6 %collective-permute-done.24.refs_5_ = bf16[256,1024]{1,0:T(8,128)(2,1)} collective-permute-done((bf16[256,1024]{1,0:T(8,128)(2,1)}, bf16[256,1024]{1,0:T(8,128)(2,1)}, u32[]{:S(2)}, u32[]{:S(2)}) %collective-permute-start.24) | collective-permute-done | bytes 524320 | tf_op jit(solution)/shard_map/ppermute | solution.py:909
  234.7 5.8 %branch_back.1 = (bf16[1024,128]{1,0:T(8,128)(2,1)S(1)}, f32[1024,384]{1,0:T(8,128)S(1)}, bf16[1024,512]{1,0:T(8,128)(2,1)S(1)}, f32[8,1024]{1,0:T(8,128)S(1)}, f32[8,384]{1,0:T(8,128)S(1)}) custom-call(s32[1]{0:T(128)} %bitcast.refs_0_, bf16[256,1024]{1,0:T(8,128)(2,1)S(1)} %copy-done.12, bf16[256,1024]{1,0:T(8,128)(2,1)} %collective-permute-done.20.refs_2_, ...), custom_call_target="tpu_custom_call" | custom-call | flops 2000000000 | bytes 10000000 | tf_op jit(solution)/shard_map/branch_back/pallas_call | solution.py:717
  240.6 2.3 collective-permute-start.26
  242.8 3.4 collective-permute-start.27
  246.3 6.6 %attn_bwd.1 = (bf16[1024,128]{1,0:T(8,128)(2,1)S(1)}, bf16[1024,128]{1,0:T(8,128)(2,1)S(1)}) custom-call(bf16[1024,128]{1,0:T(8,128)(2,1)S(1)} %copy-done.14, bf16[1024,128]{1,0:T(8,128)(2,1)S(1)} %copy-done.16, f32[1024,128]{1,0:T(8,128)S(1)} %copy-done.11, bf16[1024,128]{1,0:T(8,128)(2,1)S(1)} %get-tuple-element.81.out_ref, ...), custom_call_target="tpu_custom_call" | custom-call | flops 3000000000 | bytes 6000000 | tf_op jit(solution)/shard_map/attn_bwd/pallas_call | solution.py:185
  253.0 18.8 %scan_bwd.1 = (bf16[1024,1152]{1,0:T(8,128)(2,1)S(1)}, f32[8,640]{1,0:T(8,128)S(1)}, f32[16,128]{1,0:T(8,128)S(1)}, f32[8,384]{1,0:T(8,128)S(1)}) custom-call(f32[1024,1408]{1,0:T(8,128)S(1)} %bitcast.27, f32[1024,1408]{1,0:T(8,128)S(1)} %bitcast.27, s32[1024,128]{1,0:T(8,128)S(1)} %broadcast_in_dim.73.start_ref.refs_1_.refs_2_, ...), custom_call_target="tpu_custom_call" | custom-call | flops 6000000000 | bytes 20000000 | tf_op jit(solution)/shard_map/scan_bwd/pallas_call | solution.py:532
  271.8 6.6 %mixer_wgrad.1 = (bf16[512,1920]{1,0:T(8,128)(2,1)}, bf16[512,1920]{1,0:T(8,128)(2,1)S(1)}) custom-call(s32[1]{0:T(128)} %bitcast.6.refs_0_, bf16[1024,1024]{1,0:T(8,128)(2,1)S(1)} %copy-done.5, bf16[1024,128]{1,0:T(8,128)(2,1)S(1)} %get-tuple-element.102.refs_2_.refs_1_, bf16[1024,128]{1,0:T(8,128)(2,1)S(1)} %get-tuple-element.103.refs_3_.refs_2_, ...), custom_call_target="tpu_custom_call" | custom-call | flops 3000000000 | bytes 10000000 | tf_op jit(solution)/shard_map/mixer_wgrad/pallas_call | solution.py:767
  278.5 5.0 %back_proj.1 = (f32[256,1024]{1,0:T(8,128)S(1)}, bf16[256,1024]{1,0:T(8,128)(2,1)S(1)}, bf16[256,1024]{1,0:T(8,128)(2,1)S(1)}, bf16[256,1024]{1,0:T(8,128)(2,1)S(1)}, f32[8,1024]{1,0:T(8,128)S(1)}) custom-call(s32[1]{0:T(128)} %bitcast.refs_0_, bf16[1024,128]{1,0:T(8,128)(2,1)S(1)} %get-tuple-element.102.refs_2_.refs_1_, ...), custom_call_target="tpu_custom_call" | custom-call | flops 3000000000 | bytes 10000000 | tf_op jit(solution)/shard_map/back_proj/pallas_call | solution.py:819
  285.3 3.9 add_convert_fusion
  289.2 4.7 %collective-permute-start.29 = (bf16[256,1024]{1,0:T(8,128)(2,1)S(1)}, bf16[256,1024]{1,0:T(8,128)(2,1)}, u32[]{:S(2)}, u32[]{:S(2)}) collective-permute-start(bf16[256,1024]{1,0:T(8,128)(2,1)S(1)} %get-tuple-element.115), channel_id=1, source_target_pairs={{0,1},{3,2},{4,5},{7,6},{8,9},{11,10},{12,13},{15,14},{16,17},{19,... | collective-permute-start | bytes 1572872 | tf_op jit(solution)/shard_map/ppermute | solution.py:909
  293.9 1.5 collective-permute-start.30
  295.4 1.5 collective-permute-start.34
  296.9 3.3 collective-permute-start.31
  302.2 4.5 %collective-permute-done.35 = f32[16,1024]{1,0:T(8,128)S(1)} collective-permute-done((f32[16,1024]{1,0:T(8,128)S(1)}, f32[16,1024]{1,0:T(8,128)S(1)}, u32[]{:S(2)}, u32[]{:S(2)}) %collective-permute-start.35) | collective-permute-done | bytes 65568 | tf_op jit(solution)/shard_map/ppermute | solution.py:992
  309.8 6.3 %collective-permute-done.31 = bf16[256,1024]{1,0:T(8,128)(2,1)} collective-permute-done((bf16[256,1024]{1,0:T(8,128)(2,1)S(1)}, bf16[256,1024]{1,0:T(8,128)(2,1)}, u32[]{:S(2)}, u32[]{:S(2)}) %collective-permute-start.31) | collective-permute-done | bytes 524320 | tf_op jit(solution)/shard_map/ppermute | solution.py:909
  316.1 3.0 fusion.15
  319.1 5.9 %collective-permute-start.36 = (bf16[256,1024]{1,0:T(8,128)(2,1)}, bf16[256,1024]{1,0:T(8,128)(2,1)S(1)}, u32[]{:S(2)}, u32[]{:S(2)}) collective-permute-start(bf16[256,1024]{1,0:T(8,128)(2,1)} %get-tuple-element.216), channel_id=1, source_target_pairs={{0,1},{1,2},{2,3},{4,5},{5,6},{6,7},{8,9},{9,10},{10,11},{12,13},{... | collective-permute-start | bytes 1572872 | tf_op jit(solution)/shard_map/ppermute | solution.py:909
  326.4 5.3 %collective-permute-start.38 = (bf16[128,1536]{1,0:T(8,128)(2,1)S(1)}, bf16[128,1536]{1,0:T(8,128)(2,1)}, u32[]{:S(2)}, u32[]{:S(2)}) collective-permute-start(bf16[128,1536]{1,0:T(8,128)(2,1)S(1)} %get-tuple-element.214), channel_id=1, source_target_pairs={{0,1},{3,2},{4,5},{7,6},{8,9},{11,10},{12,13},{15,14},{16,17},{19,... | collective-permute-start | bytes 1179656 | tf_op jit(solution)/shard_map/ppermute | solution.py:909
  333.1 3.3 collective-permute-start.40
  338.4 7.5 %collective-permute-done.38 = bf16[128,1536]{1,0:T(8,128)(2,1)} collective-permute-done((bf16[128,1536]{1,0:T(8,128)(2,1)S(1)}, bf16[128,1536]{1,0:T(8,128)(2,1)}, u32[]{:S(2)}, u32[]{:S(2)}) %collective-permute-start.38) | collective-permute-done | bytes 393248 | tf_op jit(solution)/shard_map/ppermute | solution.py:909
  345.9 6.9 %collective-permute-done.40 = bf16[128,1536]{1,0:T(8,128)(2,1)} collective-permute-done((bf16[128,1536]{1,0:T(8,128)(2,1)S(1)}, bf16[128,1536]{1,0:T(8,128)(2,1)}, u32[]{:S(2)}, u32[]{:S(2)}) %collective-permute-start.40) | collective-permute-done | bytes 393248 | tf_op jit(solution)/shard_map/ppermute | solution.py:909
  355.8 4.5 %collective-permute-start.41 = (bf16[128,640]{1,0:T(8,128)(2,1)}, bf16[128,640]{1,0:T(8,128)(2,1)}, u32[]{:S(2)}, u32[]{:S(2)}) collective-permute-start(bf16[128,640]{1,0:T(8,128)(2,1)} %maximum_maximum_fusion), channel_id=1, source_target_pairs={{0,1},{1,2},{2,3},{3,0},{4,5},{5,6},{6,7},{7,4},{8,9},{9,10},{10,1... | collective-permute-start | bytes 491528 | tf_op jit(solution)/shard_map/ppermute | solution.py:905
  360.4 2.4 collective-permute-start.43
  365.1 2.6 fusion.18
  367.8 2.3 collective-permute-start.44
  372.2 1.6 copy.60
  374.9 2.6 fusion.7
  (252 shorter events, 56.5 us)
Async XLA Ops:
  7.2 36.8 %copy-start.48 = (f32[384]{0:T(512)S(1)}, f32[384]{0:T(512)}, u32[]{:S(2)}) copy-start(f32[384]{0:T(512)} %param.39) | copy-start | bytes 4612
  7.2 36.8 %copy-start.49 = (f32[256]{0:T(256)S(1)}, f32[256]{0:T(256)}, u32[]{:S(2)}) copy-start(f32[256]{0:T(256)} %param.40) | copy-start | bytes 3076
  7.2 36.8 %copy-start.50 = (f32[6]{0:T(128)S(1)}, f32[6]{0:T(128)}, u32[]{:S(2)}) copy-start(f32[6]{0:T(128)} %param.43) | copy-start | bytes 76
  7.2 36.9 %copy-start.51 = (f32[6]{0:T(128)S(1)}, f32[6]{0:T(128)}, u32[]{:S(2)}) copy-start(f32[6]{0:T(128)} %param.42) | copy-start | bytes 76
  7.2 37.0 %copy-start.52 = (f32[6]{0:T(128)S(1)}, f32[6]{0:T(128)}, u32[]{:S(2)}) copy-start(f32[6]{0:T(128)} %param.41) | copy-start | bytes 76
  7.2 37.0 %copy-start.44 = (f32[4,384]{1,0:T(4,128)S(1)}, f32[4,384]{1,0:T(4,128)}, u32[]{:S(2)}) copy-start(f32[4,384]{1,0:T(4,128)} %param.37) | copy-start | bytes 18436
  7.3 37.0 %copy-start.45 = (f32[4,256]{1,0:T(4,128)S(1)}, f32[4,256]{1,0:T(4,128)}, u32[]{:S(2)}) copy-start(f32[4,256]{1,0:T(4,128)} %param.38) | copy-start | bytes 12292
  7.3 37.0 %copy-start.42 = (s32[1,1024]{1,0:T(1,128)S(1)}, s32[1,1024]{1,0:T(1,128)}, u32[]{:S(2)}) copy-start(s32[1,1024]{1,0:T(1,128)} %param.28) | copy-start | bytes 12292
  7.3 64.7 %all-gather.3.cloned.1.call-start = ((), (), s32[]{:S(2)}) async-start(), calls=%async_computation.2 | async-start | bytes 4423680 | tf_op jit(solution)/shard_map/all_gather | solution.py:1054
  10.9 161.6 %all-gather.5.cloned.1.call-start = ((), (), s32[]{:S(2)}) async-start(), calls=%async_computation.3 | async-start | bytes 14155776 | tf_op jit(solution)/shard_map/all_gather | solution.py:1086
  11.0 28.9 %collective-permute-start.2 = (bf16[256,1024]{1,0:T(8,128)(2,1)}, bf16[256,1024]{1,0:T(8,128)(2,1)S(1)}, u32[]{:S(2)}, u32[]{:S(2)}) collective-permute-start(bf16[256,1024]{1,0:T(8,128)(2,1)} %refs_1_.3), channel_id=1, source_target_pairs={{0,1},{1,2},{2,3},{4,5},{5,6},{6,7},{8,9},{9,10},{10,11},{12,13},{... | collective-permute-start | bytes 1572872 | tf_op jit(solution)/shard_map/ppermute | solution.py:909
  16.0 24.0 %collective-permute-start.3 = (bf16[256,1024]{1,0:T(8,128)(2,1)}, bf16[256,1024]{1,0:T(8,128)(2,1)S(1)}, u32[]{:S(2)}, u32[]{:S(2)}) collective-permute-start(bf16[256,1024]{1,0:T(8,128)(2,1)} %refs_1_.3), channel_id=1, source_target_pairs={{1,0},{2,1},{3,2},{5,4},{6,5},{7,6},{9,8},{10,9},{11,10},{13,12},{... | collective-permute-start | bytes 1572872 | tf_op jit(solution)/shard_map/ppermute | solution.py:909
  19.3 16.6 %collective-permute-start = (bf16[128,1536]{1,0:T(8,128)(2,1)}, bf16[128,1536]{1,0:T(8,128)(2,1)S(1)}, u32[]{:S(2)}, u32[]{:S(2)}) collective-permute-start(bf16[128,1536]{1,0:T(8,128)(2,1)} %pack_ffn.1), channel_id=1, source_target_pairs={{0,1},{1,2},{2,3},{4,5},{5,6},{6,7},{8,9},{9,10},{10,11},{12,13},{... | collective-permute-start | bytes 1179656 | tf_op jit(solution)/shard_map/ppermute | solution.py:909
  23.8 16.1 %collective-permute-start.1 = (bf16[128,1536]{1,0:T(8,128)(2,1)}, bf16[128,1536]{1,0:T(8,128)(2,1)S(1)}, u32[]{:S(2)}, u32[]{:S(2)}) collective-permute-start(bf16[128,1536]{1,0:T(8,128)(2,1)} %pack_ffn.1), channel_id=1, source_target_pairs={{1,0},{2,1},{3,2},{5,4},{6,5},{7,6},{9,8},{10,9},{11,10},{13,12},{... | collective-permute-start | bytes 1179656 | tf_op jit(solution)/shard_map/ppermute | solution.py:909
  39.9 34.1 %copy-start.31 = (bf16[256,1024]{1,0:T(8,128)(2,1)}, bf16[256,1024]{1,0:T(8,128)(2,1)S(1)}, u32[]{:S(2)}) copy-start(bf16[256,1024]{1,0:T(8,128)(2,1)S(1)} %collective-permute-done.2.refs_2_) | copy-start | bytes 1572868
  39.9 34.1 %copy-start.32 = (bf16[256,1024]{1,0:T(8,128)(2,1)}, bf16[256,1024]{1,0:T(8,128)(2,1)S(1)}, u32[]{:S(2)}) copy-start(bf16[256,1024]{1,0:T(8,128)(2,1)S(1)} %collective-permute-done.3.refs_7_) | copy-start | bytes 1572868
  39.9 17.7 %collective-permute-start.4 = (bf16[256,1024]{1,0:T(8,128)(2,1)S(1)}, bf16[256,1024]{1,0:T(8,128)(2,1)S(1)}, u32[]{:S(2)}, u32[]{:S(2)}) collective-permute-start(bf16[256,1024]{1,0:T(8,128)(2,1)S(1)} %collective-permute-done.3.refs_7_), channel_id=1, source_target_pairs={{2,0},{6,4},{10,8},{14,12},{18,16},{22,20},{26,24},{30,28}} | collective-permute-start | bytes 1572872 | tf_op jit(solution)/shard_map/ppermute | solution.py:909
  41.2 16.4 %collective-permute-start.5 = (bf16[256,1024]{1,0:T(8,128)(2,1)S(1)}, bf16[256,1024]{1,0:T(8,128)(2,1)S(1)}, u32[]{:S(2)}, u32[]{:S(2)}) collective-permute-start(bf16[256,1024]{1,0:T(8,128)(2,1)S(1)} %collective-permute-done.2.refs_2_), channel_id=1, source_target_pairs={{1,2},{2,3},{5,6},{6,7},{9,10},{10,11},{13,14},{14,15},{17,18},{18... | collective-permute-start | bytes 1572872 | tf_op jit(solution)/shard_map/ppermute | solution.py:909
  41.9 24.6 %collective-permute-start.6 = (bf16[256,1024]{1,0:T(8,128)(2,1)S(1)}, bf16[256,1024]{1,0:T(8,128)(2,1)S(1)}, u32[]{:S(2)}, u32[]{:S(2)}) collective-permute-start(bf16[256,1024]{1,0:T(8,128)(2,1)S(1)} %collective-permute-done.3.refs_7_), channel_id=1, source_target_pairs={{2,1},{1,0},{6,5},{5,4},{10,9},{9,8},{14,13},{13,12},{18,17},{17,1... | collective-permute-start | bytes 1572872 | tf_op jit(solution)/shard_map/ppermute | solution.py:909
  43.3 23.3 %collective-permute-start.7 = (bf16[256,1024]{1,0:T(8,128)(2,1)S(1)}, bf16[256,1024]{1,0:T(8,128)(2,1)S(1)}, u32[]{:S(2)}, u32[]{:S(2)}) collective-permute-start(bf16[256,1024]{1,0:T(8,128)(2,1)S(1)} %collective-permute-done.2.refs_2_), channel_id=1, source_target_pairs={{1,3},{5,7},{9,11},{13,15},{17,19},{21,23},{25,27},{29,31}} | collective-permute-start | bytes 1572872 | tf_op jit(solution)/shard_map/ppermute | solution.py:909
  66.6 25.5 %collective-permute-start.16 = (bf16[128,1536]{1,0:T(8,128)(2,1)}, bf16[128,1536]{1,0:T(8,128)(2,1)}, u32[]{:S(2)}, u32[]{:S(2)}) collective-permute-start(bf16[128,1536]{1,0:T(8,128)(2,1)} %copy-done.39), channel_id=1, source_target_pairs={{2,0},{6,4},{10,8},{14,12},{18,16},{22,20},{26,24},{30,28}} | collective-permute-start | bytes 1179656 | tf_op jit(solution)/shard_map/ppermute | solution.py:909
  67.9 24.2 %collective-permute-start.18 = (bf16[128,1536]{1,0:T(8,128)(2,1)}, bf16[128,1536]{1,0:T(8,128)(2,1)}, u32[]{:S(2)}, u32[]{:S(2)}) collective-permute-start(bf16[128,1536]{1,0:T(8,128)(2,1)} %copy-done.39), channel_id=1, source_target_pairs={{2,1},{1,0},{6,5},{5,4},{10,9},{9,8},{14,13},{13,12},{18,17},{17,1... | collective-permute-start | bytes 1179656 | tf_op jit(solution)/shard_map/ppermute | solution.py:909
  69.2 22.9 %collective-permute-start.17 = (bf16[128,1536]{1,0:T(8,128)(2,1)}, bf16[128,1536]{1,0:T(8,128)(2,1)}, u32[]{:S(2)}, u32[]{:S(2)}) collective-permute-start(bf16[128,1536]{1,0:T(8,128)(2,1)} %copy-done.37), channel_id=1, source_target_pairs={{1,2},{2,3},{5,6},{6,7},{9,10},{10,11},{13,14},{14,15},{17,18},{18... | collective-permute-start | bytes 1179656 | tf_op jit(solution)/shard_map/ppermute | solution.py:909
  70.6 21.5 %collective-permute-start.19 = (bf16[128,1536]{1,0:T(8,128)(2,1)}, bf16[128,1536]{1,0:T(8,128)(2,1)}, u32[]{:S(2)}, u32[]{:S(2)}) collective-permute-start(bf16[128,1536]{1,0:T(8,128)(2,1)} %copy-done.37), channel_id=1, source_target_pairs={{1,3},{5,7},{9,11},{13,15},{17,19},{21,23},{25,27},{29,31}} | collective-permute-start | bytes 1179656 | tf_op jit(solution)/shard_map/ppermute | solution.py:909
  96.2 219.8 %reduce-scatter.3.cloned.1.call-start = ((), (), s32[]{:S(2)}) async-start(), calls=%async_computation.4 | async-start | bytes 14155776 | tf_op jit(solution)/shard_map/reduce_scatter | solution.py:1096
  96.3 15.5 %collective-permute-start.10 = (f32[1,1024]{1,0:T(1,128)S(1)}, f32[1,1024]{1,0:T(1,128)S(1)}, u32[]{:S(2)}, u32[]{:S(2)}) collective-permute-start(f32[1,1024]{1,0:T(1,128)S(1)} %slice.135), channel_id=1, source_target_pairs={{0,3},{1,0},{2,1},{3,2},{4,7},{5,4},{6,5},{7,6},{8,11},{9,8},{10,9... | collective-permute-start | bytes 12296 | tf_op jit(solution)/shard_map/ppermute | solution.py:905
  100.4 11.4 %collective-permute-start.8 = (f32[1,1024]{1,0:T(1,128)S(1)}, f32[1,1024]{1,0:T(1,128)S(1)}, u32[]{:S(2)}, u32[]{:S(2)}) collective-permute-start(f32[1,1024]{1,0:T(1,128)S(1)} %slice.135), channel_id=1, source_target_pairs={{0,1},{1,2},{2,3},{3,0},{4,5},{5,6},{6,7},{7,4},{8,9},{9,10},{10,1... | collective-permute-start | bytes 12296 | tf_op jit(solution)/shard_map/ppermute | solution.py:905
  103.1 8.7 %collective-permute-start.9 = (f32[1,1024]{1,0:T(1,128)S(1)}, f32[1,1024]{1,0:T(1,128)S(1)}, u32[]{:S(2)}, u32[]{:S(2)}) collective-permute-start(f32[1,1024]{1,0:T(1,128)S(1)} %slice.135), channel_id=1, source_target_pairs={{0,2},{1,3},{2,0},{3,1},{4,6},{5,7},{6,4},{7,5},{8,10},{9,11},{10,... | collective-permute-start | bytes 12296 | tf_op jit(solution)/shard_map/ppermute | solution.py:905
  114.4 15.9 %collective-permute-start.13 = (bf16[256,1024]{1,0:T(8,128)(2,1)}, bf16[256,1024]{1,0:T(8,128)(2,1)S(1)}, u32[]{:S(2)}, u32[]{:S(2)}) collective-permute-start(bf16[256,1024]{1,0:T(8,128)(2,1)} %get-tuple-element.238), channel_id=1, source_target_pairs={{0,2},{3,1},{4,6},{7,5},{8,10},{11,9},{12,14},{15,13},{16,18},{19,... | collective-permute-start | bytes 1572872 | tf_op jit(solution)/shard_map/ppermute | solution.py:909
  118.9 20.5 %collective-permute-start.11 = (bf16[256,1024]{1,0:T(8,128)(2,1)}, bf16[256,1024]{1,0:T(8,128)(2,1)S(1)}, u32[]{:S(2)}, u32[]{:S(2)}) collective-permute-start(bf16[256,1024]{1,0:T(8,128)(2,1)} %convolution_convert_fusion), channel_id=1, source_target_pairs={{0,1},{3,2},{4,5},{7,6},{8,9},{11,10},{12,13},{15,14},{16,17},{19,... | collective-permute-start | bytes 1572872 | tf_op jit(solution)/shard_map/ppermute | solution.py:909
  120.2 19.2 %collective-permute-start.12 = (bf16[256,1024]{1,0:T(8,128)(2,1)}, bf16[256,1024]{1,0:T(8,128)(2,1)}, u32[]{:S(2)}, u32[]{:S(2)}) collective-permute-start(bf16[256,1024]{1,0:T(8,128)(2,1)} %convolution_convert_fusion), channel_id=1, source_target_pairs={{1,2},{2,1},{5,6},{6,5},{9,10},{10,9},{13,14},{14,13},{17,18},{18,... | collective-permute-start | bytes 1572872 | tf_op jit(solution)/shard_map/ppermute | solution.py:909
  143.5 15.3 %collective-permute-start.14 = (bf16[256,1024]{1,0:T(8,128)(2,1)}, bf16[256,1024]{1,0:T(8,128)(2,1)}, u32[]{:S(2)}, u32[]{:S(2)}) collective-permute-start(bf16[256,1024]{1,0:T(8,128)(2,1)} %get-tuple-element.217), channel_id=1, source_target_pairs={{0,1},{1,2},{2,3},{4,5},{5,6},{6,7},{8,9},{9,10},{10,11},{12,13},{... | collective-permute-start | bytes 1572872 | tf_op jit(solution)/shard_map/ppermute | solution.py:909
  148.8 14.9 %collective-permute-start.15 = (bf16[256,1024]{1,0:T(8,128)(2,1)}, bf16[256,1024]{1,0:T(8,128)(2,1)}, u32[]{:S(2)}, u32[]{:S(2)}) collective-permute-start(bf16[256,1024]{1,0:T(8,128)(2,1)} %get-tuple-element.218), channel_id=1, source_target_pairs={{3,2},{2,1},{1,0},{7,6},{6,5},{5,4},{11,10},{10,9},{9,8},{15,14},{... | collective-permute-start | bytes 1572872 | tf_op jit(solution)/shard_map/ppermute | solution.py:909
  190.1 148.4 %reduce-scatter.5.cloned.1.call-start = ((), (), s32[]{:S(2)}) async-start(), calls=%async_computation.5 | async-start | bytes 2457600 | tf_op jit(solution)/shard_map/reduce_scatter | solution.py:975
  191.1 16.1 %collective-permute-start.21 = (bf16[256,1024]{1,0:T(8,128)(2,1)S(1)}, bf16[256,1024]{1,0:T(8,128)(2,1)}, u32[]{:S(2)}, u32[]{:S(2)}) collective-permute-start(bf16[256,1024]{1,0:T(8,128)(2,1)S(1)} %copy-done.12), channel_id=1, source_target_pairs={{1,0},{2,1},{3,2},{5,4},{6,5},{7,6},{9,8},{10,9},{11,10},{13,12},{... | collective-permute-start | bytes 1572872 | tf_op jit(solution)/shard_map/ppermute | solution.py:909
  192.4 16.1 %collective-permute-start.20 = (bf16[256,1024]{1,0:T(8,128)(2,1)S(1)}, bf16[256,1024]{1,0:T(8,128)(2,1)}, u32[]{:S(2)}, u32[]{:S(2)}) collective-permute-start(bf16[256,1024]{1,0:T(8,128)(2,1)S(1)} %copy-done.12), channel_id=1, source_target_pairs={{0,1},{1,2},{2,3},{4,5},{5,6},{6,7},{8,9},{9,10},{10,11},{12,13},{... | collective-permute-start | bytes 1572872 | tf_op jit(solution)/shard_map/ppermute | solution.py:909
  207.1 18.0 %collective-permute-start.22 = (bf16[256,1024]{1,0:T(8,128)(2,1)}, bf16[256,1024]{1,0:T(8,128)(2,1)}, u32[]{:S(2)}, u32[]{:S(2)}) collective-permute-start(bf16[256,1024]{1,0:T(8,128)(2,1)} %collective-permute-done.21.refs_7_), channel_id=1, source_target_pairs={{2,0},{6,4},{10,8},{14,12},{18,16},{22,20},{26,24},{30,28}} | collective-permute-start | bytes 1572872 | tf_op jit(solution)/shard_map/ppermute | solution.py:909
  208.4 16.7 %collective-permute-start.23 = (bf16[256,1024]{1,0:T(8,128)(2,1)}, bf16[256,1024]{1,0:T(8,128)(2,1)}, u32[]{:S(2)}, u32[]{:S(2)}) collective-permute-start(bf16[256,1024]{1,0:T(8,128)(2,1)} %collective-permute-done.20.refs_2_), channel_id=1, source_target_pairs={{1,2},{2,3},{5,6},{6,7},{9,10},{10,11},{13,14},{14,15},{17,18},{18... | collective-permute-start | bytes 1572872 | tf_op jit(solution)/shard_map/ppermute | solution.py:909
  209.9 24.8 %collective-permute-start.24 = (bf16[256,1024]{1,0:T(8,128)(2,1)}, bf16[256,1024]{1,0:T(8,128)(2,1)}, u32[]{:S(2)}, u32[]{:S(2)}) collective-permute-start(bf16[256,1024]{1,0:T(8,128)(2,1)} %collective-permute-done.21.refs_7_), channel_id=1, source_target_pairs={{2,1},{1,0},{6,5},{5,4},{10,9},{9,8},{14,13},{13,12},{18,17},{17,1... | collective-permute-start | bytes 1572872 | tf_op jit(solution)/shard_map/ppermute | solution.py:909
  211.2 23.5 %collective-permute-start.25 = (bf16[256,1024]{1,0:T(8,128)(2,1)}, bf16[256,1024]{1,0:T(8,128)(2,1)}, u32[]{:S(2)}, u32[]{:S(2)}) collective-permute-start(bf16[256,1024]{1,0:T(8,128)(2,1)} %collective-permute-done.20.refs_2_), channel_id=1, source_target_pairs={{1,3},{5,7},{9,11},{13,15},{17,19},{21,23},{25,27},{29,31}} | collective-permute-start | bytes 1572872 | tf_op jit(solution)/shard_map/ppermute | solution.py:909
  215.5 30.7 %copy-start.11 = (f32[1024,128]{1,0:T(8,128)S(1)}, f32[1024,128]{1,0:T(8,128)}, u32[]{:S(2)}) copy-start(f32[1024,128]{1,0:T(8,128)} %copy-done.10) | copy-start | bytes 1572868
  215.5 30.7 %copy-start.14 = (bf16[1024,128]{1,0:T(8,128)(2,1)S(1)}, bf16[1024,128]{1,0:T(8,128)(2,1)}, u32[]{:S(2)}) copy-start(bf16[1024,128]{1,0:T(8,128)(2,1)} %copy-done.13) | copy-start | bytes 786436
  215.5 30.7 %copy-start.16 = (bf16[1024,128]{1,0:T(8,128)(2,1)S(1)}, bf16[1024,128]{1,0:T(8,128)(2,1)}, u32[]{:S(2)}) copy-start(bf16[1024,128]{1,0:T(8,128)(2,1)} %copy-done.15) | copy-start | bytes 786436
  240.6 12.3 %collective-permute-start.26 = (f32[1,1024]{1,0:T(1,128)S(1)}, f32[1,1024]{1,0:T(1,128)S(1)}, u32[]{:S(2)}, u32[]{:S(2)}) collective-permute-start(f32[1,1024]{1,0:T(1,128)S(1)} %slice.138), channel_id=1, source_target_pairs={{0,1},{1,2},{2,3},{3,0},{4,5},{5,6},{6,7},{7,4},{8,9},{9,10},{10,1... | collective-permute-start | bytes 12296 | tf_op jit(solution)/shard_map/ppermute | solution.py:905
  242.8 10.0 %collective-permute-start.27 = (f32[1,1024]{1,0:T(1,128)S(1)}, f32[1,1024]{1,0:T(1,128)S(1)}, u32[]{:S(2)}, u32[]{:S(2)}) collective-permute-start(f32[1,1024]{1,0:T(1,128)S(1)} %slice.138), channel_id=1, source_target_pairs={{0,2},{1,3},{2,0},{3,1},{4,6},{5,7},{6,4},{7,5},{8,10},{9,11},{10,... | collective-permute-start | bytes 12296 | tf_op jit(solution)/shard_map/ppermute | solution.py:905
  246.2 6.7 %collective-permute-start.28 = (f32[1,1024]{1,0:T(1,128)S(1)}, f32[1,1024]{1,0:T(1,128)S(1)}, u32[]{:S(2)}, u32[]{:S(2)}) collective-permute-start(f32[1,1024]{1,0:T(1,128)S(1)} %slice.138), channel_id=1, source_target_pairs={{0,3},{1,0},{2,1},{3,2},{4,7},{5,4},{6,5},{7,6},{8,11},{9,8},{10,9... | collective-permute-start | bytes 12296 | tf_op jit(solution)/shard_map/ppermute | solution.py:905
  278.4 6.8 %collective-permute-start.33 = (bf16[512,1920]{1,0:T(8,128)(2,1)}, bf16[512,1920]{1,0:T(8,128)(2,1)}, u32[]{:S(2)}, u32[]{:S(2)}) collective-permute-start(bf16[512,1920]{1,0:T(8,128)(2,1)} %get-tuple-element.110), channel_id=1, source_target_pairs={{0,4},{4,0},{8,12},{12,8},{16,20},{20,16},{24,28},{28,24},{1,5},{5... | collective-permute-start | bytes 5898248 | tf_op jit(solution)/shard_map/ppermute | solution.py:968
  283.8 1.5 collective-permute-start.32
  289.2 26.9 %collective-permute-start.29 = (bf16[256,1024]{1,0:T(8,128)(2,1)S(1)}, bf16[256,1024]{1,0:T(8,128)(2,1)}, u32[]{:S(2)}, u32[]{:S(2)}) collective-permute-start(bf16[256,1024]{1,0:T(8,128)(2,1)S(1)} %get-tuple-element.115), channel_id=1, source_target_pairs={{0,1},{3,2},{4,5},{7,6},{8,9},{11,10},{12,13},{15,14},{16,17},{19,... | collective-permute-start | bytes 1572872 | tf_op jit(solution)/shard_map/ppermute | solution.py:909
  293.9 22.2 %collective-permute-start.30 = (bf16[256,1024]{1,0:T(8,128)(2,1)S(1)}, bf16[256,1024]{1,0:T(8,128)(2,1)}, u32[]{:S(2)}, u32[]{:S(2)}) collective-permute-start(bf16[256,1024]{1,0:T(8,128)(2,1)S(1)} %get-tuple-element.115), channel_id=1, source_target_pairs={{1,2},{2,1},{5,6},{6,5},{9,10},{10,9},{13,14},{14,13},{17,18},{18,... | collective-permute-start | bytes 1572872 | tf_op jit(solution)/shard_map/ppermute | solution.py:909
  295.4 6.0 %collective-permute-start.34 = (f32[16,1024]{1,0:T(8,128)S(1)}, f32[16,1024]{1,0:T(8,128)S(1)}, u32[]{:S(2)}, u32[]{:S(2)}) collective-permute-start(f32[16,1024]{1,0:T(8,128)S(1)} %add.182), channel_id=1, source_target_pairs={{0,8},{4,12},{8,0},{12,4},{16,24},{20,28},{24,16},{28,20},{1,9},{5... | collective-permute-start | bytes 196616 | tf_op jit(solution)/shard_map/ppermute | solution.py:992
  296.9 19.2 %collective-permute-start.31 = (bf16[256,1024]{1,0:T(8,128)(2,1)S(1)}, bf16[256,1024]{1,0:T(8,128)(2,1)}, u32[]{:S(2)}, u32[]{:S(2)}) collective-permute-start(bf16[256,1024]{1,0:T(8,128)(2,1)S(1)} %broadcast_select_fusion), channel_id=1, source_target_pairs={{0,2},{3,1},{4,6},{7,5},{8,10},{11,9},{12,14},{15,13},{16,18},{19,... | collective-permute-start | bytes 1572872 | tf_op jit(solution)/shard_map/ppermute | solution.py:909
  301.3 5.4 %collective-permute-start.35 = (f32[16,1024]{1,0:T(8,128)S(1)}, f32[16,1024]{1,0:T(8,128)S(1)}, u32[]{:S(2)}, u32[]{:S(2)}) collective-permute-start(f32[16,1024]{1,0:T(8,128)S(1)} %add.184), channel_id=1, source_target_pairs={{0,16},{4,20},{8,24},{12,28},{16,0},{20,4},{24,8},{28,12},{1,17},{... | collective-permute-start | bytes 196616 | tf_op jit(solution)/shard_map/ppermute | solution.py:992
  319.1 36.0 %copy-start.46 = (bf16[2,128]{1,0:T(2,128)(2,1)S(1)}, bf16[2,128]{1,0:T(2,128)(2,1)}, u32[]{:S(2)}) copy-start(bf16[2,128]{1,0:T(2,128)(2,1)} %dynamic-slice_convert_fusion) | copy-start | bytes 1540
  319.1 33.8 %collective-permute-start.36 = (bf16[256,1024]{1,0:T(8,128)(2,1)}, bf16[256,1024]{1,0:T(8,128)(2,1)S(1)}, u32[]{:S(2)}, u32[]{:S(2)}) collective-permute-start(bf16[256,1024]{1,0:T(8,128)(2,1)} %get-tuple-element.216), channel_id=1, source_target_pairs={{0,1},{1,2},{2,3},{4,5},{5,6},{6,7},{8,9},{9,10},{10,11},{12,13},{... | collective-permute-start | bytes 1572872 | tf_op jit(solution)/shard_map/ppermute | solution.py:909
  325.0 27.9 %collective-permute-start.37 = (bf16[256,1024]{1,0:T(8,128)(2,1)}, bf16[256,1024]{1,0:T(8,128)(2,1)S(1)}, u32[]{:S(2)}, u32[]{:S(2)}) collective-permute-start(bf16[256,1024]{1,0:T(8,128)(2,1)} %get-tuple-element.215), channel_id=1, source_target_pairs={{3,2},{2,1},{1,0},{7,6},{6,5},{5,4},{11,10},{10,9},{9,8},{15,14},{... | collective-permute-start | bytes 1572872 | tf_op jit(solution)/shard_map/ppermute | solution.py:909
  326.4 19.6 %collective-permute-start.38 = (bf16[128,1536]{1,0:T(8,128)(2,1)S(1)}, bf16[128,1536]{1,0:T(8,128)(2,1)}, u32[]{:S(2)}, u32[]{:S(2)}) collective-permute-start(bf16[128,1536]{1,0:T(8,128)(2,1)S(1)} %get-tuple-element.214), channel_id=1, source_target_pairs={{0,1},{3,2},{4,5},{7,6},{8,9},{11,10},{12,13},{15,14},{16,17},{19,... | collective-permute-start | bytes 1179656 | tf_op jit(solution)/shard_map/ppermute | solution.py:909
  331.7 14.3 %collective-permute-start.39 = (bf16[128,1536]{1,0:T(8,128)(2,1)S(1)}, bf16[128,1536]{1,0:T(8,128)(2,1)}, u32[]{:S(2)}, u32[]{:S(2)}) collective-permute-start(bf16[128,1536]{1,0:T(8,128)(2,1)S(1)} %get-tuple-element.214), channel_id=1, source_target_pairs={{1,2},{2,1},{5,6},{6,5},{9,10},{10,9},{13,14},{14,13},{17,18},{18,... | collective-permute-start | bytes 1179656 | tf_op jit(solution)/shard_map/ppermute | solution.py:909
  333.1 19.8 %collective-permute-start.40 = (bf16[128,1536]{1,0:T(8,128)(2,1)S(1)}, bf16[128,1536]{1,0:T(8,128)(2,1)}, u32[]{:S(2)}, u32[]{:S(2)}) collective-permute-start(bf16[128,1536]{1,0:T(8,128)(2,1)S(1)} %get-tuple-element.213), channel_id=1, source_target_pairs={{0,2},{3,1},{4,6},{7,5},{8,10},{11,9},{12,14},{15,13},{16,18},{19,... | collective-permute-start | bytes 1179656 | tf_op jit(solution)/shard_map/ppermute | solution.py:909
  355.8 22.5 %collective-permute-start.41 = (bf16[128,640]{1,0:T(8,128)(2,1)}, bf16[128,640]{1,0:T(8,128)(2,1)}, u32[]{:S(2)}, u32[]{:S(2)}) collective-permute-start(bf16[128,640]{1,0:T(8,128)(2,1)} %maximum_maximum_fusion), channel_id=1, source_target_pairs={{0,1},{1,2},{2,3},{3,0},{4,5},{5,6},{6,7},{7,4},{8,9},{9,10},{10,1... | collective-permute-start | bytes 491528 | tf_op jit(solution)/shard_map/ppermute | solution.py:905
  360.4 17.9 %collective-permute-start.42 = (bf16[128,640]{1,0:T(8,128)(2,1)}, bf16[128,640]{1,0:T(8,128)(2,1)}, u32[]{:S(2)}, u32[]{:S(2)}) collective-permute-start(bf16[128,640]{1,0:T(8,128)(2,1)} %maximum_maximum_fusion), channel_id=1, source_target_pairs={{0,2},{1,3},{2,0},{3,1},{4,6},{5,7},{6,4},{7,5},{8,10},{9,11},{10,... | collective-permute-start | bytes 491528 | tf_op jit(solution)/shard_map/ppermute | solution.py:905
  360.4 17.9 %collective-permute-start.43 = (bf16[128,640]{1,0:T(8,128)(2,1)}, bf16[128,640]{1,0:T(8,128)(2,1)}, u32[]{:S(2)}, u32[]{:S(2)}) collective-permute-start(bf16[128,640]{1,0:T(8,128)(2,1)} %maximum_maximum_fusion), channel_id=1, source_target_pairs={{0,3},{1,0},{2,1},{3,2},{4,7},{5,4},{6,5},{7,6},{8,11},{9,8},{10,9... | collective-permute-start | bytes 491528 | tf_op jit(solution)/shard_map/ppermute | solution.py:905
  367.8 14.1 %collective-permute-start.44 = (bf16[128,1536]{1,0:T(8,128)(2,1)}, bf16[128,1536]{1,0:T(8,128)(2,1)}, u32[]{:S(2)}, u32[]{:S(2)}) collective-permute-start(bf16[128,1536]{1,0:T(8,128)(2,1)} %get-tuple-element.211), channel_id=1, source_target_pairs={{0,1},{1,2},{2,3},{4,5},{5,6},{6,7},{8,9},{9,10},{10,11},{12,13},{... | collective-permute-start | bytes 1179656 | tf_op jit(solution)/shard_map/ppermute | solution.py:909
  370.1 11.8 %collective-permute-start.45 = (bf16[128,1536]{1,0:T(8,128)(2,1)}, bf16[128,1536]{1,0:T(8,128)(2,1)}, u32[]{:S(2)}, u32[]{:S(2)}) collective-permute-start(bf16[128,1536]{1,0:T(8,128)(2,1)} %get-tuple-element.212), channel_id=1, source_target_pairs={{3,2},{2,1},{1,0},{7,6},{6,5},{5,4},{11,10},{10,9},{9,8},{15,14},{... | collective-permute-start | bytes 1179656 | tf_op jit(solution)/shard_map/ppermute | solution.py:909
  (41 other events, 332.0 us)
Sparse Core Ops, SparseCore 0:
  11.1 38.3 all-gather.2
  96.4 76.1 all-gather.4
  190.2 92.3 reduce-scatter.2
  289.3 34.2 reduce-scatter.4

commit v2 on v1

--- a/solution.py
+++ b/solution.py
@@ -729,8 +729,15 @@
     )(rank, *pieces, out_w, att_mixed, gain)
 
 
-def wgrad_kernel(step, own, core_ref, rows_ref, gq_ref, gkv_ref, grest_ref, gow_ref, theirs_ref, ours_ref):
+def wgrad_kernel(step, own, core_ref, rows_ref, gq_ref, gkv_ref, grest_ref, gow_ref, theirs_ref, ours_ref, turned_ref):
     turn = pl.program_id(0)
+
+    @pl.when(turn == 0)
+    def _():
+        for row in range(0, rows_ref.shape[0], LANES):
+            span = slice(row, row + LANES)
+            turned_ref[:, span] = jnp.transpose(rows_ref[span, :].astype(F32)).astype(BF16)
+
     first = core_ref[0] == 0
     sources = []
     for ref in (gq_ref, gkv_ref, grest_ref, gow_ref):
@@ -748,7 +755,7 @@
                     count += 1
                 span = slice(lane, lane + count * LANES)
                 to = slice(at * LANES, (at + count) * LANES)
-                value = ref[:, span].astype(F32) if ref is gow_ref else mm_tn(rows_ref[...], ref[:, span])
+                value = ref[:, span].astype(F32) if ref is gow_ref else mm(turned_ref[...], ref[:, span])
                 for chip in range(value.shape[0] // (2 * own)):
                     even = value[2 * chip * own : (2 * chip + 1) * own]
                     odd = value[(2 * chip + 1) * own : (2 * chip + 2) * own]
@@ -770,6 +777,7 @@
         in_specs=[pl.BlockSpec(memory_space=pltpu.SMEM)] + [whole(arg.shape) for arg in args],
         out_specs=[pl.BlockSpec((model // 2, step * LANES), lambda i: (0, i))] * 2,
         out_shape=[jax.ShapeDtypeStruct((model // 2, width), BF16)] * 2,
+        scratch_shapes=[pltpu.VMEM((model, length), BF16)],
         compiler_params=pltpu.CompilerParams(vmem_limit_bytes=32 * MIB),
         cost_estimate=pl.CostEstimate(flops=3 * 10**9, bytes_accessed=10**7, transcendentals=0),
         name="mixer_wgrad",
@@ -828,14 +836,17 @@
     )(rank, grad_q, grad_kv, grad_rest, mixer_w, rows_one, gain, gain_two)
 
 
-def ffn_kernel(middle_ref, cot_ref, gain_ref, w_ref, out_ref, gmid_ref, glow_ref, ggain_ref, gw_ref, low_ref, sum_ref, gsum_ref):
+def ffn_kernel(middle_ref, cot_ref, gain_ref, w_ref, out_ref, gmid_ref, glow_ref, ggain_ref, gw_ref, low_ref, low_t_ref, cot_t_ref, sum_ref, gsum_ref):
     step = pl.program_id(0)
     hidden = w_ref.shape[1] // 3
 
     @pl.when(step == 0)
     def _():
         middle = middle_ref[...]
-        low_ref[...] = (middle * rms_scale(middle) * gain_ref[...]).astype(BF16)
+        low = middle * rms_scale(middle) * gain_ref[...]
+        low_ref[...] = low.astype(BF16)
+        low_t_ref[...] = jnp.transpose(low).astype(BF16)
+        cot_t_ref[...] = jnp.transpose(cot_ref[...].astype(F32)).astype(BF16)
         sum_ref[...] = jnp.zeros_like(sum_ref)
         gsum_ref[...] = jnp.zeros_like(gsum_ref)
 
@@ -847,12 +858,12 @@
     silu_gate = gate_pre * sig
     act = (silu_gate * up_pre).astype(BF16)
     sum_ref[...] += mm_nt(act, w_ref[:, 2 * hidden :])
-    gw_ref[:, 2 * hidden :] = mm_tn(cot, act).astype(BF16)
+    gw_ref[:, 2 * hidden :] = mm(cot_t_ref[...], act).astype(BF16)
     grad_hidden = mm(cot, w_ref[:, 2 * hidden :])
     grad_gate = (grad_hidden * up_pre * sig * (1.0 + gate_pre * (1.0 - sig))).astype(BF16)
     grad_up = (grad_hidden * silu_gate).astype(BF16)
-    gw_ref[:, :hidden] = mm_tn(low, grad_gate).astype(BF16)
-    gw_ref[:, hidden : 2 * hidden] = mm_tn(low, grad_up).astype(BF16)
+    gw_ref[:, :hidden] = mm(low_t_ref[...], grad_gate).astype(BF16)
+    gw_ref[:, hidden : 2 * hidden] = mm(low_t_ref[...], grad_up).astype(BF16)
     gsum_ref[...] += mm_nt(grad_gate, w_ref[:, :hidden]) + mm_nt(grad_up, w_ref[:, hidden : 2 * hidden])
 
     @pl.when(step == pl.num_programs(0) - 1)
@@ -887,6 +898,8 @@
         ],
         scratch_shapes=[
             pltpu.VMEM((rows, model), BF16),
+            pltpu.VMEM((model, rows), BF16),
+            pltpu.VMEM((model, rows), BF16),
             pltpu.VMEM((rows, model), F32),
             pltpu.VMEM((rows, model), F32),
         ],
@@ -1058,7 +1071,7 @@
     gain_two = mixer_w[:, dat + HD + 1].astype(F32)[None, :]
     ffn_own = pack_ffn(w_gate, w_up, w_down)
     ffn_first, x_first = lax.optimization_barrier((first_phase(ffn_own, parts), first_phase(x_in, parts)))
-    x_pieces = second_phase(x_in, x_first, parts)
+    x_pieces = after(second_phase(x_in, x_first, parts), gain_one, gain_two)
     ffn_pieces = second_phase(ffn_own, after(ffn_first, x_pieces), parts)
 
     seg = segments[0]
@@ -1130,11 +1143,12 @@
     size = lax.axis_size("dp")
     small = small + lax.ppermute(small, "dp", [(i, i ^ 1) for i in range(size)])
 
-    chip_share = chip_total(theirs, ours, small)
-    small = butterfly(after(small, chip_share), "dp", size, 2)
-    firsts = after(sum_first(terms, rank, parts), small, grad_ffn_own)
+    firsts = sum_first(terms, rank, parts)
+    chip_share = chip_total(theirs, ours, firsts)
+    firsts = after(firsts, grad_ffn_own)
     seconds = sum_second(terms, firsts, rank, parts)
     grad_w = sum_over_chips(chip_share)
+    small = butterfly(after(small, seconds), "dp", size, 2)
     seconds, ffn_firsts, grad_w = lax.optimization_barrier((seconds, sum_first(ffn_terms, rank, parts), grad_w))
     ffn_seconds = sum_second(ffn_terms, ffn_firsts, rank, parts)
     grad_one = sum_last(terms, seconds)
@@ -1159,13 +1173,19 @@
         ],
         axis=0,
     )
-    keyval = jnp.zeros((own, 2 * KVH * HD), BF16)
-    keyval = lax.dynamic_update_slice(keyval, grad_w[:, qwidth : qwidth + HD], (0, kv_head * HD))
-    keyval = lax.dynamic_update_slice(keyval, grad_w[:, qwidth + HD : zat], (0, (KVH + kv_head) * HD))
-    shared = group_total(jnp.concatenate([keyval, grad_w[:, bat:dat], small_rows.astype(BF16)], axis=1), parts)
+    payload = jnp.concatenate([grad_w[:, qwidth:zat], grad_w[:, bat:dat], small_rows.astype(BF16)], axis=1)
+    same, other, shared = 0.0, 0.0, 0.0
+    for shift in range(parts):
+        share = (shifted(payload, "tensor", parts, shift) if shift else payload).astype(F32)
+        head = (lax.rem(rank + parts - shift, parts) * (qwidth // HD)) // (QH // KVH)
+        shared = shared + share[:, 2 * HD :]
+        same = same + jnp.where(head == kv_head, share[:, : 2 * HD], 0.0)
+        other = other + jnp.where(head == kv_head, 0.0, share[:, : 2 * HD])
+    first, second = jnp.where(kv_head == 0, same, other), jnp.where(kv_head == 0, other, same)
+    grad_keyval = jnp.concatenate([first[:, :HD], second[:, :HD], first[:, HD:], second[:, HD:]], axis=1)
     grad_ffn = sum_last(ffn_terms, ffn_seconds)
     grad_w = grad_w.astype(F32)
-    small_rows = shared[:, 2 * KVH * HD + 2 * NS :]
+    small_rows = shared[:, 2 * NS :]
     grad_norm_one, grad_norm_two = small_rows[0, :own], small_rows[1, :own]
     conv_parts = jnp.concatenate([small_rows[2 : KW + 3], small_rows[KW + 3 : 2 * KW + 4]], axis=1)
     grad_conv_bc, grad_bias_bc = conv_parts[:KW], conv_parts[KW]
@@ -1175,11 +1195,11 @@
         grad_input,
         grad_norm_one,
         grad_w[:, :qwidth],
-        shared[:, : 2 * KVH * HD],
+        grad_keyval,
         grad_w[:, width : width + qwidth].T,
         grad_w[:, zat:xat],
         grad_w[:, xat:bat],
-        shared[:, 2 * KVH * HD : 2 * KVH * HD + 2 * NS],
+        shared[:, : 2 * NS],
         grad_w[:, dat : dat + heads],
         grad_conv_x,
         grad_conv_bc,

time: 399 us -> 403 us (1.010)
  waiting for transfers between devices: 129 us -> 141 us
  other arithmetic: 33.5 us -> 29.4 us
    reduce_scatter x1, waiting for transfers between devices: 0.01 us -> 13.3 us  [sum_over_chips(): lax.psum_scatter(values, 'dp', scatter_dimension=0, axis_index_groups=gro...]
    all_gather x1, waiting for transfers between devices: 0.01 us -> 4.6 us  [local(): mixer_w = lax.all_gather(mixer_own, 'dp', axis=0, tiled=True)]
    ppermute x2, waiting for transfers between devices: 5.64 us -> 1.39 us  [butterfly(): lax.ppermute(values, axis, [(i, i ^ step) for i in range(size)])]
    unnamed x115 -> x113, local copies, waits for them, and re-layouts: 10.3 us -> 10.2 us
  transfers between devices with their start and end apart: 50 -> 50, of which waited for: 18 -> 20; matrix products, arithmetic and copies ran while one was open for 13% -> 10% of each run, Pallas kernels for 16% -> 16%
where the time goes in v2:
time: 403 us; the launch traced here: 396 us
  waiting for transfers between devices  141 us (35%)
  starting transfers between devices  100 us (25%)
  Pallas kernels  81.6 us (20%)
  other arithmetic  29.4 us (7%)
  local copies, waits for them, and re-layouts  18.6 us (5%)
  between operations  15.5 us (4%)
  matrix products  10.1 us (3%)
    ppermute x33, waiting for transfers between devices, sent(): return lax.ppermute(values, 'tensor', pairs)  112 us
    ppermute x33, starting transfers between devices, sent(): return lax.ppermute(values, 'tensor', pairs)  78.7 us
    ppermute x9, starting transfers between devices, shifted(): lax.ppermute(values, axis, [(i, (i + shift) % size) for i in range(size)])  19 us
    pallas_call x1, Pallas kernels, scan_backward(): pl.pallas_call(body, grid=(blocks,), in_specs=[pl.BlockSpec((BLOCK, width...  18.7 us
    pallas_call x1, Pallas kernels, ffn_both(): pl.pallas_call(ffn_kernel, grid=(parts,), in_specs=[rowspec, rowspec, pl....  17.8 us
    reduce_scatter x1, waiting for transfers between devices, sum_over_chips(): lax.psum_scatter(values, 'dp', scatter_dimension=0, axis_index_groups=gro...  13.3 us
    unnamed x113, local copies, waits for them, and re-layouts  10.2 us
    pallas_call x1, Pallas kernels, scan_forward(): pl.pallas_call(body, grid=(blocks,), in_specs=[pl.BlockSpec((BLOCK, width...  8.21 us
  transfers between devices with their start and end apart: 50, of which 20 were waited for; matrix products, arithmetic and copies ran while one was open for 10% of the time, Pallas kernels for 16%

profile of v2, /device:TPU:0, one launch (start us, length us, event | category | flops | bytes accessed | tf_op | source)
XLA Modules:
  0.0 396.3 jit_solution(6313460719621202012)
XLA Ops:
  8.7 2.2 pack_mixer.1
  11.0 5.0 %collective-permute-start.2 = (bf16[256,1024]{1,0:T(8,128)(2,1)}, bf16[256,1024]{1,0:T(8,128)(2,1)S(1)}, u32[]{:S(2)}, u32[]{:S(2)}) collective-permute-start(bf16[256,1024]{1,0:T(8,128)(2,1)} %refs_1_.2), channel_id=1, source_target_pairs={{0,1},{1,2},{2,3},{4,5},{5,6},{6,7},{8,9},{9,10},{10,11},{12,13},{... | collective-permute-start | bytes 1572872 | tf_op jit(solution)/shard_map/ppermute | solution.py:922
  17.3 2.0 pack_ffn.1
  19.2 4.6 %collective-permute-start = (bf16[128,1536]{1,0:T(8,128)(2,1)}, bf16[128,1536]{1,0:T(8,128)(2,1)S(1)}, u32[]{:S(2)}, u32[]{:S(2)}) collective-permute-start(bf16[128,1536]{1,0:T(8,128)(2,1)} %pack_ffn.1), channel_id=1, source_target_pairs={{0,1},{1,2},{2,3},{4,5},{5,6},{6,7},{8,9},{9,10},{10,11},{12,13},{... | collective-permute-start | bytes 1179656 | tf_op jit(solution)/shard_map/ppermute | solution.py:922
  25.1 10.8 %collective-permute-done = bf16[128,1536]{1,0:T(8,128)(2,1)S(1)} collective-permute-done((bf16[128,1536]{1,0:T(8,128)(2,1)}, bf16[128,1536]{1,0:T(8,128)(2,1)S(1)}, u32[]{:S(2)}, u32[]{:S(2)}) %collective-permute-start) | collective-permute-done | bytes 393248 | tf_op jit(solution)/shard_map/ppermute | solution.py:922
  35.9 4.0 %collective-permute-done.1 = bf16[128,1536]{1,0:T(8,128)(2,1)S(1)} collective-permute-done((bf16[128,1536]{1,0:T(8,128)(2,1)}, bf16[128,1536]{1,0:T(8,128)(2,1)S(1)}, u32[]{:S(2)}, u32[]{:S(2)}) %collective-permute-start.1) | collective-permute-done | bytes 393248 | tf_op jit(solution)/shard_map/ppermute | solution.py:922
  44.8 4.6 %all-gather.3.cloned.1.call-done.refs_4_ = bf16[1024,1920]{1,0:T(8,128)(2,1)} async-done(((bf16[128,1920]{1,0:T(8,128)(2,1)}), bf16[1024,1920]{1,0:T(8,128)(2,1)}) %all-gather.3.cloned.1.call-update) | async-done | bytes 3932176 | tf_op jit(solution)/shard_map/all_gather | solution.py:1067
  49.4 2.1 convert_reduce_fusion.1
  51.5 6.1 %collective-permute-done.4.refs_3_ = bf16[256,1024]{1,0:T(8,128)(2,1)S(1)} collective-permute-done((bf16[256,1024]{1,0:T(8,128)(2,1)S(1)}, bf16[256,1024]{1,0:T(8,128)(2,1)S(1)}, u32[]{:S(2)}, u32[]{:S(2)}) %collective-permute-start.4) | collective-permute-done | bytes 524320 | tf_op jit(solution)/shard_map/ppermute | solution.py:922
  57.6 8.9 %collective-permute-done.6.refs_5_ = bf16[256,1024]{1,0:T(8,128)(2,1)S(1)} collective-permute-done((bf16[256,1024]{1,0:T(8,128)(2,1)S(1)}, bf16[256,1024]{1,0:T(8,128)(2,1)S(1)}, u32[]{:S(2)}, u32[]{:S(2)}) %collective-permute-start.6) | collective-permute-done | bytes 524320 | tf_op jit(solution)/shard_map/ppermute | solution.py:922
  69.2 1.4 collective-permute-start.17
  72.1 4.4 %norm_rows.1.refs_1_.refs_5_ = bf16[1024,1024]{1,0:T(8,128)(2,1)} custom-call(s32[1]{0:T(128)} %bitcast.refs_0_, bf16[256,1024]{1,0:T(8,128)(2,1)} %refs_1_.2, bf16[256,1024]{1,0:T(8,128)(2,1)} %copy-done.33, bf16[256,1024]{1,0:T(8,128)(2,1)} %copy-done.35, bf16[256,1024]{1,0:T(8,128)(2,1)} %copy-done.36, bf16[256,1024]{1,0:T(8,128)(2,1)} %copy-done.37, ...), custom_call_target="tpu_custom_call" | custom-call | flops 10000000 | bytes 5000000 | tf_op jit(solution)/shard_map/norm_rows/pallas_call | solution.py:663
  76.5 5.0 %fusion.q_ref.kv_ref.refs_0_.refs_1_ = f32[1024,1408]{1,0:T(8,128)S(1)} fusion(bf16[1024,1024]{1,0:T(8,128)(2,1)} %norm_rows.1.refs_1_.refs_5_, bf16[1024,1920]{1,0:T(8,128)(2,1)S(1)} %copy-done.2), kind=kOutput, calls=%fused_computation.2 | convolution fusion | flops 2952790016 | bytes 10747904 | tf_op jit(solution)/shard_map/dot_general | solution.py:30
  81.8 8.2 %scan_fwd.1 = (f32[1024,384]{1,0:T(8,128)S(1)}, f32[1024,384]{1,0:T(8,128)S(1)}, bf16[8,128,384]{2,1,0:T(8,128)(2,1)S(1)}, f32[8,1024]{1,0:T(8,128)S(1)}) custom-call(f32[1024,1408]{1,0:T(8,128)S(1)} %fusion.q_ref.kv_ref.refs_0_.refs_1_, s32[1024,128]{1,0:T(8,128)S(1)} %broadcast_in_dim.82.start_ref.refs_1_.refs_2_, ...), custom_call_target="tpu_custom_call" | custom-call | flops 2000000000 | bytes 10000000 | tf_op jit(solution)/shard_map/scan_fwd/pallas_call | solution.py:497
  90.1 1.6 broadcast_select_fusion.4
  94.3 5.0 %collective-permute-start.10 = (f32[1,1024]{1,0:T(1,128)S(1)}, f32[1,1024]{1,0:T(1,128)S(1)}, u32[]{:S(2)}, u32[]{:S(2)}) collective-permute-start(f32[1,1024]{1,0:T(1,128)S(1)} %slice.170), channel_id=1, source_target_pairs={{0,3},{1,0},{2,1},{3,2},{4,7},{5,4},{6,5},{7,6},{8,11},{9,8},{10,9... | collective-permute-start | bytes 12296 | tf_op jit(solution)/shard_map/ppermute | solution.py:918
  99.3 1.8 collective-permute-start.8
  102.5 2.8 copy-done.1
  105.4 4.4 %attn_fwd.1 = (bf16[1024,128]{1,0:T(8,128)(2,1)S(1)}, f32[1024,128]{1,0:T(8,128)S(1)}, bf16[1024,128]{1,0:T(8,128)(2,1)S(1)}, bf16[1024,128]{1,0:T(8,128)(2,1)S(1)}) custom-call(f32[1024,1408]{1,0:T(8,128)S(1)} %copy-done.1, f32[1024,1408]{1,0:T(8,128)S(1)} %copy-done.1, f32[1024,128]{1,0:T(8,128)S(1)} %copy-done.6, f32[1024,128]{1,0:T(8,128)S(1)} %copy-done.7, ...), custom_call_target="tpu_custom_call" | custom-call | flops 1000000000 | bytes 6000000 | tf_op jit(solution)/shard_map/attn_fwd/pallas_call | solution.py:165
  110.7 1.6 select_convert_fusion
  112.4 3.2 collective-permute-start.13
  116.9 2.1 collective-permute-start.11
  119.0 1.5 collective-permute-start.12
  120.4 7.9 %collective-permute-done.13 = bf16[256,1024]{1,0:T(8,128)(2,1)S(1)} collective-permute-done((bf16[256,1024]{1,0:T(8,128)(2,1)}, bf16[256,1024]{1,0:T(8,128)(2,1)S(1)}, u32[]{:S(2)}, u32[]{:S(2)}) %collective-permute-start.13) | collective-permute-done | bytes 524320 | tf_op jit(solution)/shard_map/ppermute | solution.py:922
  128.3 9.1 %collective-permute-done.11 = bf16[256,1024]{1,0:T(8,128)(2,1)} collective-permute-done((bf16[256,1024]{1,0:T(8,128)(2,1)}, bf16[256,1024]{1,0:T(8,128)(2,1)}, u32[]{:S(2)}, u32[]{:S(2)}) %collective-permute-start.11) | collective-permute-done | bytes 524320 | tf_op jit(solution)/shard_map/ppermute | solution.py:922
  137.4 3.3 fusion.9
  140.7 5.3 %collective-permute-start.14 = (bf16[256,1024]{1,0:T(8,128)(2,1)}, bf16[256,1024]{1,0:T(8,128)(2,1)}, u32[]{:S(2)}, u32[]{:S(2)}) collective-permute-start(bf16[256,1024]{1,0:T(8,128)(2,1)} %get-tuple-element.234), channel_id=1, source_target_pairs={{0,1},{1,2},{2,3},{4,5},{5,6},{6,7},{8,9},{9,10},{10,11},{12,13},{... | collective-permute-start | bytes 1572872 | tf_op jit(solution)/shard_map/ppermute | solution.py:922
  147.4 1.7 fusion.22
  149.1 7.8 %collective-permute-done.14 = bf16[256,1024]{1,0:T(8,128)(2,1)} collective-permute-done((bf16[256,1024]{1,0:T(8,128)(2,1)}, bf16[256,1024]{1,0:T(8,128)(2,1)}, u32[]{:S(2)}, u32[]{:S(2)}) %collective-permute-start.14) | collective-permute-done | bytes 524320 | tf_op jit(solution)/shard_map/ppermute | solution.py:922
  156.9 4.9 %collective-permute-done.15 = bf16[256,1024]{1,0:T(8,128)(2,1)} collective-permute-done((bf16[256,1024]{1,0:T(8,128)(2,1)}, bf16[256,1024]{1,0:T(8,128)(2,1)}, u32[]{:S(2)}, u32[]{:S(2)}) %collective-permute-start.15) | collective-permute-done | bytes 524320 | tf_op jit(solution)/shard_map/ppermute | solution.py:922
  161.8 2.5 fusion.16
  164.2 6.3 %all-gather.5.cloned.1.call-done.w_ref = bf16[1024,6144]{1,0:T(8,128)(2,1)} async-done(((bf16[128,6144]{1,0:T(8,128)(2,1)}), bf16[1024,6144]{1,0:T(8,128)(2,1)}) %all-gather.5.cloned.1.call-update) | async-done | bytes 12582928 | tf_op jit(solution)/shard_map/all_gather | solution.py:1099
  170.6 17.8 %ffn_both.1 = (bf16[256,1024]{1,0:T(8,128)(2,1)}, f32[256,1024]{1,0:T(8,128)}, bf16[256,1024]{1,0:T(8,128)(2,1)}, f32[8,1024]{1,0:T(8,128)}, bf16[1024,6144]{1,0:T(8,128)(2,1)}) custom-call(f32[256,1024]{1,0:T(8,128)} %get-tuple-element.240.middle_ref, bf16[256,1024]{1,0:T(8,128)(2,1)} %cot_ref.1, f32[1,1024]{1,0:T(1,128)} %bitcast.32, ...), custom_call_target="tpu_custom_call" | custom-call | flops 10000000000 | bytes 30000000 | tf_op jit(solution)/shard_map/ffn_both/pallas_call | solution.py:887
  190.7 5.4 %collective-permute-start.20 = (bf16[256,1024]{1,0:T(8,128)(2,1)S(1)}, bf16[256,1024]{1,0:T(8,128)(2,1)}, u32[]{:S(2)}, u32[]{:S(2)}) collective-permute-start(bf16[256,1024]{1,0:T(8,128)(2,1)S(1)} %copy-done.11), channel_id=1, source_target_pairs={{0,1},{1,2},{2,3},{4,5},{5,6},{6,7},{8,9},{9,10},{10,11},{12,13},{... | collective-permute-start | bytes 1572872 | tf_op jit(solution)/shard_map/ppermute | solution.py:922
  196.0 9.4 %collective-permute-done.21.refs_7_ = bf16[256,1024]{1,0:T(8,128)(2,1)} collective-permute-done((bf16[256,1024]{1,0:T(8,128)(2,1)S(1)}, bf16[256,1024]{1,0:T(8,128)(2,1)}, u32[]{:S(2)}, u32[]{:S(2)}) %collective-permute-start.21) | collective-permute-done | bytes 524320 | tf_op jit(solution)/shard_map/ppermute | solution.py:922
  206.8 1.5 collective-permute-start.23
  209.5 1.7 collective-permute-start.25
  213.9 9.6 %collective-permute-done.22.refs_3_ = bf16[256,1024]{1,0:T(8,128)(2,1)} collective-permute-done((bf16[256,1024]{1,0:T(8,128)(2,1)}, bf16[256,1024]{1,0:T(8,128)(2,1)}, u32[]{:S(2)}, u32[]{:S(2)}) %collective-permute-start.22) | collective-permute-done | bytes 524320 | tf_op jit(solution)/shard_map/ppermute | solution.py:922
  223.5 9.6 %collective-permute-done.24.refs_5_ = bf16[256,1024]{1,0:T(8,128)(2,1)} collective-permute-done((bf16[256,1024]{1,0:T(8,128)(2,1)}, bf16[256,1024]{1,0:T(8,128)(2,1)}, u32[]{:S(2)}, u32[]{:S(2)}) %collective-permute-start.24) | collective-permute-done | bytes 524320 | tf_op jit(solution)/shard_map/ppermute | solution.py:922
  233.1 5.8 %branch_back.1 = (bf16[1024,128]{1,0:T(8,128)(2,1)S(1)}, f32[1024,384]{1,0:T(8,128)S(1)}, bf16[1024,512]{1,0:T(8,128)(2,1)S(1)}, f32[8,1024]{1,0:T(8,128)S(1)}, f32[8,384]{1,0:T(8,128)S(1)}) custom-call(s32[1]{0:T(128)} %bitcast.refs_0_, bf16[256,1024]{1,0:T(8,128)(2,1)S(1)} %copy-done.11, bf16[256,1024]{1,0:T(8,128)(2,1)} %collective-permute-done.20.refs_2_, ...), custom_call_target="tpu_custom_call" | custom-call | flops 2000000000 | bytes 10000000 | tf_op jit(solution)/shard_map/branch_back/pallas_call | solution.py:717
  238.9 2.3 collective-permute-start.26
  241.2 3.4 collective-permute-start.27
  244.6 6.6 %attn_bwd.1 = (bf16[1024,128]{1,0:T(8,128)(2,1)S(1)}, bf16[1024,128]{1,0:T(8,128)(2,1)S(1)}) custom-call(bf16[1024,128]{1,0:T(8,128)(2,1)S(1)} %copy-done.13, bf16[1024,128]{1,0:T(8,128)(2,1)S(1)} %copy-done.15, f32[1024,128]{1,0:T(8,128)S(1)} %copy-done.10, bf16[1024,128]{1,0:T(8,128)(2,1)S(1)} %get-tuple-element.95.out_ref, ...), custom_call_target="tpu_custom_call" | custom-call | flops 3000000000 | bytes 6000000 | tf_op jit(solution)/shard_map/attn_bwd/pallas_call | solution.py:185
  251.4 18.7 %scan_bwd.1 = (bf16[1024,1152]{1,0:T(8,128)(2,1)S(1)}, f32[8,640]{1,0:T(8,128)S(1)}, f32[16,128]{1,0:T(8,128)S(1)}, f32[8,384]{1,0:T(8,128)S(1)}) custom-call(f32[1024,1408]{1,0:T(8,128)S(1)} %bitcast.27, f32[1024,1408]{1,0:T(8,128)S(1)} %bitcast.27, s32[1024,128]{1,0:T(8,128)S(1)} %broadcast_in_dim.82.start_ref.refs_1_.refs_2_, ...), custom_call_target="tpu_custom_call" | custom-call | flops 6000000000 | bytes 20000000 | tf_op jit(solution)/shard_map/scan_bwd/pallas_call | solution.py:532
  270.1 6.5 %mixer_wgrad.1 = (bf16[512,1920]{1,0:T(8,128)(2,1)S(1)}, bf16[512,1920]{1,0:T(8,128)(2,1)S(1)}) custom-call(s32[1]{0:T(128)} %bitcast.6.refs_0_, bf16[1024,1024]{1,0:T(8,128)(2,1)S(1)} %copy-done.5, bf16[1024,128]{1,0:T(8,128)(2,1)S(1)} %get-tuple-element.116.refs_2_.refs_1_, bf16[1024,128]{1,0:T(8,128)(2,1)S(1)} %get-tuple-element.117.refs_3_.refs_2_, ...), custom_call_target="tpu_custom_call" | custom-call | flops 3000000000 | bytes 10000000 | tf_op jit(solution)/shard_map/mixer_wgrad/pallas_call | solution.py:774
  276.7 5.1 %back_proj.1 = (f32[256,1024]{1,0:T(8,128)S(1)}, bf16[256,1024]{1,0:T(8,128)(2,1)S(1)}, bf16[256,1024]{1,0:T(8,128)(2,1)S(1)}, bf16[256,1024]{1,0:T(8,128)(2,1)S(1)}, f32[8,1024]{1,0:T(8,128)S(1)}) custom-call(s32[1]{0:T(128)} %bitcast.refs_0_, bf16[1024,128]{1,0:T(8,128)(2,1)S(1)} %get-tuple-element.116.refs_2_.refs_1_, ...), custom_call_target="tpu_custom_call" | custom-call | flops 3000000000 | bytes 10000000 | tf_op jit(solution)/shard_map/back_proj/pallas_call | solution.py:827
  281.9 3.5 collective-permute-start.31
  285.4 1.8 collective-permute-start.29
  287.9 9.7 %collective-permute-done.31 = bf16[256,1024]{1,0:T(8,128)(2,1)S(1)} collective-permute-done((bf16[256,1024]{1,0:T(8,128)(2,1)S(1)}, bf16[256,1024]{1,0:T(8,128)(2,1)S(1)}, u32[]{:S(2)}, u32[]{:S(2)}) %collective-permute-start.31) | collective-permute-done | bytes 524320 | tf_op jit(solution)/shard_map/ppermute | solution.py:922
  297.6 10.8 %collective-permute-done.29 = bf16[256,1024]{1,0:T(8,128)(2,1)S(1)} collective-permute-done((bf16[256,1024]{1,0:T(8,128)(2,1)S(1)}, bf16[256,1024]{1,0:T(8,128)(2,1)S(1)}, u32[]{:S(2)}, u32[]{:S(2)}) %collective-permute-start.29) | collective-permute-done | bytes 524320 | tf_op jit(solution)/shard_map/ppermute | solution.py:922
  309.4 1.7 add_convert_fusion
  312.2 2.7 fusion.15
  314.9 5.6 %collective-permute-start.32 = (bf16[256,1024]{1,0:T(8,128)(2,1)}, bf16[256,1024]{1,0:T(8,128)(2,1)S(1)}, u32[]{:S(2)}, u32[]{:S(2)}) collective-permute-start(bf16[256,1024]{1,0:T(8,128)(2,1)} %get-tuple-element.233), channel_id=1, source_target_pairs={{0,1},{1,2},{2,3},{4,5},{5,6},{6,7},{8,9},{9,10},{10,11},{12,13},{... | collective-permute-start | bytes 1572872 | tf_op jit(solution)/shard_map/ppermute | solution.py:922
  322.6 5.3 %collective-permute-start.34 = (bf16[128,1536]{1,0:T(8,128)(2,1)}, bf16[128,1536]{1,0:T(8,128)(2,1)}, u32[]{:S(2)}, u32[]{:S(2)}) collective-permute-start(bf16[128,1536]{1,0:T(8,128)(2,1)} %get-tuple-element.231), channel_id=1, source_target_pairs={{0,1},{3,2},{4,5},{7,6},{8,9},{11,10},{12,13},{15,14},{16,17},{19,... | collective-permute-start | bytes 1179656 | tf_op jit(solution)/shard_map/ppermute | solution.py:922
  329.3 3.3 collective-permute-start.36
  332.6 13.3 %reduce-scatter.5.cloned.1.call-done = bf16[128,1920]{1,0:T(8,128)(2,1)} async-done(((bf16[512,1920]{1,0:T(8,128)(2,1)}), bf16[128,1920]{1,0:T(8,128)(2,1)}) %reduce-scatter.5.cloned.1.call-update) | async-done | bytes 491536 | tf_op jit(solution)/shard_map/reduce_scatter | solution.py:988
  345.9 2.9 collective-permute-done.36
  350.0 1.7 fusion.47
  351.7 2.7 fusion.18
  354.4 7.4 %collective-permute-start.44 = (bf16[128,1536]{1,0:T(8,128)(2,1)}, bf16[128,1536]{1,0:T(8,128)(2,1)}, u32[]{:S(2)}, u32[]{:S(2)}) collective-permute-start(bf16[128,1536]{1,0:T(8,128)(2,1)} %get-tuple-element.228), channel_id=1, source_target_pairs={{0,1},{1,2},{2,3},{4,5},{5,6},{6,7},{8,9},{9,10},{10,11},{12,13},{... | collective-permute-start | bytes 1179656 | tf_op jit(solution)/shard_map/ppermute | solution.py:922
  363.1 1.5 collective-permute-start.39
  371.9 2.7 collective-permute-start.41
  374.6 2.4 collective-permute-start.43
  379.6 3.2 collective-permute-done.42
  (257 shorter events, 53.2 us)
Async XLA Ops:
  7.2 36.8 %copy-start.47 = (f32[384]{0:T(512)S(1)}, f32[384]{0:T(512)}, u32[]{:S(2)}) copy-start(f32[384]{0:T(512)} %param.39) | copy-start | bytes 4612
  7.2 36.8 %copy-start.48 = (f32[256]{0:T(256)S(1)}, f32[256]{0:T(256)}, u32[]{:S(2)}) copy-start(f32[256]{0:T(256)} %param.40) | copy-start | bytes 3076
  7.2 36.8 %copy-start.49 = (f32[6]{0:T(128)S(1)}, f32[6]{0:T(128)}, u32[]{:S(2)}) copy-start(f32[6]{0:T(128)} %param.43) | copy-start | bytes 76
  7.2 37.0 %copy-start.50 = (f32[6]{0:T(128)S(1)}, f32[6]{0:T(128)}, u32[]{:S(2)}) copy-start(f32[6]{0:T(128)} %param.42) | copy-start | bytes 76
  7.2 37.0 %copy-start.51 = (f32[6]{0:T(128)S(1)}, f32[6]{0:T(128)}, u32[]{:S(2)}) copy-start(f32[6]{0:T(128)} %param.41) | copy-start | bytes 76
  7.2 37.0 %copy-start.45 = (f32[4,384]{1,0:T(4,128)S(1)}, f32[4,384]{1,0:T(4,128)}, u32[]{:S(2)}) copy-start(f32[4,384]{1,0:T(4,128)} %param.37) | copy-start | bytes 18436
  7.3 37.0 %copy-start.46 = (f32[4,256]{1,0:T(4,128)S(1)}, f32[4,256]{1,0:T(4,128)}, u32[]{:S(2)}) copy-start(f32[4,256]{1,0:T(4,128)} %param.38) | copy-start | bytes 12292
  7.3 37.0 %copy-start.43 = (s32[1,1024]{1,0:T(1,128)S(1)}, s32[1,1024]{1,0:T(1,128)}, u32[]{:S(2)}) copy-start(s32[1,1024]{1,0:T(1,128)} %param.28) | copy-start | bytes 12292
  7.3 42.1 %all-gather.3.cloned.1.call-start = ((), (), s32[]{:S(2)}) async-start(), calls=%async_computation.2 | async-start | bytes 4423680 | tf_op jit(solution)/shard_map/all_gather | solution.py:1067
  10.9 159.6 %all-gather.5.cloned.1.call-start = ((), (), s32[]{:S(2)}) async-start(), calls=%async_computation.3 | async-start | bytes 14155776 | tf_op jit(solution)/shard_map/all_gather | solution.py:1099
  11.0 28.9 %collective-permute-start.2 = (bf16[256,1024]{1,0:T(8,128)(2,1)}, bf16[256,1024]{1,0:T(8,128)(2,1)S(1)}, u32[]{:S(2)}, u32[]{:S(2)}) collective-permute-start(bf16[256,1024]{1,0:T(8,128)(2,1)} %refs_1_.2), channel_id=1, source_target_pairs={{0,1},{1,2},{2,3},{4,5},{5,6},{6,7},{8,9},{9,10},{10,11},{12,13},{... | collective-permute-start | bytes 1572872 | tf_op jit(solution)/shard_map/ppermute | solution.py:922
  16.0 24.0 %collective-permute-start.3 = (bf16[256,1024]{1,0:T(8,128)(2,1)}, bf16[256,1024]{1,0:T(8,128)(2,1)S(1)}, u32[]{:S(2)}, u32[]{:S(2)}) collective-permute-start(bf16[256,1024]{1,0:T(8,128)(2,1)} %refs_1_.2), channel_id=1, source_target_pairs={{1,0},{2,1},{3,2},{5,4},{6,5},{7,6},{9,8},{10,9},{11,10},{13,12},{... | collective-permute-start | bytes 1572872 | tf_op jit(solution)/shard_map/ppermute | solution.py:922
  19.2 16.6 %collective-permute-start = (bf16[128,1536]{1,0:T(8,128)(2,1)}, bf16[128,1536]{1,0:T(8,128)(2,1)S(1)}, u32[]{:S(2)}, u32[]{:S(2)}) collective-permute-start(bf16[128,1536]{1,0:T(8,128)(2,1)} %pack_ffn.1), channel_id=1, source_target_pairs={{0,1},{1,2},{2,3},{4,5},{5,6},{6,7},{8,9},{9,10},{10,11},{12,13},{... | collective-permute-start | bytes 1179656 | tf_op jit(solution)/shard_map/ppermute | solution.py:922
  23.8 16.1 %collective-permute-start.1 = (bf16[128,1536]{1,0:T(8,128)(2,1)}, bf16[128,1536]{1,0:T(8,128)(2,1)S(1)}, u32[]{:S(2)}, u32[]{:S(2)}) collective-permute-start(bf16[128,1536]{1,0:T(8,128)(2,1)} %pack_ffn.1), channel_id=1, source_target_pairs={{1,0},{2,1},{3,2},{5,4},{6,5},{7,6},{9,8},{10,9},{11,10},{13,12},{... | collective-permute-start | bytes 1179656 | tf_op jit(solution)/shard_map/ppermute | solution.py:922
  39.9 32.1 %copy-start.33 = (bf16[256,1024]{1,0:T(8,128)(2,1)}, bf16[256,1024]{1,0:T(8,128)(2,1)S(1)}, u32[]{:S(2)}) copy-start(bf16[256,1024]{1,0:T(8,128)(2,1)S(1)} %collective-permute-done.2.refs_2_) | copy-start | bytes 1572868
  39.9 32.1 %copy-start.34 = (bf16[256,1024]{1,0:T(8,128)(2,1)}, bf16[256,1024]{1,0:T(8,128)(2,1)S(1)}, u32[]{:S(2)}) copy-start(bf16[256,1024]{1,0:T(8,128)(2,1)S(1)} %collective-permute-done.3.refs_7_) | copy-start | bytes 1572868
  39.9 17.7 %collective-permute-start.4 = (bf16[256,1024]{1,0:T(8,128)(2,1)S(1)}, bf16[256,1024]{1,0:T(8,128)(2,1)S(1)}, u32[]{:S(2)}, u32[]{:S(2)}) collective-permute-start(bf16[256,1024]{1,0:T(8,128)(2,1)S(1)} %collective-permute-done.3.refs_7_), channel_id=1, source_target_pairs={{2,0},{6,4},{10,8},{14,12},{18,16},{22,20},{26,24},{30,28}} | collective-permute-start | bytes 1572872 | tf_op jit(solution)/shard_map/ppermute | solution.py:922
  41.2 16.4 %collective-permute-start.5 = (bf16[256,1024]{1,0:T(8,128)(2,1)S(1)}, bf16[256,1024]{1,0:T(8,128)(2,1)S(1)}, u32[]{:S(2)}, u32[]{:S(2)}) collective-permute-start(bf16[256,1024]{1,0:T(8,128)(2,1)S(1)} %collective-permute-done.2.refs_2_), channel_id=1, source_target_pairs={{1,2},{2,3},{5,6},{6,7},{9,10},{10,11},{13,14},{14,15},{17,18},{18... | collective-permute-start | bytes 1572872 | tf_op jit(solution)/shard_map/ppermute | solution.py:922
  42.0 24.6 %collective-permute-start.6 = (bf16[256,1024]{1,0:T(8,128)(2,1)S(1)}, bf16[256,1024]{1,0:T(8,128)(2,1)S(1)}, u32[]{:S(2)}, u32[]{:S(2)}) collective-permute-start(bf16[256,1024]{1,0:T(8,128)(2,1)S(1)} %collective-permute-done.3.refs_7_), channel_id=1, source_target_pairs={{2,1},{1,0},{6,5},{5,4},{10,9},{9,8},{14,13},{13,12},{18,17},{17,1... | collective-permute-start | bytes 1572872 | tf_op jit(solution)/shard_map/ppermute | solution.py:922
  43.3 23.3 %collective-permute-start.7 = (bf16[256,1024]{1,0:T(8,128)(2,1)S(1)}, bf16[256,1024]{1,0:T(8,128)(2,1)S(1)}, u32[]{:S(2)}, u32[]{:S(2)}) collective-permute-start(bf16[256,1024]{1,0:T(8,128)(2,1)S(1)} %collective-permute-done.2.refs_2_), channel_id=1, source_target_pairs={{1,3},{5,7},{9,11},{13,15},{17,19},{21,23},{25,27},{29,31}} | collective-permute-start | bytes 1572872 | tf_op jit(solution)/shard_map/ppermute | solution.py:922
  66.6 23.5 %collective-permute-start.16 = (bf16[128,1536]{1,0:T(8,128)(2,1)}, bf16[128,1536]{1,0:T(8,128)(2,1)}, u32[]{:S(2)}, u32[]{:S(2)}) collective-permute-start(bf16[128,1536]{1,0:T(8,128)(2,1)} %copy-done.41), channel_id=1, source_target_pairs={{2,0},{6,4},{10,8},{14,12},{18,16},{22,20},{26,24},{30,28}} | collective-permute-start | bytes 1179656 | tf_op jit(solution)/shard_map/ppermute | solution.py:922
  67.9 22.2 %collective-permute-start.18 = (bf16[128,1536]{1,0:T(8,128)(2,1)}, bf16[128,1536]{1,0:T(8,128)(2,1)}, u32[]{:S(2)}, u32[]{:S(2)}) collective-permute-start(bf16[128,1536]{1,0:T(8,128)(2,1)} %copy-done.41), channel_id=1, source_target_pairs={{2,1},{1,0},{6,5},{5,4},{10,9},{9,8},{14,13},{13,12},{18,17},{17,1... | collective-permute-start | bytes 1179656 | tf_op jit(solution)/shard_map/ppermute | solution.py:922
  69.2 20.9 %collective-permute-start.17 = (bf16[128,1536]{1,0:T(8,128)(2,1)}, bf16[128,1536]{1,0:T(8,128)(2,1)}, u32[]{:S(2)}, u32[]{:S(2)}) collective-permute-start(bf16[128,1536]{1,0:T(8,128)(2,1)} %copy-done.39), channel_id=1, source_target_pairs={{1,2},{2,3},{5,6},{6,7},{9,10},{10,11},{13,14},{14,15},{17,18},{18... | collective-permute-start | bytes 1179656 | tf_op jit(solution)/shard_map/ppermute | solution.py:922
  70.6 19.5 %collective-permute-start.19 = (bf16[128,1536]{1,0:T(8,128)(2,1)}, bf16[128,1536]{1,0:T(8,128)(2,1)}, u32[]{:S(2)}, u32[]{:S(2)}) collective-permute-start(bf16[128,1536]{1,0:T(8,128)(2,1)} %copy-done.39), channel_id=1, source_target_pairs={{1,3},{5,7},{9,11},{13,15},{17,19},{21,23},{25,27},{29,31}} | collective-permute-start | bytes 1179656 | tf_op jit(solution)/shard_map/ppermute | solution.py:922
  94.2 217.3 %reduce-scatter.3.cloned.1.call-start = ((), (), s32[]{:S(2)}) async-start(), calls=%async_computation.4 | async-start | bytes 14155776 | tf_op jit(solution)/shard_map/reduce_scatter | solution.py:1109
  94.3 15.5 %collective-permute-start.10 = (f32[1,1024]{1,0:T(1,128)S(1)}, f32[1,1024]{1,0:T(1,128)S(1)}, u32[]{:S(2)}, u32[]{:S(2)}) collective-permute-start(f32[1,1024]{1,0:T(1,128)S(1)} %slice.170), channel_id=1, source_target_pairs={{0,3},{1,0},{2,1},{3,2},{4,7},{5,4},{6,5},{7,6},{8,11},{9,8},{10,9... | collective-permute-start | bytes 12296 | tf_op jit(solution)/shard_map/ppermute | solution.py:918
  99.3 10.5 %collective-permute-start.8 = (f32[1,1024]{1,0:T(1,128)S(1)}, f32[1,1024]{1,0:T(1,128)S(1)}, u32[]{:S(2)}, u32[]{:S(2)}) collective-permute-start(f32[1,1024]{1,0:T(1,128)S(1)} %slice.170), channel_id=1, source_target_pairs={{0,1},{1,2},{2,3},{3,0},{4,5},{5,6},{6,7},{7,4},{8,9},{9,10},{10,1... | collective-permute-start | bytes 12296 | tf_op jit(solution)/shard_map/ppermute | solution.py:918
  101.1 8.7 %collective-permute-start.9 = (f32[1,1024]{1,0:T(1,128)S(1)}, f32[1,1024]{1,0:T(1,128)S(1)}, u32[]{:S(2)}, u32[]{:S(2)}) collective-permute-start(f32[1,1024]{1,0:T(1,128)S(1)} %slice.170), channel_id=1, source_target_pairs={{0,2},{1,3},{2,0},{3,1},{4,6},{5,7},{6,4},{7,5},{8,10},{9,11},{10,... | collective-permute-start | bytes 12296 | tf_op jit(solution)/shard_map/ppermute | solution.py:918
  112.4 15.9 %collective-permute-start.13 = (bf16[256,1024]{1,0:T(8,128)(2,1)}, bf16[256,1024]{1,0:T(8,128)(2,1)S(1)}, u32[]{:S(2)}, u32[]{:S(2)}) collective-permute-start(bf16[256,1024]{1,0:T(8,128)(2,1)} %get-tuple-element.257), channel_id=1, source_target_pairs={{0,2},{3,1},{4,6},{7,5},{8,10},{11,9},{12,14},{15,13},{16,18},{19,... | collective-permute-start | bytes 1572872 | tf_op jit(solution)/shard_map/ppermute | solution.py:922
  116.9 20.5 %collective-permute-start.11 = (bf16[256,1024]{1,0:T(8,128)(2,1)}, bf16[256,1024]{1,0:T(8,128)(2,1)}, u32[]{:S(2)}, u32[]{:S(2)}) collective-permute-start(bf16[256,1024]{1,0:T(8,128)(2,1)} %convolution_convert_fusion), channel_id=1, source_target_pairs={{0,1},{3,2},{4,5},{7,6},{8,9},{11,10},{12,13},{15,14},{16,17},{19,... | collective-permute-start | bytes 1572872 | tf_op jit(solution)/shard_map/ppermute | solution.py:922
  119.0 18.4 %collective-permute-start.12 = (bf16[256,1024]{1,0:T(8,128)(2,1)}, bf16[256,1024]{1,0:T(8,128)(2,1)}, u32[]{:S(2)}, u32[]{:S(2)}) collective-permute-start(bf16[256,1024]{1,0:T(8,128)(2,1)} %convolution_convert_fusion), channel_id=1, source_target_pairs={{1,2},{2,1},{5,6},{6,5},{9,10},{10,9},{13,14},{14,13},{17,18},{18,... | collective-permute-start | bytes 1572872 | tf_op jit(solution)/shard_map/ppermute | solution.py:922
  140.7 16.1 %collective-permute-start.14 = (bf16[256,1024]{1,0:T(8,128)(2,1)}, bf16[256,1024]{1,0:T(8,128)(2,1)}, u32[]{:S(2)}, u32[]{:S(2)}) collective-permute-start(bf16[256,1024]{1,0:T(8,128)(2,1)} %get-tuple-element.234), channel_id=1, source_target_pairs={{0,1},{1,2},{2,3},{4,5},{5,6},{6,7},{8,9},{9,10},{10,11},{12,13},{... | collective-permute-start | bytes 1572872 | tf_op jit(solution)/shard_map/ppermute | solution.py:922
  146.1 15.7 %collective-permute-start.15 = (bf16[256,1024]{1,0:T(8,128)(2,1)}, bf16[256,1024]{1,0:T(8,128)(2,1)}, u32[]{:S(2)}, u32[]{:S(2)}) collective-permute-start(bf16[256,1024]{1,0:T(8,128)(2,1)} %get-tuple-element.235), channel_id=1, source_target_pairs={{3,2},{2,1},{1,0},{7,6},{6,5},{5,4},{11,10},{10,9},{9,8},{15,14},{... | collective-permute-start | bytes 1572872 | tf_op jit(solution)/shard_map/ppermute | solution.py:922
  188.4 157.6 %reduce-scatter.5.cloned.1.call-start = ((), (), s32[]{:S(2)}) async-start(), calls=%async_computation.5 | async-start | bytes 2457600 | tf_op jit(solution)/shard_map/reduce_scatter | solution.py:988
  189.4 16.1 %collective-permute-start.21 = (bf16[256,1024]{1,0:T(8,128)(2,1)S(1)}, bf16[256,1024]{1,0:T(8,128)(2,1)}, u32[]{:S(2)}, u32[]{:S(2)}) collective-permute-start(bf16[256,1024]{1,0:T(8,128)(2,1)S(1)} %copy-done.11), channel_id=1, source_target_pairs={{1,0},{2,1},{3,2},{5,4},{6,5},{7,6},{9,8},{10,9},{11,10},{13,12},{... | collective-permute-start | bytes 1572872 | tf_op jit(solution)/shard_map/ppermute | solution.py:922
  190.7 16.1 %collective-permute-start.20 = (bf16[256,1024]{1,0:T(8,128)(2,1)S(1)}, bf16[256,1024]{1,0:T(8,128)(2,1)}, u32[]{:S(2)}, u32[]{:S(2)}) collective-permute-start(bf16[256,1024]{1,0:T(8,128)(2,1)S(1)} %copy-done.11), channel_id=1, source_target_pairs={{0,1},{1,2},{2,3},{4,5},{5,6},{6,7},{8,9},{9,10},{10,11},{12,13},{... | collective-permute-start | bytes 1572872 | tf_op jit(solution)/shard_map/ppermute | solution.py:922
  205.5 18.0 %collective-permute-start.22 = (bf16[256,1024]{1,0:T(8,128)(2,1)}, bf16[256,1024]{1,0:T(8,128)(2,1)}, u32[]{:S(2)}, u32[]{:S(2)}) collective-permute-start(bf16[256,1024]{1,0:T(8,128)(2,1)} %collective-permute-done.21.refs_7_), channel_id=1, source_target_pairs={{2,0},{6,4},{10,8},{14,12},{18,16},{22,20},{26,24},{30,28}} | collective-permute-start | bytes 1572872 | tf_op jit(solution)/shard_map/ppermute | solution.py:922
  206.8 16.7 %collective-permute-start.23 = (bf16[256,1024]{1,0:T(8,128)(2,1)}, bf16[256,1024]{1,0:T(8,128)(2,1)}, u32[]{:S(2)}, u32[]{:S(2)}) collective-permute-start(bf16[256,1024]{1,0:T(8,128)(2,1)} %collective-permute-done.20.refs_2_), channel_id=1, source_target_pairs={{1,2},{2,3},{5,6},{6,7},{9,10},{10,11},{13,14},{14,15},{17,18},{18... | collective-permute-start | bytes 1572872 | tf_op jit(solution)/shard_map/ppermute | solution.py:922
  208.3 24.8 %collective-permute-start.24 = (bf16[256,1024]{1,0:T(8,128)(2,1)}, bf16[256,1024]{1,0:T(8,128)(2,1)}, u32[]{:S(2)}, u32[]{:S(2)}) collective-permute-start(bf16[256,1024]{1,0:T(8,128)(2,1)} %collective-permute-done.21.refs_7_), channel_id=1, source_target_pairs={{2,1},{1,0},{6,5},{5,4},{10,9},{9,8},{14,13},{13,12},{18,17},{17,1... | collective-permute-start | bytes 1572872 | tf_op jit(solution)/shard_map/ppermute | solution.py:922
  209.5 23.6 %collective-permute-start.25 = (bf16[256,1024]{1,0:T(8,128)(2,1)}, bf16[256,1024]{1,0:T(8,128)(2,1)}, u32[]{:S(2)}, u32[]{:S(2)}) collective-permute-start(bf16[256,1024]{1,0:T(8,128)(2,1)} %collective-permute-done.20.refs_2_), channel_id=1, source_target_pairs={{1,3},{5,7},{9,11},{13,15},{17,19},{21,23},{25,27},{29,31}} | collective-permute-start | bytes 1572872 | tf_op jit(solution)/shard_map/ppermute | solution.py:922
  213.8 30.7 %copy-start.10 = (f32[1024,128]{1,0:T(8,128)S(1)}, f32[1024,128]{1,0:T(8,128)}, u32[]{:S(2)}) copy-start(f32[1024,128]{1,0:T(8,128)} %copy-done.9) | copy-start | bytes 1572868
  213.8 30.7 %copy-start.13 = (bf16[1024,128]{1,0:T(8,128)(2,1)S(1)}, bf16[1024,128]{1,0:T(8,128)(2,1)}, u32[]{:S(2)}) copy-start(bf16[1024,128]{1,0:T(8,128)(2,1)} %copy-done.12) | copy-start | bytes 786436
  213.9 30.7 %copy-start.15 = (bf16[1024,128]{1,0:T(8,128)(2,1)S(1)}, bf16[1024,128]{1,0:T(8,128)(2,1)}, u32[]{:S(2)}) copy-start(bf16[1024,128]{1,0:T(8,128)(2,1)} %copy-done.14) | copy-start | bytes 786436
  238.9 12.3 %collective-permute-start.26 = (f32[1,1024]{1,0:T(1,128)S(1)}, f32[1,1024]{1,0:T(1,128)S(1)}, u32[]{:S(2)}, u32[]{:S(2)}) collective-permute-start(f32[1,1024]{1,0:T(1,128)S(1)} %slice.172), channel_id=1, source_target_pairs={{0,1},{1,2},{2,3},{3,0},{4,5},{5,6},{6,7},{7,4},{8,9},{9,10},{10,1... | collective-permute-start | bytes 12296 | tf_op jit(solution)/shard_map/ppermute | solution.py:918
  241.2 10.0 %collective-permute-start.27 = (f32[1,1024]{1,0:T(1,128)S(1)}, f32[1,1024]{1,0:T(1,128)S(1)}, u32[]{:S(2)}, u32[]{:S(2)}) collective-permute-start(f32[1,1024]{1,0:T(1,128)S(1)} %slice.172), channel_id=1, source_target_pairs={{0,2},{1,3},{2,0},{3,1},{4,6},{5,7},{6,4},{7,5},{8,10},{9,11},{10,... | collective-permute-start | bytes 12296 | tf_op jit(solution)/shard_map/ppermute | solution.py:918
  244.6 6.7 %collective-permute-start.28 = (f32[1,1024]{1,0:T(1,128)S(1)}, f32[1,1024]{1,0:T(1,128)S(1)}, u32[]{:S(2)}, u32[]{:S(2)}) collective-permute-start(f32[1,1024]{1,0:T(1,128)S(1)} %slice.172), channel_id=1, source_target_pairs={{0,3},{1,0},{2,1},{3,2},{4,7},{5,4},{6,5},{7,6},{8,11},{9,8},{10,9... | collective-permute-start | bytes 12296 | tf_op jit(solution)/shard_map/ppermute | solution.py:918
  276.6 31.8 %collective-permute-start.37 = (bf16[512,1920]{1,0:T(8,128)(2,1)S(1)}, bf16[512,1920]{1,0:T(8,128)(2,1)S(1)}, u32[]{:S(2)}, u32[]{:S(2)}) collective-permute-start(bf16[512,1920]{1,0:T(8,128)(2,1)S(1)} %get-tuple-element.124), channel_id=1, source_target_pairs={{0,4},{4,0},{8,12},{12,8},{16,20},{20,16},{24,28},{28,24},{1,5},{5... | collective-permute-start | bytes 5898248 | tf_op jit(solution)/shard_map/ppermute | solution.py:981
  281.9 15.7 %collective-permute-start.31 = (bf16[256,1024]{1,0:T(8,128)(2,1)S(1)}, bf16[256,1024]{1,0:T(8,128)(2,1)S(1)}, u32[]{:S(2)}, u32[]{:S(2)}) collective-permute-start(bf16[256,1024]{1,0:T(8,128)(2,1)S(1)} %broadcast_select_fusion), channel_id=1, source_target_pairs={{0,2},{3,1},{4,6},{7,5},{8,10},{11,9},{12,14},{15,13},{16,18},{19,... | collective-permute-start | bytes 1572872 | tf_op jit(solution)/shard_map/ppermute | solution.py:922
  285.4 23.0 %collective-permute-start.29 = (bf16[256,1024]{1,0:T(8,128)(2,1)S(1)}, bf16[256,1024]{1,0:T(8,128)(2,1)S(1)}, u32[]{:S(2)}, u32[]{:S(2)}) collective-permute-start(bf16[256,1024]{1,0:T(8,128)(2,1)S(1)} %get-tuple-element.129), channel_id=1, source_target_pairs={{0,1},{3,2},{4,5},{7,6},{8,9},{11,10},{12,13},{15,14},{16,17},{19,... | collective-permute-start | bytes 1572872 | tf_op jit(solution)/shard_map/ppermute | solution.py:922
  287.2 21.3 %collective-permute-start.30 = (bf16[256,1024]{1,0:T(8,128)(2,1)S(1)}, bf16[256,1024]{1,0:T(8,128)(2,1)S(1)}, u32[]{:S(2)}, u32[]{:S(2)}) collective-permute-start(bf16[256,1024]{1,0:T(8,128)(2,1)S(1)} %get-tuple-element.129), channel_id=1, source_target_pairs={{1,2},{2,1},{5,6},{6,5},{9,10},{10,9},{13,14},{14,13},{17,18},{18,... | collective-permute-start | bytes 1572872 | tf_op jit(solution)/shard_map/ppermute | solution.py:922
  311.4 17.9 %collective-permute-start.38 = (f32[16,1024]{1,0:T(8,128)S(1)}, f32[16,1024]{1,0:T(8,128)S(1)}, u32[]{:S(2)}, u32[]{:S(2)}) collective-permute-start(f32[16,1024]{1,0:T(8,128)S(1)} %concatenate.36), channel_id=1, source_target_pairs={{0,4},{4,0},{8,12},{12,8},{16,20},{20,16},{24,28},{28,24},{1,5},{5... | collective-permute-start | bytes 196616 | tf_op jit(solution)/shard_map/ppermute | solution.py:1144
  314.9 34.0 %collective-permute-start.32 = (bf16[256,1024]{1,0:T(8,128)(2,1)}, bf16[256,1024]{1,0:T(8,128)(2,1)S(1)}, u32[]{:S(2)}, u32[]{:S(2)}) collective-permute-start(bf16[256,1024]{1,0:T(8,128)(2,1)} %get-tuple-element.233), channel_id=1, source_target_pairs={{0,1},{1,2},{2,3},{4,5},{5,6},{6,7},{8,9},{9,10},{10,11},{12,13},{... | collective-permute-start | bytes 1572872 | tf_op jit(solution)/shard_map/ppermute | solution.py:922
  320.5 28.4 %collective-permute-start.33 = (bf16[256,1024]{1,0:T(8,128)(2,1)}, bf16[256,1024]{1,0:T(8,128)(2,1)S(1)}, u32[]{:S(2)}, u32[]{:S(2)}) collective-permute-start(bf16[256,1024]{1,0:T(8,128)(2,1)} %get-tuple-element.232), channel_id=1, source_target_pairs={{3,2},{2,1},{1,0},{7,6},{6,5},{5,4},{11,10},{10,9},{9,8},{15,14},{... | collective-permute-start | bytes 1572872 | tf_op jit(solution)/shard_map/ppermute | solution.py:922
  322.6 23.3 %collective-permute-start.34 = (bf16[128,1536]{1,0:T(8,128)(2,1)}, bf16[128,1536]{1,0:T(8,128)(2,1)}, u32[]{:S(2)}, u32[]{:S(2)}) collective-permute-start(bf16[128,1536]{1,0:T(8,128)(2,1)} %get-tuple-element.231), channel_id=1, source_target_pairs={{0,1},{3,2},{4,5},{7,6},{8,9},{11,10},{12,13},{15,14},{16,17},{19,... | collective-permute-start | bytes 1179656 | tf_op jit(solution)/shard_map/ppermute | solution.py:922
  327.9 18.1 %collective-permute-start.35 = (bf16[128,1536]{1,0:T(8,128)(2,1)}, bf16[128,1536]{1,0:T(8,128)(2,1)}, u32[]{:S(2)}, u32[]{:S(2)}) collective-permute-start(bf16[128,1536]{1,0:T(8,128)(2,1)} %get-tuple-element.231), channel_id=1, source_target_pairs={{1,2},{2,1},{5,6},{6,5},{9,10},{10,9},{13,14},{14,13},{17,18},{18,... | collective-permute-start | bytes 1179656 | tf_op jit(solution)/shard_map/ppermute | solution.py:922
  329.3 19.6 %collective-permute-start.36 = (bf16[128,1536]{1,0:T(8,128)(2,1)S(1)}, bf16[128,1536]{1,0:T(8,128)(2,1)}, u32[]{:S(2)}, u32[]{:S(2)}) collective-permute-start(bf16[128,1536]{1,0:T(8,128)(2,1)S(1)} %get-tuple-element.230), channel_id=1, source_target_pairs={{0,2},{3,1},{4,6},{7,5},{8,10},{11,9},{12,14},{15,13},{16,18},{19,... | collective-permute-start | bytes 1179656 | tf_op jit(solution)/shard_map/ppermute | solution.py:922
  332.6 32.0 %copy-start.25 = (bf16[256,1024]{1,0:T(8,128)(2,1)S(1)}, bf16[256,1024]{1,0:T(8,128)(2,1)}, u32[]{:S(2)}) copy-start(bf16[256,1024]{1,0:T(8,128)(2,1)} %refs_1_.2) | copy-start | bytes 1572868
  354.4 31.9 %collective-permute-start.44 = (bf16[128,1536]{1,0:T(8,128)(2,1)}, bf16[128,1536]{1,0:T(8,128)(2,1)}, u32[]{:S(2)}, u32[]{:S(2)}) collective-permute-start(bf16[128,1536]{1,0:T(8,128)(2,1)} %get-tuple-element.228), channel_id=1, source_target_pairs={{0,1},{1,2},{2,3},{4,5},{5,6},{6,7},{8,9},{9,10},{10,11},{12,13},{... | collective-permute-start | bytes 1179656 | tf_op jit(solution)/shard_map/ppermute | solution.py:922
  361.9 24.5 %collective-permute-start.45 = (bf16[128,1536]{1,0:T(8,128)(2,1)}, bf16[128,1536]{1,0:T(8,128)(2,1)}, u32[]{:S(2)}, u32[]{:S(2)}) collective-permute-start(bf16[128,1536]{1,0:T(8,128)(2,1)} %get-tuple-element.229), channel_id=1, source_target_pairs={{3,2},{2,1},{1,0},{7,6},{6,5},{5,4},{11,10},{10,9},{9,8},{15,14},{... | collective-permute-start | bytes 1179656 | tf_op jit(solution)/shard_map/ppermute | solution.py:922
  363.1 4.3 %collective-permute-start.39 = (f32[16,1024]{1,0:T(8,128)S(1)}, f32[16,1024]{1,0:T(8,128)S(1)}, u32[]{:S(2)}, u32[]{:S(2)}) collective-permute-start(f32[16,1024]{1,0:T(8,128)S(1)} %add.217), channel_id=1, source_target_pairs={{0,8},{4,12},{8,0},{12,4},{16,24},{20,28},{24,16},{28,20},{1,9},{5... | collective-permute-start | bytes 196616 | tf_op jit(solution)/shard_map/ppermute | solution.py:1005
  367.5 4.3 %collective-permute-start.40 = (f32[16,1024]{1,0:T(8,128)S(1)}, f32[16,1024]{1,0:T(8,128)S(1)}, u32[]{:S(2)}, u32[]{:S(2)}) collective-permute-start(f32[16,1024]{1,0:T(8,128)S(1)} %add.218), channel_id=1, source_target_pairs={{0,16},{4,20},{8,24},{12,28},{16,0},{20,4},{24,8},{28,12},{1,17},{... | collective-permute-start | bytes 196616 | tf_op jit(solution)/shard_map/ppermute | solution.py:1005
  371.9 7.6 %collective-permute-start.41 = (bf16[128,512]{1,0:T(8,128)(2,1)S(1)}, bf16[128,512]{1,0:T(8,128)(2,1)S(1)}, u32[]{:S(2)}, u32[]{:S(2)}) collective-permute-start(bf16[128,512]{1,0:T(8,128)(2,1)S(1)} %get-tuple-element.248), channel_id=1, source_target_pairs={{0,1},{1,2},{2,3},{3,0},{4,5},{5,6},{6,7},{7,4},{8,9},{9,10},{10,1... | collective-permute-start | bytes 393224 | tf_op jit(solution)/shard_map/ppermute | solution.py:918
  374.6 8.2 %collective-permute-start.42 = (bf16[128,512]{1,0:T(8,128)(2,1)S(1)}, bf16[128,512]{1,0:T(8,128)(2,1)S(1)}, u32[]{:S(2)}, u32[]{:S(2)}) collective-permute-start(bf16[128,512]{1,0:T(8,128)(2,1)S(1)} %get-tuple-element.248), channel_id=1, source_target_pairs={{0,2},{1,3},{2,0},{3,1},{4,6},{5,7},{6,4},{7,5},{8,10},{9,11},{10,... | collective-permute-start | bytes 393224 | tf_op jit(solution)/shard_map/ppermute | solution.py:918
  374.6 8.2 %collective-permute-start.43 = (bf16[128,512]{1,0:T(8,128)(2,1)S(1)}, bf16[128,512]{1,0:T(8,128)(2,1)S(1)}, u32[]{:S(2)}, u32[]{:S(2)}) collective-permute-start(bf16[128,512]{1,0:T(8,128)(2,1)S(1)} %get-tuple-element.248), channel_id=1, source_target_pairs={{0,3},{1,0},{2,1},{3,2},{4,7},{5,4},{6,5},{7,6},{8,11},{9,8},{10,9... | collective-permute-start | bytes 393224 | tf_op jit(solution)/shard_map/ppermute | solution.py:918
  (42 other events, 317.2 us)
Sparse Core Ops, SparseCore 0:
  11.1 38.3 all-gather.2
  94.4 76.1 all-gather.4
  188.5 92.3 reduce-scatter.2
  311.3 34.6 reduce-scatter.4

commit v3 on v1

--- a/solution.py
+++ b/solution.py
@@ -1057,8 +1057,8 @@
     gain_one = mixer_w[:, dat + HD].astype(F32)[None, :]
     gain_two = mixer_w[:, dat + HD + 1].astype(F32)[None, :]
     ffn_own = pack_ffn(w_gate, w_up, w_down)
-    ffn_first, x_first = lax.optimization_barrier((first_phase(ffn_own, parts), first_phase(x_in, parts)))
-    x_pieces = second_phase(x_in, x_first, parts)
+    ffn_first, x_first = first_phase(ffn_own, parts), first_phase(x_in, parts)
+    x_pieces = after(second_phase(x_in, x_first, parts), gain_one, gain_two)
     ffn_pieces = second_phase(ffn_own, after(ffn_first, x_pieces), parts)
 
     seg = segments[0]

time: 399 us -> 396 us (level)
  waiting for transfers between devices: 129 us -> 117 us
  starting transfers between devices: 100 us -> 109 us
    ppermute x33, waiting for transfers between devices: 116 us -> 103 us  [sent(): return lax.ppermute(values, 'tensor', pairs)]
    ppermute x33, starting transfers between devices: 76.6 us -> 82.9 us  [sent(): return lax.ppermute(values, 'tensor', pairs)]
    unnamed x115 -> x107, local copies, waits for them, and re-layouts: 10.3 us -> 9.98 us
  transfers between devices with their start and end apart: 50 -> 50, of which waited for: 18 -> 19; matrix products, arithmetic and copies ran while one was open for 13% -> 13% of each run, Pallas kernels for 16% -> 16%
where the time goes in v3:
time: 396 us; the launch traced here: 388 us
  waiting for transfers between devices  117 us (30%)
  starting transfers between devices  109 us (28%)
  Pallas kernels  81.4 us (21%)
  other arithmetic  33.8 us (9%)
  local copies, waits for them, and re-layouts  22.1 us (6%)
  between operations  15.4 us (4%)
  matrix products  10.1 us (3%)
    ppermute x33, waiting for transfers between devices, sent(): return lax.ppermute(values, 'tensor', pairs)  103 us
    ppermute x33, starting transfers between devices, sent(): return lax.ppermute(values, 'tensor', pairs)  82.9 us
    ppermute x9, starting transfers between devices, shifted(): lax.ppermute(values, axis, [(i, (i + shift) % size) for i in range(size)])  22.8 us
    pallas_call x1, Pallas kernels, scan_backward(): pl.pallas_call(body, grid=(blocks,), in_specs=[pl.BlockSpec((BLOCK, width...  18.8 us
    pallas_call x1, Pallas kernels, ffn_both(): pl.pallas_call(ffn_kernel, grid=(parts,), in_specs=[rowspec, rowspec, pl....  17.4 us
    unnamed x107, local copies, waits for them, and re-layouts  9.98 us
    pallas_call x1, Pallas kernels, scan_forward(): pl.pallas_call(body, grid=(blocks,), in_specs=[pl.BlockSpec((BLOCK, width...  8.2 us
  transfers between devices with their start and end apart: 50, of which 19 were waited for; matrix products, arithmetic and copies ran while one was open for 13% of the time, Pallas kernels for 16%

profile of v3, /device:TPU:0, one launch (start us, length us, event | category | flops | bytes accessed | tf_op | source)
XLA Modules:
  0.0 388.3 jit_solution(7313546908880542125)
XLA Ops:
  8.7 2.2 pack_mixer.1
  12.3 5.6 %collective-permute-start = (bf16[256,1024]{1,0:T(8,128)(2,1)}, bf16[256,1024]{1,0:T(8,128)(2,1)S(1)}, u32[]{:S(2)}, u32[]{:S(2)}) collective-permute-start(bf16[256,1024]{1,0:T(8,128)(2,1)} %refs_1_.2), channel_id=1, source_target_pairs={{0,1},{1,2},{2,3},{4,5},{5,6},{6,7},{8,9},{9,10},{10,11},{12,13},{... | collective-permute-start | bytes 1572872 | tf_op jit(solution)/shard_map/ppermute | solution.py:909
  17.9 10.2 %collective-permute-done.1.refs_7_ = bf16[256,1024]{1,0:T(8,128)(2,1)S(1)} collective-permute-done((bf16[256,1024]{1,0:T(8,128)(2,1)}, bf16[256,1024]{1,0:T(8,128)(2,1)S(1)}, u32[]{:S(2)}, u32[]{:S(2)}) %collective-permute-start.1) | collective-permute-done | bytes 524320 | tf_op jit(solution)/shard_map/ppermute | solution.py:909
  32.1 2.0 pack_ffn.1
  34.1 9.3 %collective-permute-start.14 = (bf16[128,1536]{1,0:T(8,128)(2,1)}, bf16[128,1536]{1,0:T(8,128)(2,1)}, u32[]{:S(2)}, u32[]{:S(2)}) collective-permute-start(bf16[128,1536]{1,0:T(8,128)(2,1)} %pack_ffn.1), channel_id=1, source_target_pairs={{0,1},{1,2},{2,3},{4,5},{5,6},{6,7},{8,9},{9,10},{10,11},{12,13},{... | collective-permute-start | bytes 1179656 | tf_op jit(solution)/shard_map/ppermute | solution.py:909
  43.6 2.1 collective-permute-done.2.refs_3_
  47.7 1.8 all-gather.3.cloned.1.call-done.refs_4_
  49.4 2.1 convert_reduce_fusion.1
  51.5 3.9 %collective-permute-done.4.refs_5_ = bf16[256,1024]{1,0:T(8,128)(2,1)S(1)} collective-permute-done((bf16[256,1024]{1,0:T(8,128)(2,1)S(1)}, bf16[256,1024]{1,0:T(8,128)(2,1)S(1)}, u32[]{:S(2)}, u32[]{:S(2)}) %collective-permute-start.4) | collective-permute-done | bytes 524320 | tf_op jit(solution)/shard_map/ppermute | solution.py:909
  55.4 8.4 %collective-permute-done.15 = bf16[128,1536]{1,0:T(8,128)(2,1)} collective-permute-done((bf16[128,1536]{1,0:T(8,128)(2,1)}, bf16[128,1536]{1,0:T(8,128)(2,1)}, u32[]{:S(2)}, u32[]{:S(2)}) %collective-permute-start.15) | collective-permute-done | bytes 393248 | tf_op jit(solution)/shard_map/ppermute | solution.py:909
  69.3 4.4 %norm_rows.1.refs_1_.refs_5_ = bf16[1024,1024]{1,0:T(8,128)(2,1)} custom-call(s32[1]{0:T(128)} %bitcast.refs_0_, bf16[256,1024]{1,0:T(8,128)(2,1)} %refs_1_.2, bf16[256,1024]{1,0:T(8,128)(2,1)} %copy-done.32, bf16[256,1024]{1,0:T(8,128)(2,1)} %copy-done.33, bf16[256,1024]{1,0:T(8,128)(2,1)} %copy-done.34, bf16[256,1024]{1,0:T(8,128)(2,1)} %copy-done.35, ...), custom_call_target="tpu_custom_call" | custom-call | flops 10000000 | bytes 5000000 | tf_op jit(solution)/shard_map/norm_rows/pallas_call | solution.py:663
  73.7 5.0 %fusion.q_ref.kv_ref.refs_0_.refs_1_ = f32[1024,1408]{1,0:T(8,128)S(1)} fusion(bf16[1024,1024]{1,0:T(8,128)(2,1)} %norm_rows.1.refs_1_.refs_5_, bf16[1024,1920]{1,0:T(8,128)(2,1)S(1)} %copy-done.2), kind=kOutput, calls=%fused_computation.2 | convolution fusion | flops 2952790016 | bytes 10747904 | tf_op jit(solution)/shard_map/dot_general | solution.py:30
  79.0 8.2 %scan_fwd.1 = (f32[1024,384]{1,0:T(8,128)S(1)}, f32[1024,384]{1,0:T(8,128)S(1)}, bf16[8,128,384]{2,1,0:T(8,128)(2,1)S(1)}, f32[8,1024]{1,0:T(8,128)S(1)}) custom-call(f32[1024,1408]{1,0:T(8,128)S(1)} %fusion.q_ref.kv_ref.refs_0_.refs_1_, s32[1024,128]{1,0:T(8,128)S(1)} %broadcast_in_dim.73.start_ref.refs_1_.refs_2_, ...), custom_call_target="tpu_custom_call" | custom-call | flops 2000000000 | bytes 10000000 | tf_op jit(solution)/shard_map/scan_fwd/pallas_call | solution.py:497
  87.3 1.6 broadcast_select_fusion.4
  91.7 7.7 %collective-permute-start.6 = (f32[1,1024]{1,0:T(1,128)S(1)}, f32[1,1024]{1,0:T(1,128)S(1)}, u32[]{:S(2)}, u32[]{:S(2)}) collective-permute-start(f32[1,1024]{1,0:T(1,128)S(1)} %slice.136), channel_id=1, source_target_pairs={{0,1},{1,2},{2,3},{3,0},{4,5},{5,6},{6,7},{7,4},{8,9},{9,10},{10,1... | collective-permute-start | bytes 12296 | tf_op jit(solution)/shard_map/ppermute | solution.py:905
  99.4 2.6 collective-permute-start.8
  102.0 3.3 copy-done.1
  105.3 4.4 %attn_fwd.1 = (bf16[1024,128]{1,0:T(8,128)(2,1)S(1)}, f32[1024,128]{1,0:T(8,128)S(1)}, bf16[1024,128]{1,0:T(8,128)(2,1)S(1)}, bf16[1024,128]{1,0:T(8,128)(2,1)S(1)}) custom-call(f32[1024,1408]{1,0:T(8,128)S(1)} %copy-done.1, f32[1024,1408]{1,0:T(8,128)S(1)} %copy-done.1, f32[1024,128]{1,0:T(8,128)S(1)} %copy-done.7, f32[1024,128]{1,0:T(8,128)S(1)} %copy-done.8, ...), custom_call_target="tpu_custom_call" | custom-call | flops 1000000000 | bytes 6000000 | tf_op jit(solution)/shard_map/attn_fwd/pallas_call | solution.py:165
  110.7 1.6 select_convert_fusion
  112.3 1.8 collective-permute-start.11
  116.0 3.8 collective-permute-start.9
  119.9 6.9 %collective-permute-done.11 = bf16[256,1024]{1,0:T(8,128)(2,1)S(1)} collective-permute-done((bf16[256,1024]{1,0:T(8,128)(2,1)}, bf16[256,1024]{1,0:T(8,128)(2,1)S(1)}, u32[]{:S(2)}, u32[]{:S(2)}) %collective-permute-start.11) | collective-permute-done | bytes 524320 | tf_op jit(solution)/shard_map/ppermute | solution.py:909
  126.8 8.8 %collective-permute-done.9 = bf16[256,1024]{1,0:T(8,128)(2,1)} collective-permute-done((bf16[256,1024]{1,0:T(8,128)(2,1)}, bf16[256,1024]{1,0:T(8,128)(2,1)}, u32[]{:S(2)}, u32[]{:S(2)}) %collective-permute-start.9) | collective-permute-done | bytes 524320 | tf_op jit(solution)/shard_map/ppermute | solution.py:909
  135.6 3.4 fusion.9
  139.0 6.0 %collective-permute-start.12 = (bf16[256,1024]{1,0:T(8,128)(2,1)}, bf16[256,1024]{1,0:T(8,128)(2,1)}, u32[]{:S(2)}, u32[]{:S(2)}) collective-permute-start(bf16[256,1024]{1,0:T(8,128)(2,1)} %get-tuple-element.223), channel_id=1, source_target_pairs={{0,1},{1,2},{2,3},{4,5},{5,6},{6,7},{8,9},{9,10},{10,11},{12,13},{... | collective-permute-start | bytes 1572872 | tf_op jit(solution)/shard_map/ppermute | solution.py:909
  146.3 1.7 fusion.22
  148.0 7.9 %collective-permute-done.12 = bf16[256,1024]{1,0:T(8,128)(2,1)} collective-permute-done((bf16[256,1024]{1,0:T(8,128)(2,1)}, bf16[256,1024]{1,0:T(8,128)(2,1)}, u32[]{:S(2)}, u32[]{:S(2)}) %collective-permute-start.12) | collective-permute-done | bytes 524320 | tf_op jit(solution)/shard_map/ppermute | solution.py:909
  155.9 4.9 %collective-permute-done.13 = bf16[256,1024]{1,0:T(8,128)(2,1)} collective-permute-done((bf16[256,1024]{1,0:T(8,128)(2,1)}, bf16[256,1024]{1,0:T(8,128)(2,1)}, u32[]{:S(2)}, u32[]{:S(2)}) %collective-permute-start.13) | collective-permute-done | bytes 524320 | tf_op jit(solution)/shard_map/ppermute | solution.py:909
  160.8 2.5 fusion.16
  163.3 5.7 %all-gather.5.cloned.1.call-done.w_ref = bf16[1024,6144]{1,0:T(8,128)(2,1)} async-done(((bf16[128,6144]{1,0:T(8,128)(2,1)}), bf16[1024,6144]{1,0:T(8,128)(2,1)}) %all-gather.5.cloned.1.call-update) | async-done | bytes 12582928 | tf_op jit(solution)/shard_map/all_gather | solution.py:1086
  169.0 17.4 %ffn_both.1 = (bf16[256,1024]{1,0:T(8,128)(2,1)}, f32[256,1024]{1,0:T(8,128)}, bf16[256,1024]{1,0:T(8,128)(2,1)}, f32[8,1024]{1,0:T(8,128)}, bf16[1024,6144]{1,0:T(8,128)(2,1)}) custom-call(f32[256,1024]{1,0:T(8,128)} %get-tuple-element.229.middle_ref, bf16[256,1024]{1,0:T(8,128)(2,1)} %cot_ref.1, f32[1,1024]{1,0:T(1,128)} %bitcast.32, ...), custom_call_target="tpu_custom_call" | custom-call | flops 10000000000 | bytes 30000000 | tf_op jit(solution)/shard_map/ffn_both/pallas_call | solution.py:876
  188.7 5.3 %collective-permute-start.20 = (bf16[256,1024]{1,0:T(8,128)(2,1)S(1)}, bf16[256,1024]{1,0:T(8,128)(2,1)}, u32[]{:S(2)}, u32[]{:S(2)}) collective-permute-start(bf16[256,1024]{1,0:T(8,128)(2,1)S(1)} %copy-done.12), channel_id=1, source_target_pairs={{0,1},{1,2},{2,3},{4,5},{5,6},{6,7},{8,9},{9,10},{10,11},{12,13},{... | collective-permute-start | bytes 1572872 | tf_op jit(solution)/shard_map/ppermute | solution.py:909
  194.1 9.4 %collective-permute-done.21.refs_7_ = bf16[256,1024]{1,0:T(8,128)(2,1)} collective-permute-done((bf16[256,1024]{1,0:T(8,128)(2,1)S(1)}, bf16[256,1024]{1,0:T(8,128)(2,1)}, u32[]{:S(2)}, u32[]{:S(2)}) %collective-permute-start.21) | collective-permute-done | bytes 524320 | tf_op jit(solution)/shard_map/ppermute | solution.py:909
  204.8 1.5 collective-permute-start.23
  207.6 1.6 collective-permute-start.25
  211.9 9.6 %collective-permute-done.22.refs_3_ = bf16[256,1024]{1,0:T(8,128)(2,1)} collective-permute-done((bf16[256,1024]{1,0:T(8,128)(2,1)}, bf16[256,1024]{1,0:T(8,128)(2,1)}, u32[]{:S(2)}, u32[]{:S(2)}) %collective-permute-start.22) | collective-permute-done | bytes 524320 | tf_op jit(solution)/shard_map/ppermute | solution.py:909
  221.5 9.6 %collective-permute-done.24.refs_5_ = bf16[256,1024]{1,0:T(8,128)(2,1)} collective-permute-done((bf16[256,1024]{1,0:T(8,128)(2,1)}, bf16[256,1024]{1,0:T(8,128)(2,1)}, u32[]{:S(2)}, u32[]{:S(2)}) %collective-permute-start.24) | collective-permute-done | bytes 524320 | tf_op jit(solution)/shard_map/ppermute | solution.py:909
  231.1 5.8 %branch_back.1 = (bf16[1024,128]{1,0:T(8,128)(2,1)S(1)}, f32[1024,384]{1,0:T(8,128)S(1)}, bf16[1024,512]{1,0:T(8,128)(2,1)S(1)}, f32[8,1024]{1,0:T(8,128)S(1)}, f32[8,384]{1,0:T(8,128)S(1)}) custom-call(s32[1]{0:T(128)} %bitcast.refs_0_, bf16[256,1024]{1,0:T(8,128)(2,1)S(1)} %copy-done.12, bf16[256,1024]{1,0:T(8,128)(2,1)} %collective-permute-done.20.refs_2_, ...), custom_call_target="tpu_custom_call" | custom-call | flops 2000000000 | bytes 10000000 | tf_op jit(solution)/shard_map/branch_back/pallas_call | solution.py:717
  237.0 2.2 collective-permute-start.26
  239.2 3.4 collective-permute-start.27
  242.6 6.6 %attn_bwd.1 = (bf16[1024,128]{1,0:T(8,128)(2,1)S(1)}, bf16[1024,128]{1,0:T(8,128)(2,1)S(1)}) custom-call(bf16[1024,128]{1,0:T(8,128)(2,1)S(1)} %copy-done.14, bf16[1024,128]{1,0:T(8,128)(2,1)S(1)} %copy-done.16, f32[1024,128]{1,0:T(8,128)S(1)} %copy-done.11, bf16[1024,128]{1,0:T(8,128)(2,1)S(1)} %get-tuple-element.89.out_ref, ...), custom_call_target="tpu_custom_call" | custom-call | flops 3000000000 | bytes 6000000 | tf_op jit(solution)/shard_map/attn_bwd/pallas_call | solution.py:185
  249.4 18.8 %scan_bwd.1 = (bf16[1024,1152]{1,0:T(8,128)(2,1)S(1)}, f32[8,640]{1,0:T(8,128)S(1)}, f32[16,128]{1,0:T(8,128)S(1)}, f32[8,384]{1,0:T(8,128)S(1)}) custom-call(f32[1024,1408]{1,0:T(8,128)S(1)} %bitcast.27, f32[1024,1408]{1,0:T(8,128)S(1)} %bitcast.27, s32[1024,128]{1,0:T(8,128)S(1)} %broadcast_in_dim.73.start_ref.refs_1_.refs_2_, ...), custom_call_target="tpu_custom_call" | custom-call | flops 6000000000 | bytes 20000000 | tf_op jit(solution)/shard_map/scan_bwd/pallas_call | solution.py:532
  268.2 6.6 %mixer_wgrad.1 = (bf16[512,1920]{1,0:T(8,128)(2,1)}, bf16[512,1920]{1,0:T(8,128)(2,1)S(1)}) custom-call(s32[1]{0:T(128)} %bitcast.6.refs_0_, bf16[1024,1024]{1,0:T(8,128)(2,1)S(1)} %copy-done.5, bf16[1024,128]{1,0:T(8,128)(2,1)S(1)} %get-tuple-element.108.refs_2_.refs_1_, bf16[1024,128]{1,0:T(8,128)(2,1)S(1)} %get-tuple-element.109.refs_3_.refs_2_, ...), custom_call_target="tpu_custom_call" | custom-call | flops 3000000000 | bytes 10000000 | tf_op jit(solution)/shard_map/mixer_wgrad/pallas_call | solution.py:767
  274.9 5.0 %back_proj.1 = (f32[256,1024]{1,0:T(8,128)S(1)}, bf16[256,1024]{1,0:T(8,128)(2,1)S(1)}, bf16[256,1024]{1,0:T(8,128)(2,1)S(1)}, bf16[256,1024]{1,0:T(8,128)(2,1)S(1)}, f32[8,1024]{1,0:T(8,128)S(1)}) custom-call(s32[1]{0:T(128)} %bitcast.refs_0_, bf16[1024,128]{1,0:T(8,128)(2,1)S(1)} %get-tuple-element.108.refs_2_.refs_1_, ...), custom_call_target="tpu_custom_call" | custom-call | flops 3000000000 | bytes 10000000 | tf_op jit(solution)/shard_map/back_proj/pallas_call | solution.py:819
  281.7 3.9 add_convert_fusion
  285.6 4.7 %collective-permute-start.29 = (bf16[256,1024]{1,0:T(8,128)(2,1)S(1)}, bf16[256,1024]{1,0:T(8,128)(2,1)}, u32[]{:S(2)}, u32[]{:S(2)}) collective-permute-start(bf16[256,1024]{1,0:T(8,128)(2,1)S(1)} %get-tuple-element.121), channel_id=1, source_target_pairs={{0,1},{3,2},{4,5},{7,6},{8,9},{11,10},{12,13},{15,14},{16,17},{19,... | collective-permute-start | bytes 1572872 | tf_op jit(solution)/shard_map/ppermute | solution.py:909
  290.3 1.5 collective-permute-start.30
  291.8 1.6 collective-permute-start.34
  293.4 3.3 collective-permute-start.31
  298.6 4.5 %collective-permute-done.35 = f32[16,1024]{1,0:T(8,128)S(1)} collective-permute-done((f32[16,1024]{1,0:T(8,128)S(1)}, f32[16,1024]{1,0:T(8,128)S(1)}, u32[]{:S(2)}, u32[]{:S(2)}) %collective-permute-start.35) | collective-permute-done | bytes 65568 | tf_op jit(solution)/shard_map/ppermute | solution.py:992
  306.2 6.3 %collective-permute-done.31 = bf16[256,1024]{1,0:T(8,128)(2,1)} collective-permute-done((bf16[256,1024]{1,0:T(8,128)(2,1)S(1)}, bf16[256,1024]{1,0:T(8,128)(2,1)}, u32[]{:S(2)}, u32[]{:S(2)}) %collective-permute-start.31) | collective-permute-done | bytes 524320 | tf_op jit(solution)/shard_map/ppermute | solution.py:909
  312.5 3.0 fusion.15
  315.5 5.9 %collective-permute-start.36 = (bf16[256,1024]{1,0:T(8,128)(2,1)}, bf16[256,1024]{1,0:T(8,128)(2,1)S(1)}, u32[]{:S(2)}, u32[]{:S(2)}) collective-permute-start(bf16[256,1024]{1,0:T(8,128)(2,1)} %get-tuple-element.222), channel_id=1, source_target_pairs={{0,1},{1,2},{2,3},{4,5},{5,6},{6,7},{8,9},{9,10},{10,11},{12,13},{... | collective-permute-start | bytes 1572872 | tf_op jit(solution)/shard_map/ppermute | solution.py:909
  322.8 5.3 %collective-permute-start.38 = (bf16[128,1536]{1,0:T(8,128)(2,1)S(1)}, bf16[128,1536]{1,0:T(8,128)(2,1)}, u32[]{:S(2)}, u32[]{:S(2)}) collective-permute-start(bf16[128,1536]{1,0:T(8,128)(2,1)S(1)} %get-tuple-element.220), channel_id=1, source_target_pairs={{0,1},{3,2},{4,5},{7,6},{8,9},{11,10},{12,13},{15,14},{16,17},{19,... | collective-permute-start | bytes 1179656 | tf_op jit(solution)/shard_map/ppermute | solution.py:909
  328.1 1.4 collective-permute-start.39
  329.6 3.2 collective-permute-start.40
  334.8 7.5 %collective-permute-done.38 = bf16[128,1536]{1,0:T(8,128)(2,1)} collective-permute-done((bf16[128,1536]{1,0:T(8,128)(2,1)S(1)}, bf16[128,1536]{1,0:T(8,128)(2,1)}, u32[]{:S(2)}, u32[]{:S(2)}) %collective-permute-start.38) | collective-permute-done | bytes 393248 | tf_op jit(solution)/shard_map/ppermute | solution.py:909
  342.4 6.9 %collective-permute-done.40 = bf16[128,1536]{1,0:T(8,128)(2,1)} collective-permute-done((bf16[128,1536]{1,0:T(8,128)(2,1)S(1)}, bf16[128,1536]{1,0:T(8,128)(2,1)}, u32[]{:S(2)}, u32[]{:S(2)}) %collective-permute-start.40) | collective-permute-done | bytes 393248 | tf_op jit(solution)/shard_map/ppermute | solution.py:909
  352.2 4.5 %collective-permute-start.41 = (bf16[128,640]{1,0:T(8,128)(2,1)}, bf16[128,640]{1,0:T(8,128)(2,1)}, u32[]{:S(2)}, u32[]{:S(2)}) collective-permute-start(bf16[128,640]{1,0:T(8,128)(2,1)} %maximum_maximum_fusion), channel_id=1, source_target_pairs={{0,1},{1,2},{2,3},{3,0},{4,5},{5,6},{6,7},{7,4},{8,9},{9,10},{10,1... | collective-permute-start | bytes 491528 | tf_op jit(solution)/shard_map/ppermute | solution.py:905
  356.8 2.4 collective-permute-start.43
  361.5 2.7 fusion.18
  364.2 2.3 collective-permute-start.44
  368.6 1.6 copy.60
  371.3 2.6 fusion.7
  (244 shorter events, 55.0 us)
Async XLA Ops:
  7.2 36.2 %copy-start.44 = (f32[384]{0:T(512)S(1)}, f32[384]{0:T(512)}, u32[]{:S(2)}) copy-start(f32[384]{0:T(512)} %param.39) | copy-start | bytes 4612
  7.2 36.2 %copy-start.45 = (f32[256]{0:T(256)S(1)}, f32[256]{0:T(256)}, u32[]{:S(2)}) copy-start(f32[256]{0:T(256)} %param.40) | copy-start | bytes 3076
  7.2 36.2 %copy-start.46 = (f32[6]{0:T(128)S(1)}, f32[6]{0:T(128)}, u32[]{:S(2)}) copy-start(f32[6]{0:T(128)} %param.43) | copy-start | bytes 76
  7.2 36.3 %copy-start.47 = (f32[6]{0:T(128)S(1)}, f32[6]{0:T(128)}, u32[]{:S(2)}) copy-start(f32[6]{0:T(128)} %param.42) | copy-start | bytes 76
  7.2 36.4 %copy-start.48 = (f32[6]{0:T(128)S(1)}, f32[6]{0:T(128)}, u32[]{:S(2)}) copy-start(f32[6]{0:T(128)} %param.41) | copy-start | bytes 76
  7.2 39.8 %copy-start.40 = (f32[4,384]{1,0:T(4,128)S(1)}, f32[4,384]{1,0:T(4,128)}, u32[]{:S(2)}) copy-start(f32[4,384]{1,0:T(4,128)} %param.37) | copy-start | bytes 18436
  7.3 39.8 %copy-start.41 = (f32[4,256]{1,0:T(4,128)S(1)}, f32[4,256]{1,0:T(4,128)}, u32[]{:S(2)}) copy-start(f32[4,256]{1,0:T(4,128)} %param.38) | copy-start | bytes 12292
  7.3 39.8 %copy-start.38 = (s32[1,1024]{1,0:T(1,128)S(1)}, s32[1,1024]{1,0:T(1,128)}, u32[]{:S(2)}) copy-start(s32[1,1024]{1,0:T(1,128)} %param.28) | copy-start | bytes 12292
  7.3 42.2 %all-gather.3.cloned.1.call-start = ((), (), s32[]{:S(2)}) async-start(), calls=%async_computation.2 | async-start | bytes 4423680 | tf_op jit(solution)/shard_map/all_gather | solution.py:1054
  11.0 158.0 %all-gather.5.cloned.1.call-start = ((), (), s32[]{:S(2)}) async-start(), calls=%async_computation.3 | async-start | bytes 14155776 | tf_op jit(solution)/shard_map/all_gather | solution.py:1086
  11.0 17.1 %collective-permute-start.1 = (bf16[256,1024]{1,0:T(8,128)(2,1)}, bf16[256,1024]{1,0:T(8,128)(2,1)S(1)}, u32[]{:S(2)}, u32[]{:S(2)}) collective-permute-start(bf16[256,1024]{1,0:T(8,128)(2,1)} %refs_1_.2), channel_id=1, source_target_pairs={{1,0},{2,1},{3,2},{5,4},{6,5},{7,6},{9,8},{10,9},{11,10},{13,12},{... | collective-permute-start | bytes 1572872 | tf_op jit(solution)/shard_map/ppermute | solution.py:909
  12.3 17.1 %collective-permute-start = (bf16[256,1024]{1,0:T(8,128)(2,1)}, bf16[256,1024]{1,0:T(8,128)(2,1)S(1)}, u32[]{:S(2)}, u32[]{:S(2)}) collective-permute-start(bf16[256,1024]{1,0:T(8,128)(2,1)} %refs_1_.2), channel_id=1, source_target_pairs={{0,1},{1,2},{2,3},{4,5},{5,6},{6,7},{8,9},{9,10},{10,11},{12,13},{... | collective-permute-start | bytes 1572872 | tf_op jit(solution)/shard_map/ppermute | solution.py:909
  28.1 41.2 %copy-start.31 = (bf16[256,1024]{1,0:T(8,128)(2,1)}, bf16[256,1024]{1,0:T(8,128)(2,1)S(1)}, u32[]{:S(2)}) copy-start(bf16[256,1024]{1,0:T(8,128)(2,1)S(1)} %collective-permute-done.1.refs_7_) | copy-start | bytes 1572868
  28.1 17.7 %collective-permute-start.2 = (bf16[256,1024]{1,0:T(8,128)(2,1)S(1)}, bf16[256,1024]{1,0:T(8,128)(2,1)S(1)}, u32[]{:S(2)}, u32[]{:S(2)}) collective-permute-start(bf16[256,1024]{1,0:T(8,128)(2,1)S(1)} %collective-permute-done.1.refs_7_), channel_id=1, source_target_pairs={{2,0},{6,4},{10,8},{14,12},{18,16},{22,20},{26,24},{30,28}} | collective-permute-start | bytes 1572872 | tf_op jit(solution)/shard_map/ppermute | solution.py:909
  29.4 39.9 %copy-start.32 = (bf16[256,1024]{1,0:T(8,128)(2,1)}, bf16[256,1024]{1,0:T(8,128)(2,1)S(1)}, u32[]{:S(2)}) copy-start(bf16[256,1024]{1,0:T(8,128)(2,1)S(1)} %collective-permute-done.refs_2_) | copy-start | bytes 1572868
  29.4 22.1 %collective-permute-start.3 = (bf16[256,1024]{1,0:T(8,128)(2,1)S(1)}, bf16[256,1024]{1,0:T(8,128)(2,1)S(1)}, u32[]{:S(2)}, u32[]{:S(2)}) collective-permute-start(bf16[256,1024]{1,0:T(8,128)(2,1)S(1)} %collective-permute-done.refs_2_), channel_id=1, source_target_pairs={{1,2},{2,3},{5,6},{6,7},{9,10},{10,11},{13,14},{14,15},{17,18},{18... | collective-permute-start | bytes 1572872 | tf_op jit(solution)/shard_map/ppermute | solution.py:909
  30.1 25.3 %collective-permute-start.4 = (bf16[256,1024]{1,0:T(8,128)(2,1)S(1)}, bf16[256,1024]{1,0:T(8,128)(2,1)S(1)}, u32[]{:S(2)}, u32[]{:S(2)}) collective-permute-start(bf16[256,1024]{1,0:T(8,128)(2,1)S(1)} %collective-permute-done.1.refs_7_), channel_id=1, source_target_pairs={{2,1},{1,0},{6,5},{5,4},{10,9},{9,8},{14,13},{13,12},{18,17},{17,1... | collective-permute-start | bytes 1572872 | tf_op jit(solution)/shard_map/ppermute | solution.py:909
  31.4 24.0 %collective-permute-start.5 = (bf16[256,1024]{1,0:T(8,128)(2,1)S(1)}, bf16[256,1024]{1,0:T(8,128)(2,1)S(1)}, u32[]{:S(2)}, u32[]{:S(2)}) collective-permute-start(bf16[256,1024]{1,0:T(8,128)(2,1)S(1)} %collective-permute-done.refs_2_), channel_id=1, source_target_pairs={{1,3},{5,7},{9,11},{13,15},{17,19},{21,23},{25,27},{29,31}} | collective-permute-start | bytes 1572872 | tf_op jit(solution)/shard_map/ppermute | solution.py:909
  34.1 21.3 %collective-permute-start.14 = (bf16[128,1536]{1,0:T(8,128)(2,1)}, bf16[128,1536]{1,0:T(8,128)(2,1)}, u32[]{:S(2)}, u32[]{:S(2)}) collective-permute-start(bf16[128,1536]{1,0:T(8,128)(2,1)} %pack_ffn.1), channel_id=1, source_target_pairs={{0,1},{1,2},{2,3},{4,5},{5,6},{6,7},{8,9},{9,10},{10,11},{12,13},{... | collective-permute-start | bytes 1179656 | tf_op jit(solution)/shard_map/ppermute | solution.py:909
  45.8 18.1 %collective-permute-start.15 = (bf16[128,1536]{1,0:T(8,128)(2,1)}, bf16[128,1536]{1,0:T(8,128)(2,1)}, u32[]{:S(2)}, u32[]{:S(2)}) collective-permute-start(bf16[128,1536]{1,0:T(8,128)(2,1)} %pack_ffn.1), channel_id=1, source_target_pairs={{1,0},{2,1},{3,2},{5,4},{6,5},{7,6},{9,8},{10,9},{11,10},{13,12},{... | collective-permute-start | bytes 1179656 | tf_op jit(solution)/shard_map/ppermute | solution.py:909
  63.8 23.5 %collective-permute-start.16 = (bf16[128,1536]{1,0:T(8,128)(2,1)}, bf16[128,1536]{1,0:T(8,128)(2,1)}, u32[]{:S(2)}, u32[]{:S(2)}) collective-permute-start(bf16[128,1536]{1,0:T(8,128)(2,1)} %collective-permute-done.15), channel_id=1, source_target_pairs={{2,0},{6,4},{10,8},{14,12},{18,16},{22,20},{26,24},{30,28}} | collective-permute-start | bytes 1179656 | tf_op jit(solution)/shard_map/ppermute | solution.py:909
  65.1 22.2 %collective-permute-start.18 = (bf16[128,1536]{1,0:T(8,128)(2,1)}, bf16[128,1536]{1,0:T(8,128)(2,1)}, u32[]{:S(2)}, u32[]{:S(2)}) collective-permute-start(bf16[128,1536]{1,0:T(8,128)(2,1)} %collective-permute-done.15), channel_id=1, source_target_pairs={{2,1},{1,0},{6,5},{5,4},{10,9},{9,8},{14,13},{13,12},{18,17},{17,1... | collective-permute-start | bytes 1179656 | tf_op jit(solution)/shard_map/ppermute | solution.py:909
  66.4 20.9 %collective-permute-start.17 = (bf16[128,1536]{1,0:T(8,128)(2,1)}, bf16[128,1536]{1,0:T(8,128)(2,1)}, u32[]{:S(2)}, u32[]{:S(2)}) collective-permute-start(bf16[128,1536]{1,0:T(8,128)(2,1)} %collective-permute-done.14), channel_id=1, source_target_pairs={{1,2},{2,3},{5,6},{6,7},{9,10},{10,11},{13,14},{14,15},{17,18},{18... | collective-permute-start | bytes 1179656 | tf_op jit(solution)/shard_map/ppermute | solution.py:909
  67.8 19.5 %collective-permute-start.19 = (bf16[128,1536]{1,0:T(8,128)(2,1)}, bf16[128,1536]{1,0:T(8,128)(2,1)}, u32[]{:S(2)}, u32[]{:S(2)}) collective-permute-start(bf16[128,1536]{1,0:T(8,128)(2,1)} %collective-permute-done.14), channel_id=1, source_target_pairs={{1,3},{5,7},{9,11},{13,15},{17,19},{21,23},{25,27},{29,31}} | collective-permute-start | bytes 1179656 | tf_op jit(solution)/shard_map/ppermute | solution.py:909
  91.6 220.9 %reduce-scatter.3.cloned.1.call-start = ((), (), s32[]{:S(2)}) async-start(), calls=%async_computation.4 | async-start | bytes 14155776 | tf_op jit(solution)/shard_map/reduce_scatter | solution.py:1096
  91.7 18.1 %collective-permute-start.6 = (f32[1,1024]{1,0:T(1,128)S(1)}, f32[1,1024]{1,0:T(1,128)S(1)}, u32[]{:S(2)}, u32[]{:S(2)}) collective-permute-start(f32[1,1024]{1,0:T(1,128)S(1)} %slice.136), channel_id=1, source_target_pairs={{0,1},{1,2},{2,3},{3,0},{4,5},{5,6},{6,7},{7,4},{8,9},{9,10},{10,1... | collective-permute-start | bytes 12296 | tf_op jit(solution)/shard_map/ppermute | solution.py:905
  99.4 10.4 %collective-permute-start.7 = (f32[1,1024]{1,0:T(1,128)S(1)}, f32[1,1024]{1,0:T(1,128)S(1)}, u32[]{:S(2)}, u32[]{:S(2)}) collective-permute-start(f32[1,1024]{1,0:T(1,128)S(1)} %slice.136), channel_id=1, source_target_pairs={{0,2},{1,3},{2,0},{3,1},{4,6},{5,7},{6,4},{7,5},{8,10},{9,11},{10,... | collective-permute-start | bytes 12296 | tf_op jit(solution)/shard_map/ppermute | solution.py:905
  99.4 10.4 %collective-permute-start.8 = (f32[1,1024]{1,0:T(1,128)S(1)}, f32[1,1024]{1,0:T(1,128)S(1)}, u32[]{:S(2)}, u32[]{:S(2)}) collective-permute-start(f32[1,1024]{1,0:T(1,128)S(1)} %slice.136), channel_id=1, source_target_pairs={{0,3},{1,0},{2,1},{3,2},{4,7},{5,4},{6,5},{7,6},{8,11},{9,8},{10,9... | collective-permute-start | bytes 12296 | tf_op jit(solution)/shard_map/ppermute | solution.py:905
  112.3 14.5 %collective-permute-start.11 = (bf16[256,1024]{1,0:T(8,128)(2,1)}, bf16[256,1024]{1,0:T(8,128)(2,1)S(1)}, u32[]{:S(2)}, u32[]{:S(2)}) collective-permute-start(bf16[256,1024]{1,0:T(8,128)(2,1)} %get-tuple-element.244), channel_id=1, source_target_pairs={{0,2},{3,1},{4,6},{7,5},{8,10},{11,9},{12,14},{15,13},{16,18},{19,... | collective-permute-start | bytes 1572872 | tf_op jit(solution)/shard_map/ppermute | solution.py:909
  115.4 11.4 %collective-permute-start.10 = (bf16[256,1024]{1,0:T(8,128)(2,1)}, bf16[256,1024]{1,0:T(8,128)(2,1)S(1)}, u32[]{:S(2)}, u32[]{:S(2)}) collective-permute-start(bf16[256,1024]{1,0:T(8,128)(2,1)} %convolution_convert_fusion), channel_id=1, source_target_pairs={{1,2},{2,1},{5,6},{6,5},{9,10},{10,9},{13,14},{14,13},{17,18},{18,... | collective-permute-start | bytes 1572872 | tf_op jit(solution)/shard_map/ppermute | solution.py:909
  116.0 19.6 %collective-permute-start.9 = (bf16[256,1024]{1,0:T(8,128)(2,1)}, bf16[256,1024]{1,0:T(8,128)(2,1)}, u32[]{:S(2)}, u32[]{:S(2)}) collective-permute-start(bf16[256,1024]{1,0:T(8,128)(2,1)} %convolution_convert_fusion), channel_id=1, source_target_pairs={{0,1},{3,2},{4,5},{7,6},{8,9},{11,10},{12,13},{15,14},{16,17},{19,... | collective-permute-start | bytes 1572872 | tf_op jit(solution)/shard_map/ppermute | solution.py:909
  139.0 17.0 %collective-permute-start.12 = (bf16[256,1024]{1,0:T(8,128)(2,1)}, bf16[256,1024]{1,0:T(8,128)(2,1)}, u32[]{:S(2)}, u32[]{:S(2)}) collective-permute-start(bf16[256,1024]{1,0:T(8,128)(2,1)} %get-tuple-element.223), channel_id=1, source_target_pairs={{0,1},{1,2},{2,3},{4,5},{5,6},{6,7},{8,9},{9,10},{10,11},{12,13},{... | collective-permute-start | bytes 1572872 | tf_op jit(solution)/shard_map/ppermute | solution.py:909
  145.0 15.9 %collective-permute-start.13 = (bf16[256,1024]{1,0:T(8,128)(2,1)}, bf16[256,1024]{1,0:T(8,128)(2,1)}, u32[]{:S(2)}, u32[]{:S(2)}) collective-permute-start(bf16[256,1024]{1,0:T(8,128)(2,1)} %get-tuple-element.224), channel_id=1, source_target_pairs={{3,2},{2,1},{1,0},{7,6},{6,5},{5,4},{11,10},{10,9},{9,8},{15,14},{... | collective-permute-start | bytes 1572872 | tf_op jit(solution)/shard_map/ppermute | solution.py:909
  186.4 148.4 %reduce-scatter.5.cloned.1.call-start = ((), (), s32[]{:S(2)}) async-start(), calls=%async_computation.5 | async-start | bytes 2457600 | tf_op jit(solution)/shard_map/reduce_scatter | solution.py:975
  187.5 16.1 %collective-permute-start.21 = (bf16[256,1024]{1,0:T(8,128)(2,1)S(1)}, bf16[256,1024]{1,0:T(8,128)(2,1)}, u32[]{:S(2)}, u32[]{:S(2)}) collective-permute-start(bf16[256,1024]{1,0:T(8,128)(2,1)S(1)} %copy-done.12), channel_id=1, source_target_pairs={{1,0},{2,1},{3,2},{5,4},{6,5},{7,6},{9,8},{10,9},{11,10},{13,12},{... | collective-permute-start | bytes 1572872 | tf_op jit(solution)/shard_map/ppermute | solution.py:909
  188.7 16.1 %collective-permute-start.20 = (bf16[256,1024]{1,0:T(8,128)(2,1)S(1)}, bf16[256,1024]{1,0:T(8,128)(2,1)}, u32[]{:S(2)}, u32[]{:S(2)}) collective-permute-start(bf16[256,1024]{1,0:T(8,128)(2,1)S(1)} %copy-done.12), channel_id=1, source_target_pairs={{0,1},{1,2},{2,3},{4,5},{5,6},{6,7},{8,9},{9,10},{10,11},{12,13},{... | collective-permute-start | bytes 1572872 | tf_op jit(solution)/shard_map/ppermute | solution.py:909
  203.5 18.0 %collective-permute-start.22 = (bf16[256,1024]{1,0:T(8,128)(2,1)}, bf16[256,1024]{1,0:T(8,128)(2,1)}, u32[]{:S(2)}, u32[]{:S(2)}) collective-permute-start(bf16[256,1024]{1,0:T(8,128)(2,1)} %collective-permute-done.21.refs_7_), channel_id=1, source_target_pairs={{2,0},{6,4},{10,8},{14,12},{18,16},{22,20},{26,24},{30,28}} | collective-permute-start | bytes 1572872 | tf_op jit(solution)/shard_map/ppermute | solution.py:909
  204.8 16.7 %collective-permute-start.23 = (bf16[256,1024]{1,0:T(8,128)(2,1)}, bf16[256,1024]{1,0:T(8,128)(2,1)}, u32[]{:S(2)}, u32[]{:S(2)}) collective-permute-start(bf16[256,1024]{1,0:T(8,128)(2,1)} %collective-permute-done.20.refs_2_), channel_id=1, source_target_pairs={{1,2},{2,3},{5,6},{6,7},{9,10},{10,11},{13,14},{14,15},{17,18},{18... | collective-permute-start | bytes 1572872 | tf_op jit(solution)/shard_map/ppermute | solution.py:909
  206.3 24.8 %collective-permute-start.24 = (bf16[256,1024]{1,0:T(8,128)(2,1)}, bf16[256,1024]{1,0:T(8,128)(2,1)}, u32[]{:S(2)}, u32[]{:S(2)}) collective-permute-start(bf16[256,1024]{1,0:T(8,128)(2,1)} %collective-permute-done.21.refs_7_), channel_id=1, source_target_pairs={{2,1},{1,0},{6,5},{5,4},{10,9},{9,8},{14,13},{13,12},{18,17},{17,1... | collective-permute-start | bytes 1572872 | tf_op jit(solution)/shard_map/ppermute | solution.py:909
  207.6 23.6 %collective-permute-start.25 = (bf16[256,1024]{1,0:T(8,128)(2,1)}, bf16[256,1024]{1,0:T(8,128)(2,1)}, u32[]{:S(2)}, u32[]{:S(2)}) collective-permute-start(bf16[256,1024]{1,0:T(8,128)(2,1)} %collective-permute-done.20.refs_2_), channel_id=1, source_target_pairs={{1,3},{5,7},{9,11},{13,15},{17,19},{21,23},{25,27},{29,31}} | collective-permute-start | bytes 1572872 | tf_op jit(solution)/shard_map/ppermute | solution.py:909
  211.9 30.7 %copy-start.11 = (f32[1024,128]{1,0:T(8,128)S(1)}, f32[1024,128]{1,0:T(8,128)}, u32[]{:S(2)}) copy-start(f32[1024,128]{1,0:T(8,128)} %copy-done.10) | copy-start | bytes 1572868
  211.9 30.7 %copy-start.14 = (bf16[1024,128]{1,0:T(8,128)(2,1)S(1)}, bf16[1024,128]{1,0:T(8,128)(2,1)}, u32[]{:S(2)}) copy-start(bf16[1024,128]{1,0:T(8,128)(2,1)} %copy-done.13) | copy-start | bytes 786436
  211.9 30.7 %copy-start.16 = (bf16[1024,128]{1,0:T(8,128)(2,1)S(1)}, bf16[1024,128]{1,0:T(8,128)(2,1)}, u32[]{:S(2)}) copy-start(bf16[1024,128]{1,0:T(8,128)(2,1)} %copy-done.15) | copy-start | bytes 786436
  237.0 12.3 %collective-permute-start.26 = (f32[1,1024]{1,0:T(1,128)S(1)}, f32[1,1024]{1,0:T(1,128)S(1)}, u32[]{:S(2)}, u32[]{:S(2)}) collective-permute-start(f32[1,1024]{1,0:T(1,128)S(1)} %slice.138), channel_id=1, source_target_pairs={{0,1},{1,2},{2,3},{3,0},{4,5},{5,6},{6,7},{7,4},{8,9},{9,10},{10,1... | collective-permute-start | bytes 12296 | tf_op jit(solution)/shard_map/ppermute | solution.py:905
  239.2 10.0 %collective-permute-start.27 = (f32[1,1024]{1,0:T(1,128)S(1)}, f32[1,1024]{1,0:T(1,128)S(1)}, u32[]{:S(2)}, u32[]{:S(2)}) collective-permute-start(f32[1,1024]{1,0:T(1,128)S(1)} %slice.138), channel_id=1, source_target_pairs={{0,2},{1,3},{2,0},{3,1},{4,6},{5,7},{6,4},{7,5},{8,10},{9,11},{10,... | collective-permute-start | bytes 12296 | tf_op jit(solution)/shard_map/ppermute | solution.py:905
  242.6 6.7 %collective-permute-start.28 = (f32[1,1024]{1,0:T(1,128)S(1)}, f32[1,1024]{1,0:T(1,128)S(1)}, u32[]{:S(2)}, u32[]{:S(2)}) collective-permute-start(f32[1,1024]{1,0:T(1,128)S(1)} %slice.138), channel_id=1, source_target_pairs={{0,3},{1,0},{2,1},{3,2},{4,7},{5,4},{6,5},{7,6},{8,11},{9,8},{10,9... | collective-permute-start | bytes 12296 | tf_op jit(solution)/shard_map/ppermute | solution.py:905
  274.8 6.8 %collective-permute-start.33 = (bf16[512,1920]{1,0:T(8,128)(2,1)}, bf16[512,1920]{1,0:T(8,128)(2,1)}, u32[]{:S(2)}, u32[]{:S(2)}) collective-permute-start(bf16[512,1920]{1,0:T(8,128)(2,1)} %get-tuple-element.116), channel_id=1, source_target_pairs={{0,4},{4,0},{8,12},{12,8},{16,20},{20,16},{24,28},{28,24},{1,5},{5... | collective-permute-start | bytes 5898248 | tf_op jit(solution)/shard_map/ppermute | solution.py:968
  280.2 1.5 collective-permute-start.32
  285.6 26.9 %collective-permute-start.29 = (bf16[256,1024]{1,0:T(8,128)(2,1)S(1)}, bf16[256,1024]{1,0:T(8,128)(2,1)}, u32[]{:S(2)}, u32[]{:S(2)}) collective-permute-start(bf16[256,1024]{1,0:T(8,128)(2,1)S(1)} %get-tuple-element.121), channel_id=1, source_target_pairs={{0,1},{3,2},{4,5},{7,6},{8,9},{11,10},{12,13},{15,14},{16,17},{19,... | collective-permute-start | bytes 1572872 | tf_op jit(solution)/shard_map/ppermute | solution.py:909
  290.3 22.2 %collective-permute-start.30 = (bf16[256,1024]{1,0:T(8,128)(2,1)S(1)}, bf16[256,1024]{1,0:T(8,128)(2,1)}, u32[]{:S(2)}, u32[]{:S(2)}) collective-permute-start(bf16[256,1024]{1,0:T(8,128)(2,1)S(1)} %get-tuple-element.121), channel_id=1, source_target_pairs={{1,2},{2,1},{5,6},{6,5},{9,10},{10,9},{13,14},{14,13},{17,18},{18,... | collective-permute-start | bytes 1572872 | tf_op jit(solution)/shard_map/ppermute | solution.py:909
  291.8 6.0 %collective-permute-start.34 = (f32[16,1024]{1,0:T(8,128)S(1)}, f32[16,1024]{1,0:T(8,128)S(1)}, u32[]{:S(2)}, u32[]{:S(2)}) collective-permute-start(f32[16,1024]{1,0:T(8,128)S(1)} %add.182), channel_id=1, source_target_pairs={{0,8},{4,12},{8,0},{12,4},{16,24},{20,28},{24,16},{28,20},{1,9},{5... | collective-permute-start | bytes 196616 | tf_op jit(solution)/shard_map/ppermute | solution.py:992
  293.4 19.1 %collective-permute-start.31 = (bf16[256,1024]{1,0:T(8,128)(2,1)S(1)}, bf16[256,1024]{1,0:T(8,128)(2,1)}, u32[]{:S(2)}, u32[]{:S(2)}) collective-permute-start(bf16[256,1024]{1,0:T(8,128)(2,1)S(1)} %broadcast_select_fusion), channel_id=1, source_target_pairs={{0,2},{3,1},{4,6},{7,5},{8,10},{11,9},{12,14},{15,13},{16,18},{19,... | collective-permute-start | bytes 1572872 | tf_op jit(solution)/shard_map/ppermute | solution.py:909
  297.7 5.4 %collective-permute-start.35 = (f32[16,1024]{1,0:T(8,128)S(1)}, f32[16,1024]{1,0:T(8,128)S(1)}, u32[]{:S(2)}, u32[]{:S(2)}) collective-permute-start(f32[16,1024]{1,0:T(8,128)S(1)} %add.184), channel_id=1, source_target_pairs={{0,16},{4,20},{8,24},{12,28},{16,0},{20,4},{24,8},{28,12},{1,17},{... | collective-permute-start | bytes 196616 | tf_op jit(solution)/shard_map/ppermute | solution.py:992
  315.5 36.0 %copy-start.42 = (bf16[2,128]{1,0:T(2,128)(2,1)S(1)}, bf16[2,128]{1,0:T(2,128)(2,1)}, u32[]{:S(2)}) copy-start(bf16[2,128]{1,0:T(2,128)(2,1)} %dynamic-slice_convert_fusion) | copy-start | bytes 1540
  315.5 33.8 %collective-permute-start.36 = (bf16[256,1024]{1,0:T(8,128)(2,1)}, bf16[256,1024]{1,0:T(8,128)(2,1)S(1)}, u32[]{:S(2)}, u32[]{:S(2)}) collective-permute-start(bf16[256,1024]{1,0:T(8,128)(2,1)} %get-tuple-element.222), channel_id=1, source_target_pairs={{0,1},{1,2},{2,3},{4,5},{5,6},{6,7},{8,9},{9,10},{10,11},{12,13},{... | collective-permute-start | bytes 1572872 | tf_op jit(solution)/shard_map/ppermute | solution.py:909
  321.4 27.9 %collective-permute-start.37 = (bf16[256,1024]{1,0:T(8,128)(2,1)}, bf16[256,1024]{1,0:T(8,128)(2,1)S(1)}, u32[]{:S(2)}, u32[]{:S(2)}) collective-permute-start(bf16[256,1024]{1,0:T(8,128)(2,1)} %get-tuple-element.221), channel_id=1, source_target_pairs={{3,2},{2,1},{1,0},{7,6},{6,5},{5,4},{11,10},{10,9},{9,8},{15,14},{... | collective-permute-start | bytes 1572872 | tf_op jit(solution)/shard_map/ppermute | solution.py:909
  322.8 19.6 %collective-permute-start.38 = (bf16[128,1536]{1,0:T(8,128)(2,1)S(1)}, bf16[128,1536]{1,0:T(8,128)(2,1)}, u32[]{:S(2)}, u32[]{:S(2)}) collective-permute-start(bf16[128,1536]{1,0:T(8,128)(2,1)S(1)} %get-tuple-element.220), channel_id=1, source_target_pairs={{0,1},{3,2},{4,5},{7,6},{8,9},{11,10},{12,13},{15,14},{16,17},{19,... | collective-permute-start | bytes 1179656 | tf_op jit(solution)/shard_map/ppermute | solution.py:909
  328.1 14.2 %collective-permute-start.39 = (bf16[128,1536]{1,0:T(8,128)(2,1)S(1)}, bf16[128,1536]{1,0:T(8,128)(2,1)}, u32[]{:S(2)}, u32[]{:S(2)}) collective-permute-start(bf16[128,1536]{1,0:T(8,128)(2,1)S(1)} %get-tuple-element.220), channel_id=1, source_target_pairs={{1,2},{2,1},{5,6},{6,5},{9,10},{10,9},{13,14},{14,13},{17,18},{18,... | collective-permute-start | bytes 1179656 | tf_op jit(solution)/shard_map/ppermute | solution.py:909
  329.6 19.7 %collective-permute-start.40 = (bf16[128,1536]{1,0:T(8,128)(2,1)S(1)}, bf16[128,1536]{1,0:T(8,128)(2,1)}, u32[]{:S(2)}, u32[]{:S(2)}) collective-permute-start(bf16[128,1536]{1,0:T(8,128)(2,1)S(1)} %get-tuple-element.219), channel_id=1, source_target_pairs={{0,2},{3,1},{4,6},{7,5},{8,10},{11,9},{12,14},{15,13},{16,18},{19,... | collective-permute-start | bytes 1179656 | tf_op jit(solution)/shard_map/ppermute | solution.py:909
  352.2 22.5 %collective-permute-start.41 = (bf16[128,640]{1,0:T(8,128)(2,1)}, bf16[128,640]{1,0:T(8,128)(2,1)}, u32[]{:S(2)}, u32[]{:S(2)}) collective-permute-start(bf16[128,640]{1,0:T(8,128)(2,1)} %maximum_maximum_fusion), channel_id=1, source_target_pairs={{0,1},{1,2},{2,3},{3,0},{4,5},{5,6},{6,7},{7,4},{8,9},{9,10},{10,1... | collective-permute-start | bytes 491528 | tf_op jit(solution)/shard_map/ppermute | solution.py:905
  356.8 17.9 %collective-permute-start.42 = (bf16[128,640]{1,0:T(8,128)(2,1)}, bf16[128,640]{1,0:T(8,128)(2,1)}, u32[]{:S(2)}, u32[]{:S(2)}) collective-permute-start(bf16[128,640]{1,0:T(8,128)(2,1)} %maximum_maximum_fusion), channel_id=1, source_target_pairs={{0,2},{1,3},{2,0},{3,1},{4,6},{5,7},{6,4},{7,5},{8,10},{9,11},{10,... | collective-permute-start | bytes 491528 | tf_op jit(solution)/shard_map/ppermute | solution.py:905
  356.8 17.9 %collective-permute-start.43 = (bf16[128,640]{1,0:T(8,128)(2,1)}, bf16[128,640]{1,0:T(8,128)(2,1)}, u32[]{:S(2)}, u32[]{:S(2)}) collective-permute-start(bf16[128,640]{1,0:T(8,128)(2,1)} %maximum_maximum_fusion), channel_id=1, source_target_pairs={{0,3},{1,0},{2,1},{3,2},{4,7},{5,4},{6,5},{7,6},{8,11},{9,8},{10,9... | collective-permute-start | bytes 491528 | tf_op jit(solution)/shard_map/ppermute | solution.py:905
  364.2 14.1 %collective-permute-start.44 = (bf16[128,1536]{1,0:T(8,128)(2,1)}, bf16[128,1536]{1,0:T(8,128)(2,1)}, u32[]{:S(2)}, u32[]{:S(2)}) collective-permute-start(bf16[128,1536]{1,0:T(8,128)(2,1)} %get-tuple-element.217), channel_id=1, source_target_pairs={{0,1},{1,2},{2,3},{4,5},{5,6},{6,7},{8,9},{9,10},{10,11},{12,13},{... | collective-permute-start | bytes 1179656 | tf_op jit(solution)/shard_map/ppermute | solution.py:909
  366.5 11.8 %collective-permute-start.45 = (bf16[128,1536]{1,0:T(8,128)(2,1)}, bf16[128,1536]{1,0:T(8,128)(2,1)}, u32[]{:S(2)}, u32[]{:S(2)}) collective-permute-start(bf16[128,1536]{1,0:T(8,128)(2,1)} %get-tuple-element.218), channel_id=1, source_target_pairs={{3,2},{2,1},{1,0},{7,6},{6,5},{5,4},{11,10},{10,9},{9,8},{15,14},{... | collective-permute-start | bytes 1179656 | tf_op jit(solution)/shard_map/ppermute | solution.py:909
  (37 other events, 342.2 us)
Sparse Core Ops, SparseCore 0:
  11.1 38.3 all-gather.2
  91.7 77.2 all-gather.4
  186.6 92.4 reduce-scatter.2
  285.7 34.2 reduce-scatter.4
